TPU v7x, 32 devices: a whole 2x2x4 slice. The times are simulated.
32 devices in a mesh: fsdp: 32 (over z, y, x, core).
Axes of the slice: x: 2, y: 2, z: 4, core: 2. Of those that a mesh axis runs over, the one named last changes fastest.
Arguments:
- tokens: bfloat16 [32768, 1024], P('fsdp'), may hold values from -6 to 6
- segments: int32 [32, 1024], P('fsdp'), may hold values from 0 to 7, never falling along the last dimension, each value on 1 to 512 neighbouring positions
- cotangent: bfloat16 [32768, 1024], P('fsdp'), may hold values from -6 to 6
- w_query: bfloat16 [1024, 2048], P('fsdp'), may hold values from -0.1875 to 0.1875
- w_key: bfloat16 [1024, 1024], P('fsdp'), may hold values from -0.1875 to 0.1875
- w_value: bfloat16 [1024, 1024], P('fsdp'), may hold values from -0.1875 to 0.1875
- w_out: bfloat16 [2048, 1024], P(None, 'fsdp'), may hold values from -1 to 1
- w_gate: bfloat16 [1024, 3072], P('fsdp'), may hold values from -0.1875 to 0.1875
- w_up: bfloat16 [1024, 3072], P('fsdp'), may hold values from -0.1875 to 0.1875
- w_down: bfloat16 [3072, 1024], P(None, 'fsdp'), may hold values from -0.109375 to 0.109375
- attn_gain: bfloat16 [1024], P('fsdp'), may hold values from 0.099609375 to 1.8984375
- mlp_gain: bfloat16 [1024], P('fsdp'), may hold values from 0.099609375 to 1.8984375
- q_gain: bfloat16 [128], replicated, may hold values from 0.099609375 to 1.8984375
- k_gain: bfloat16 [128], replicated, may hold values from 0.099609375 to 1.8984375
Outputs:
- result: bfloat16 [32768, 1024], P('fsdp')
- grad_tokens: bfloat16 [32768, 1024], P('fsdp')
- grad_query: float32 [1024, 2048], P('fsdp')
- grad_key: float32 [1024, 1024], P('fsdp')
- grad_value: float32 [1024, 1024], P('fsdp')
- grad_out: float32 [2048, 1024], P(None, 'fsdp')
- grad_gate: float32 [1024, 3072], P('fsdp')
- grad_up: float32 [1024, 3072], P('fsdp')
- grad_down: float32 [3072, 1024], P(None, 'fsdp')
- grad_attn_gain: float32 [1024], P('fsdp')
- grad_mlp_gain: float32 [1024], P('fsdp')
- grad_q_gain: float32 [128], replicated
- grad_k_gain: float32 [128], replicated
Inputs may be any that keep to these rules, and one draw needn't show every extreme that they name: `segments`: document numbers never fall along a sequence; a document is 1 to 512 tokens long, and one in each sequence is exactly that long.
All inputs are finite; a program needn't handle non-finite values.
Results may differ from a plain program's by a relative error of at most 0.014.
Values may be sent and summed in bfloat16 or wider, within the bound.
No kernel may reach another device: no remote copies, remote signals or barrier semaphores. Data moves between devices by JAX's collectives and lax.ppermute only.
A program may use at most 320 MiB of HBM per device.

v0:
```python
import math

import jax
import jax.numpy as jnp
from jax import lax
from jax.sharding import PartitionSpec as P

D = 1024
QUERY_HEADS = 16
KEY_VALUE_HEADS = 8
HEAD_SIZE = 128
FF = 3072
QBLK = 512


EPS = 1e-06
THETA = 1000000.0


def norm_parts(value_rows, gain):
    inverse = lax.rsqrt(jnp.mean(value_rows * value_rows, axis=-1, keepdims=True) + EPS)
    scaled = value_rows * inverse
    return (scaled * gain, scaled, inverse)


def norm_backward_pass(grad_in, scaled, inverse, gain):
    grad_scaled = grad_in * gain
    inner = jnp.mean(grad_scaled * scaled, axis=-1, keepdims=True)
    return inverse * (grad_scaled - scaled * inner)


def places(segment_row):
    index = jnp.arange(segment_row.shape[0], dtype=jnp.int32)
    previous = jnp.concatenate([segment_row[:1] - 1, segment_row[:-1]])
    starts = jnp.where(segment_row != previous, index, 0)
    return index - lax.cummax(starts, axis=0)


def angles(select_positions, width):
    half = width // 2
    freq = THETA ** (-jnp.arange(half, dtype=jnp.float32) / half)
    turned = select_positions.astype(jnp.float32)[:, None] * freq[None, :]
    return (jnp.cos(turned)[:, None, :], jnp.sin(turned)[:, None, :])


def rotary_embed(value_rows, rotary_cosine, rotary_sine):
    half = value_rows.shape[-1] // 2
    first = value_rows[..., :half]
    second = value_rows[..., half:]
    return jnp.concatenate(
        [
            first * rotary_cosine - second * rotary_sine,
            second * rotary_cosine + first * rotary_sine,
        ],
        axis=-1,
    )


def column_product(left, right):
    return jnp.einsum("td,tc->dc", left, right, preferred_element_type=jnp.float32)


def per_device(
    tokens,
    segments,
    cotangent,
    w_query,
    w_key,
    w_value,
    w_out,
    w_gate,
    w_up,
    w_down,
    attn_gain,
    mlp_gain,
    q_gain,
    k_gain,
):
    single_float = jnp.float32
    brain_float_sixteen = jnp.bfloat16
    token_rows = tokens.shape[0]
    segment_row = segments[0]
    index = jnp.arange(token_rows, dtype=jnp.int32)
    rotary_cosine, rotary_sine = angles(places(segment_row), HEAD_SIZE)
    query_group_count = QUERY_HEADS // KEY_VALUE_HEADS
    block = min(QBLK, token_rows)
    count = token_rows // block
    root = math.sqrt(HEAD_SIZE)
    qw = QUERY_HEADS * HEAD_SIZE
    kw = KEY_VALUE_HEADS * HEAD_SIZE
    share = D // lax.axis_size("fsdp")
    gathered = (
        lax.all_gather(w_query, "fsdp", axis=0, tiled=True),
        lax.all_gather(w_key, "fsdp", axis=0, tiled=True),
        lax.all_gather(w_value, "fsdp", axis=0, tiled=True),
        lax.all_gather(w_out, "fsdp", axis=1, tiled=True),
        lax.all_gather(w_gate, "fsdp", axis=0, tiled=True),
        lax.all_gather(w_up, "fsdp", axis=0, tiled=True),
        lax.all_gather(w_down, "fsdp", axis=1, tiled=True),
        lax.all_gather(attn_gain, "fsdp", axis=0, tiled=True),
        lax.all_gather(mlp_gain, "fsdp", axis=0, tiled=True),
    )
    wq, key_matrix, value_matrix, wo, wg, wu, wd, gain_one, gain_two = gathered
    gain_a = gain_one.astype(single_float)
    gain_m = gain_two.astype(single_float)
    query_norm_scale = q_gain.astype(single_float)
    key_norm_scale = k_gain.astype(single_float)
    inputs = tokens.astype(single_float)
    first_normalized1, scaled1, inverse1 = norm_parts(inputs, gain_a)
    first_norm_output = first_normalized1.astype(brain_float_sixteen)
    query_unnormalized = jnp.dot(
        first_norm_output, wq, preferred_element_type=single_float
    ).reshape(token_rows, QUERY_HEADS, HEAD_SIZE)
    key_unnormalized = jnp.dot(
        first_norm_output, key_matrix, preferred_element_type=single_float
    ).reshape(token_rows, KEY_VALUE_HEADS, HEAD_SIZE)
    value_rows = (
        jnp.dot(first_norm_output, value_matrix, preferred_element_type=single_float)
        .astype(brain_float_sixteen)
        .reshape(token_rows, KEY_VALUE_HEADS, HEAD_SIZE)
    )
    query_rownorm, q_scaled, q_inverse = norm_parts(query_unnormalized, query_norm_scale)
    k_normed, key_rescaled, key_inverse_norm = norm_parts(key_unnormalized, key_norm_scale)
    query_rows = (
        rotary_embed(query_rownorm, rotary_cosine, rotary_sine)
        .astype(brain_float_sixteen)
        .reshape(token_rows, KEY_VALUE_HEADS, query_group_count, HEAD_SIZE)
    )
    keys = rotary_embed(k_normed, rotary_cosine, rotary_sine).astype(brain_float_sixteen)

    def masked_scores(start, stop):
        raw = (
            jnp.einsum(
                "qgrd,kgd->grqk",
                query_rows[start:stop],
                keys[:stop],
                preferred_element_type=single_float,
            )
            / root
        )
        allowed = (segment_row[start:stop, None] == segment_row[None, :stop]) & (
            index[start:stop, None] >= index[None, :stop]
        )
        return jnp.where(allowed, raw, -1e30)

    pieces = []
    totals = []
    for step in range(count):
        start = step * block
        stop = start + block
        scores = masked_scores(start, stop)
        top = jnp.max(scores, axis=-1, keepdims=True)
        expo = jnp.exp(scores - top)
        total = jnp.sum(expo, axis=-1, keepdims=True)
        probs = (expo / total).astype(brain_float_sixteen)
        pieces.append(
            jnp.einsum(
                "grqk,kgd->qgrd", probs, value_rows[:stop], preferred_element_type=single_float
            ).reshape(block, QUERY_HEADS * HEAD_SIZE)
        )
        totals.append(top + jnp.log(total))
    attended = jnp.concatenate(pieces, axis=0).astype(brain_float_sixteen)
    after = inputs + jnp.dot(attended, wo, preferred_element_type=single_float)
    normed2, scaled2, inverse2 = norm_parts(after, gain_m)
    n_two = normed2.astype(brain_float_sixteen)
    gate = jnp.dot(n_two, wg, preferred_element_type=single_float)
    up = jnp.dot(n_two, wu, preferred_element_type=single_float)
    sigmoid = jax.nn.sigmoid(gate)
    silu = gate * sigmoid
    hidden = (silu * up).astype(brain_float_sixteen)
    result = (after + jnp.dot(hidden, wd, preferred_element_type=single_float)).astype(
        brain_float_sixteen
    )
    regathered = (
        lax.all_gather(w_query, "fsdp", axis=0, tiled=True),
        lax.all_gather(w_key, "fsdp", axis=0, tiled=True),
        lax.all_gather(w_value, "fsdp", axis=0, tiled=True),
        lax.all_gather(w_out, "fsdp", axis=1, tiled=True),
        lax.all_gather(w_gate, "fsdp", axis=0, tiled=True),
        lax.all_gather(w_up, "fsdp", axis=0, tiled=True),
        lax.all_gather(w_down, "fsdp", axis=1, tiled=True),
        lax.all_gather(attn_gain, "fsdp", axis=0, tiled=True),
        lax.all_gather(mlp_gain, "fsdp", axis=0, tiled=True),
    )
    wq, key_matrix, value_matrix, wo, wg, wu, wd, gain_one, gain_two = regathered
    gain_a = gain_one.astype(single_float)
    gain_m = gain_two.astype(single_float)
    grad_result = cotangent.astype(single_float)
    grad_hidden = jnp.einsum("td,fd->tf", cotangent, wd, preferred_element_type=single_float)
    grad_gate_low = (grad_hidden * up * sigmoid * (1.0 + gate * (1.0 - sigmoid))).astype(
        brain_float_sixteen
    )
    grad_up_low = (grad_hidden * silu).astype(brain_float_sixteen)
    grad_n_two = jnp.einsum(
        "tf,df->td", grad_gate_low, wg, preferred_element_type=single_float
    ) + jnp.einsum("tf,df->td", grad_up_low, wu, preferred_element_type=single_float)
    grad_gain_m = jnp.sum(grad_n_two * scaled2, axis=0)
    grad_after = grad_result + norm_backward_pass(grad_n_two, scaled2, inverse2, gain_m)
    joined_mlp = jnp.concatenate([grad_gate_low, grad_up_low], axis=1)
    grad_att = grad_after.astype(brain_float_sixteen)
    grad_mixed = (
        jnp.einsum("td,cd->tc", grad_att, wo, preferred_element_type=single_float)
        .astype(brain_float_sixteen)
        .reshape(token_rows, KEY_VALUE_HEADS, query_group_count, HEAD_SIZE)
    )
    grad_q_pieces = []
    key_gradient_rows = jnp.zeros((token_rows, KEY_VALUE_HEADS, HEAD_SIZE), single_float)
    value_gradient_rows = jnp.zeros((token_rows, KEY_VALUE_HEADS, HEAD_SIZE), single_float)
    for step in range(count):
        start = step * block
        stop = start + block
        scores = masked_scores(start, stop)
        probs = jnp.exp(scores - totals[step])
        probs_low = probs.astype(brain_float_sixteen)
        grad_piece = grad_mixed[start:stop]
        grad_probs = jnp.einsum(
            "qgrd,kgd->grqk", grad_piece, value_rows[:stop], preferred_element_type=single_float
        )
        delta = jnp.sum(grad_probs * probs, axis=-1, keepdims=True)
        grad_scores = (probs * (grad_probs - delta)).astype(brain_float_sixteen)
        grad_q_pieces.append(
            jnp.einsum(
                "grqk,kgd->qgrd", grad_scores, keys[:stop], preferred_element_type=single_float
            )
            / root
        )
        key_gradient_rows = key_gradient_rows.at[:stop].add(
            jnp.einsum(
                "grqk,qgrd->kgd",
                grad_scores,
                query_rows[start:stop],
                preferred_element_type=single_float,
            )
            / root
        )
        value_gradient_rows = value_gradient_rows.at[:stop].add(
            jnp.einsum("grqk,qgrd->kgd", probs_low, grad_piece, preferred_element_type=single_float)
        )
    grad_q_rot = jnp.concatenate(grad_q_pieces, axis=0).reshape(token_rows, QUERY_HEADS, HEAD_SIZE)
    grad_q_normed = rotary_embed(grad_q_rot, rotary_cosine, -rotary_sine)
    gradient_key_rownorm = rotary_embed(key_gradient_rows, rotary_cosine, -rotary_sine)
    grad_gain_q = jnp.sum(grad_q_normed * q_scaled, axis=(0, 1))
    grad_gain_k = jnp.sum(gradient_key_rownorm * key_rescaled, axis=(0, 1))
    grad_q_low = (
        norm_backward_pass(grad_q_normed, q_scaled, q_inverse, query_norm_scale)
        .astype(brain_float_sixteen)
        .reshape(token_rows, qw)
    )
    grad_k_low = (
        norm_backward_pass(gradient_key_rownorm, key_rescaled, key_inverse_norm, key_norm_scale)
        .astype(brain_float_sixteen)
        .reshape(token_rows, kw)
    )
    value_gradient_narrow = value_gradient_rows.astype(brain_float_sixteen).reshape(token_rows, kw)
    grad_n_one = (
        jnp.einsum("tc,dc->td", grad_q_low, wq, preferred_element_type=single_float)
        + jnp.einsum("tc,dc->td", grad_k_low, key_matrix, preferred_element_type=single_float)
        + jnp.einsum(
            "tc,dc->td", value_gradient_narrow, value_matrix, preferred_element_type=single_float
        )
    )
    grad_gain_a = jnp.sum(grad_n_one * scaled1, axis=0)
    grad_tokens = (grad_after + norm_backward_pass(grad_n_one, scaled1, inverse1, gain_a)).astype(
        brain_float_sixteen
    )
    gain_sums = lax.psum((grad_gain_q, grad_gain_k, grad_gain_a, grad_gain_m), "fsdp")
    offset = lax.axis_index("fsdp") * share
    attn_gain_share = lax.dynamic_slice_in_dim(gain_sums[2], offset, share)
    mlp_gain_share = lax.dynamic_slice_in_dim(gain_sums[3], offset, share)
    joined_attn = jnp.concatenate([grad_q_low, grad_k_low, value_gradient_narrow], axis=1)
    owned = lax.psum_scatter(
        jnp.concatenate(
            [
                jnp.concatenate(
                    [
                        column_product(first_norm_output, joined_attn),
                        column_product(grad_att, attended),
                    ],
                    axis=1,
                ),
                jnp.concatenate(
                    [column_product(n_two, joined_mlp), column_product(cotangent, hidden)], axis=1
                ),
            ],
            axis=1,
        ),
        "fsdp",
        scatter_dimension=0,
        tiled=True,
    )
    attn_owned = owned[:, : 2 * qw + 2 * kw]
    mlp_owned = owned[:, 2 * qw + 2 * kw :]
    grad_query = attn_owned[:, :qw]
    grad_key = attn_owned[:, qw : qw + kw]
    grad_value = attn_owned[:, qw + kw : qw + 2 * kw]
    grad_out = attn_owned[:, qw + 2 * kw :].T
    grad_gate = mlp_owned[:, :FF]
    grad_up = mlp_owned[:, FF : 2 * FF]
    grad_down = mlp_owned[:, 2 * FF :].T
    return (
        result,
        grad_tokens,
        grad_query,
        grad_key,
        grad_value,
        grad_out,
        grad_gate,
        grad_up,
        grad_down,
        attn_gain_share,
        mlp_gain_share,
        gain_sums[0],
        gain_sums[1],
    )


def solution(mesh):
    in_specs = (
        P("fsdp", None),
        P("fsdp", None),
        P("fsdp", None),
        P("fsdp", None),
        P("fsdp", None),
        P("fsdp", None),
        P(None, "fsdp"),
        P("fsdp", None),
        P("fsdp", None),
        P(None, "fsdp"),
        P("fsdp"),
        P("fsdp"),
        P(),
        P(),
    )
    out_specs = (
        P("fsdp", None),
        P("fsdp", None),
        P("fsdp", None),
        P("fsdp", None),
        P("fsdp", None),
        P(None, "fsdp"),
        P("fsdp", None),
        P("fsdp", None),
        P(None, "fsdp"),
        P("fsdp"),
        P("fsdp"),
        P(),
        P(),
    )
    return jax.shard_map(
        per_device, mesh=mesh, in_specs=in_specs, out_specs=out_specs, check_vma=False
    )
```

profile of v0, /device:TPU:0, one launch (start us, length us, event | category | flops | bytes accessed | tf_op | source)
XLA Modules:
  0.0 1416.2 jit_solution(17387548558261929550)
XLA Ops:
  17.3 42.0 %all-reduce.5 = (bf16[1024]{0:T(1024)(128)(2,1)S(1)}, bf16[1024]{0:T(1024)(128)(2,1)S(1)}) all-reduce(bf16[1024]{0:T(1024)(128)(2,1)S(1)} %dynamic-update-slice.10, bf16[1024]{0:T(1024)(128)(2,1)S(1)} %dynamic-update-slice.11), channel_id=1, replica_groups=mesh['fsdp'=32] {'fsdp'}, use_global_device_ids=true, to_apply=%add.2 | all-reduce | flops 2048 | bytes 8192
  82.4 45.9 %all-gather.8.cloned.1.call-done = bf16[1024,1024]{1,0:T(8,128)(2,1)} async-done(((bf16[32,1024]{1,0:T(8,128)(2,1)}), bf16[1024,1024]{1,0:T(8,128)(2,1)}) %all-gather.8.cloned.1.call-update) | async-done | bytes 2097168 | tf_op jit(solution)/shard_map/all_gather | solution.py:95
  138.0 54.1 %all-gather.12.cloned.1.call-done = bf16[1024,2048]{1,0:T(8,128)(2,1)} async-done(((bf16[32,2048]{1,0:T(8,128)(2,1)}), bf16[1024,2048]{1,0:T(8,128)(2,1)}) %all-gather.12.cloned.1.call-update) | async-done | bytes 4194320 | tf_op jit(solution)/shard_map/all_gather | solution.py:93
  217.6 14.7 %fusion.19 = (f32[8,2,512]{2,1,0:T(2,128)S(1)}, f32[8,1024,512,2]{2,1,3,0:T(8,128)}) fusion(pred[512,1024]{0,1:T(8,128)(4,1)S(1)} %fusion.56, bf16[512,8,2,128]{3,0,2,1:T(8,128)(2,1)S(1)} %bitcast.269, bf16[1024,8,64]{2,0,1:T(8,128)(2,1)S(1)} %copy-done.5, bf16[1024,8,64]{2,0,1:T(8,128)(2,1)S(1)} %get-tuple-element.147), kind=kOutput, calls=%fused_computation.35 | convolution fusion | flops 2176835584 | bytes 38305792 | tf_op jit(solution)/shard_map/qgrd,kgd->grqk/dot_general | solution.py:133
  248.6 10.6 fusion.57
  259.3 14.4 %fusion.3 = f32[8,2,512]{2,1,0:T(2,128)S(1)} fusion(f32[8,2,512]{2,1,0:T(2,128)S(1)} %get-tuple-element.165, f32[8,1024,512,2]{2,1,3,0:T(8,128)} %get-tuple-element.166, pred[512,1024]{0,1:T(8,128)(4,1)S(1)} %fusion.56), kind=kLoop, calls=%fused_computation.10 | loop fusion | flops 33546240 | bytes 34144256 | tf_op jit(solution)/shard_map/reduce_sum | solution.py:154
  273.7 17.2 %fusion.58 = bf16[8,128,2,512]{3,1,2,0:T(8,128)(2,1)} fusion(bf16[1024,8,128,1]{0,2,3,1:T(8,128)(2,1)} %bitcast.275, f32[8,2,512]{2,1,0:T(2,128)S(1)} %fusion.3, f32[8,2,512]{2,1,0:T(2,128)S(1)} %get-tuple-element.165, f32[8,1024,512,2]{2,1,3,0:T(8,128)} %get-tuple-element.166, pred[512,1024]{0,1:T(8,128)(4,1)S(1)} %fusion.56), kind=kOutput, calls=%fused_computation.123 | convolution fusion | flops 2190475264 | bytes 38338560 | tf_op jit(solution)/shard_map/grqk,kgd->qgrd/dot_general | solution.py:157
  301.1 25.1 %all-gather.16.cloned.1.call-done = bf16[1024,3072]{1,0:T(8,128)(2,1)} async-done(((bf16[32,3072]{1,0:T(8,128)(2,1)}), bf16[1024,3072]{1,0:T(8,128)(2,1)}) %all-gather.16.cloned.1.call-update) | async-done | bytes 6291472 | tf_op jit(solution)/shard_map/all_gather | solution.py:97
  326.3 12.4 fusion.95
  338.7 58.4 %all-gather.18.cloned.1.call-done = bf16[1024,3072]{1,0:T(8,128)(2,1)} async-done(((bf16[32,3072]{1,0:T(8,128)(2,1)}), bf16[1024,3072]{1,0:T(8,128)(2,1)}) %all-gather.18.cloned.1.call-update) | async-done | bytes 6291472 | tf_op jit(solution)/shard_map/all_gather | solution.py:98
  397.0 12.4 fusion.96
  409.5 58.5 %all-gather.20.cloned.1.call-done = bf16[3072,1024]{0,1:T(8,128)(2,1)} async-done(((bf16[3072,32]{0,1:T(8,128)(2,1)}), bf16[3072,1024]{0,1:T(8,128)(2,1)}) %all-gather.20.cloned.1.call-update) | async-done | bytes 6291472 | tf_op jit(solution)/shard_map/all_gather | solution.py:99
  468.0 23.1 %multiply_convert_fusion = (bf16[1024,3072]{1,0:T(8,128)(2,1)}, bf16[1024,3072]{1,0:T(8,128)(2,1)}, bf16[1024,3072]{1,0:T(8,128)(2,1)}) fusion(f32[1024,3072]{1,0:T(8,128)} %fusion.95, f32[1024,3072]{1,0:T(8,128)} %fusion.96, bf16[1024,1024]{1,0:T(8,128)(2,1)S(1)} %copy-done.37, bf16[3072,1024]{0,1:T(8,128)(2,1)} %all-gather.20.cloned.1.call-done), kind=kOutput, calls=%fused_computation.30 | convolution fusion | flops 6489636864 | bytes 52428800 | tf_op jit(solution)/shard_map/td,fd->tf/dot_general | solution.py:189
  491.1 10.8 fusion.97
  501.9 10.6 multiply_reduce_fusion.2
  534.9 10.8 fusion.7
  545.8 13.2 fusion.9
  566.6 23.0 %fusion.14 = f32[1024,6144]{1,0:T(8,128)} fusion(bf16[1024,1024]{0,1:T(8,128)(2,1)} %copy-done.38, bf16[1024,3072]{1,0:T(8,128)(2,1)} %get-tuple-element.132, bf16[1024,3072]{1,0:T(8,128)(2,1)} %get-tuple-element.133), kind=kOutput, calls=%fused_computation.26 | convolution fusion | flops 12910067712 | bytes 39845888 | tf_op jit(solution)/shard_map/td,tc->dc/dot_general | solution.py:60
  589.6 11.2 fusion.50
  604.9 25.0 %fusion = (f32[8,2,512]{2,1,0:T(2,128)S(1)}, f32[8,1024,512,2]{2,1,3,0:T(8,128)}) fusion(f32[8,2,512]{2,1,0:T(2,128)S(1)} %bitcast.282, f32[8,1024,512,2]{2,1,3,0:T(8,128)} %get-tuple-element.166, pred[512,1024]{0,1:T(8,128)(4,1)S(1)} %copy-done.2, bf16[1024,8,128,1]{0,2,3,1:T(8,128)(2,1)} %bitcast.276, bf16[512,8,2,128]{0,3,2,1:T(8,128)(2,1)} %bitcast.273), kind=kOutput, calls=%fused_computation.3 | convolution fusion | flops 2189418496 | bytes 71892992 | tf_op jit(solution)/shard_map/qgrd,kgd->grqk/dot_general | solution.py:216
  629.8 17.3 %fusion.47 = bf16[1024,8,128]{0,2,1:T(8,128)(2,1)} fusion(f32[512,8,128]{0,2,1:T(8,128)} %fusion.59, bf16[512,8,2,128]{0,3,2,1:T(8,128)(2,1)} %bitcast.274, f32[8,2,512]{2,1,0:T(2,128)S(1)} %bitcast.283, f32[8,1024,512,2]{2,1,3,0:T(8,128)} %get-tuple-element.166, pred[512,1024]{0,1:T(8,128)(4,1)S(1)} %copy-done.2), kind=kOutput, calls=%fused_computation.86 | convolution fusion | flops 2183135232 | bytes 40402944 | tf_op jit(solution)/shard_map/grqk,qgrd->kgd/dot_general | solution.py:237
  647.2 28.5 %fusion.2 = bf16[8,2,512,1024]{2,3,1,0:T(8,128)(2,1)} fusion(f32[8,1024,512,2]{2,1,3,0:T(8,128)} %get-tuple-element.173, f32[8,2,512]{2,1,0:T(2,128)S(1)} %get-tuple-element.172, f32[8,2,512]{2,1,0:T(2,128)S(1)} %bitcast.284, f32[8,1024,512,2]{2,1,3,0:T(8,128)} %get-tuple-element.166, pred[512,1024]{0,1:T(8,128)(4,1)S(1)} %copy-done.2), kind=kLoop, calls=%fused_computation.5 | loop fusion | flops 50331648 | bytes 84475904 | tf_op jit(solution)/shard_map/convert_element_type | solution.py:220
  675.7 11.7 multiply_bitcast_fusion
  723.9 34.0 %multiply_reduce_fusion = (f32[1024,16]{1,0:T(8,128)S(1)}, f32[1024,16,128]{2,1,0:T(8,128)}) fusion(f32[1024,16,128]{2,1,0:T(8,128)S(1)} %bitcast.256, f32[128]{0:T(128)S(1)} %copy-done.54, f32[1024,16]{1,0:T(8,128)S(1)} %copy-done.22, f32[1024,16,64]{2,1,0:T(8,128)} %get-tuple-element.136, f32[1024,16,64]{2,1,0:T(8,128)S(1)} %get-tuple-element.135), kind=kLoop, calls=%fused_computation.53 | loop fusion | flops 10469376 | bytes 25297408 | tf_op jit(solution)/shard_map/reduce_sum | solution.py:28
  758.7 11.5 bitcast_add_fusion.1
  782.6 12.8 convolution_bitcast_fusion
  817.4 15.6 %fusion.25 = (f32[2048]{0:T(1024)S(1)}, bf16[1024,2048]{1,0:T(8,128)(2,1)}) fusion(f32[1024,2048]{1,0:T(8,128)} %copy-done.12, f32[128,8,16,128]{3,2,1,0:T(8,128)S(1)} %bitcast.259, f32[128,8,16,128]{3,2,1,0:T(8,128)} %bitcast.262, f32[128,8,16,128]{3,2,1,0:T(8,128)} %bitcast.263, f32[2048]{0:T(1024)S(1)} %copy-done.49), kind=kLoop, calls=%fused_computation.43 | loop fusion | flops 16775168 | bytes 37765120 | tf_op jit(solution)/shard_map/reduce_sum | solution.py:242
  833.0 15.1 %fusion.26 = f32[1024,4096]{1,0:T(8,128)} fusion(bf16[1024,1024]{1,0:T(8,128)(2,1)S(1)} %copy-done.39, bf16[1024,1024]{1,0:T(8,128)(2,1)} %copy.143, bf16[1024,2048]{1,0:T(8,128)(2,1)} %get-tuple-element.131, bf16[1024,1024]{0,1:T(8,128)(2,1)S(1)} %copy-done.9, f32[1024]{0:T(1024)S(1)} %copy-done.44, f32[1024]{0:T(1024)S(1)} %copy-done.46), kind=kOutput, calls=%fused_computation.47 | convolution fusion | flops 8619294720 | bytes 27271168 | tf_op jit(solution)/shard_map/td,tc->dc/dot_general | solution.py:60
  848.2 42.3 %pad_maximum_fusion = f32[1024,15360]{1,0:T(8,128)} fusion(f32[1024,3072]{1,0:T(8,128)} %convolution_bitcast_fusion, f32[1024,6144]{1,0:T(8,128)} %fusion.14, f32[1024,2048]{1,0:T(8,128)} %fusion.50, f32[1024,4096]{1,0:T(8,128)} %fusion.26), kind=kLoop, calls=%fused_computation | loop fusion | flops 47185920 | bytes 125829120 | tf_op jit(solution)/shard_map/concatenate | solution.py:272
  890.5 12.6 add_convert_fusion.1
  929.8 39.0 %all-reduce.4 = (f32[1024]{0:T(1024)S(1)}, f32[1024]{0:T(1024)S(1)}, f32[128]{0:T(128)}, f32[128]{0:T(128)}) all-reduce(f32[1024]{0:T(1024)S(1)} %get-tuple-element.118, f32[1024]{0:T(1024)S(1)} %copy-done.55, f32[128]{0:T(128)S(1)} %bitcast_reduce_fusion, f32[128]{0:T(128)S(1)} %bitcast_reduce_fusion.1), channel_id=1, replica_groups=mesh['fsdp'=32] {'fsdp'}, use_global_device_ids=true, to_apply=%region_18.19 | all-reduce | flops 2304 | bytes 18432 | tf_op jit(solution)/shard_map/psum | solution.py:266
  970.0 433.1 %reduce-scatter.2.cloned.1.call-done = f32[32,15360]{1,0:T(8,128)} async-done(((f32[1024,15360]{1,0:T(8,128)}), f32[32,15360]{1,0:T(8,128)}) %reduce-scatter.2.cloned.1.call-update) | async-done | bytes 1966096 | tf_op jit(solution)/shard_map/reduce_scatter | solution.py:271
  (245 shorter events, 232.8 us)
Async XLA Ops:
  7.2 53.3 %copy-start.47 = (s32[1,1024]{1,0:T(1,128)S(1)}, s32[1,1024]{1,0:T(1,128)}, u32[]{:S(2)}) copy-start(s32[1,1024]{1,0:T(1,128)} %param.27) | copy-start | bytes 12292
  7.2 52.6 %copy-start.61 = (bf16[128]{0:T(256)(128)(2,1)S(1)}, bf16[128]{0:T(256)(128)(2,1)}, u32[]{:S(2)}) copy-start(bf16[128]{0:T(256)(128)(2,1)} %param.38) | copy-start | bytes 772
  7.2 53.9 %copy-start.62 = (bf16[128]{0:T(256)(128)(2,1)S(1)}, bf16[128]{0:T(256)(128)(2,1)}, u32[]{:S(2)}) copy-start(bf16[128]{0:T(256)(128)(2,1)} %param.39) | copy-start | bytes 772
  7.2 63.5 %all-gather.10.cloned.1.call-start = ((), (), s32[]{:S(2)}) async-start(), calls=%async_computation.2 | async-start | bytes 2162688 | tf_op jit(solution)/shard_map/all_gather | solution.py:94
  8.0 120.4 %all-gather.8.cloned.1.call-start = ((), (), s32[]{:S(2)}) async-start(), calls=%async_computation.1 | async-start | bytes 2162688 | tf_op jit(solution)/shard_map/all_gather | solution.py:95
  8.7 183.4 %all-gather.12.cloned.1.call-start = ((), (), s32[]{:S(2)}) async-start(), calls=%async_computation.3 | async-start | bytes 4325376 | tf_op jit(solution)/shard_map/all_gather | solution.py:93
  9.5 281.5 %all-gather.14.cloned.1.call-start = ((), (), s32[]{:S(2)}) async-start(), calls=%async_computation.4 | async-start | bytes 4325376 | tf_op jit(solution)/shard_map/all_gather | solution.py:96
  10.0 316.2 %all-gather.16.cloned.1.call-start = ((), (), s32[]{:S(2)}) async-start(), calls=%async_computation.5 | async-start | bytes 6488064 | tf_op jit(solution)/shard_map/all_gather | solution.py:97
  10.6 386.4 %all-gather.18.cloned.1.call-start = ((), (), s32[]{:S(2)}) async-start(), calls=%async_computation.6 | async-start | bytes 6488064 | tf_op jit(solution)/shard_map/all_gather | solution.py:98
  11.2 456.8 %all-gather.20.cloned.1.call-start = ((), (), s32[]{:S(2)}) async-start(), calls=%async_computation.7 | async-start | bytes 6488064 | tf_op jit(solution)/shard_map/all_gather | solution.py:99
  11.9 1391.2 %reduce-scatter.2.cloned.1.call-start = ((), (), s32[]{:S(2)}) async-start(), calls=%async_computation.8 | async-start | bytes 64880640 | tf_op jit(solution)/shard_map/reduce_scatter | solution.py:271
  16.7 111.6 %copy-start.7 = (bf16[1024,1024]{0,1:T(8,128)(2,1)}, bf16[1024,1024]{0,1:T(8,128)(2,1)S(1)}, u32[]{:S(2)}) copy-start(bf16[1024,1024]{0,1:T(8,128)(2,1)S(1)} %copy.107) | copy-start | bytes 6291460
  59.3 132.9 %copy-start.43 = (f32[1024]{0:T(1024)}, f32[1024]{0:T(1024)S(1)}, u32[]{:S(2)}) copy-start(f32[1024]{0:T(1024)S(1)} %convert_element_type.90) | copy-start | bytes 12292
  59.8 132.4 %copy-start.45 = (f32[1024]{0:T(1024)}, f32[1024]{0:T(1024)S(1)}, u32[]{:S(2)}) copy-start(f32[1024]{0:T(1024)S(1)} %add_rsqrt_fusion.3) | copy-start | bytes 12292
  59.8 145.8 %copy-start.53 = (f32[128]{0:T(128)}, f32[128]{0:T(128)S(1)}, u32[]{:S(2)}) copy-start(f32[128]{0:T(128)S(1)} %convert_element_type.95) | copy-start | bytes 1540
  61.1 72.7 %copy-start.51 = (f32[128]{0:T(128)}, f32[128]{0:T(128)S(1)}, u32[]{:S(2)}) copy-start(f32[128]{0:T(128)S(1)} %convert_element_type.93) | copy-start | bytes 1540
  70.0 140.5 %copy-start.19 = (f32[1024,64]{1,0:T(8,128)}, f32[1024,64]{1,0:T(8,128)S(1)}, u32[]{:S(2)}) copy-start(f32[1024,64]{1,0:T(8,128)S(1)} %get-tuple-element.160) | copy-start | bytes 786436
  70.7 203.0 %copy-start.1 = (pred[512,1024]{0,1:T(8,128)(4,1)}, pred[512,1024]{0,1:T(8,128)(4,1)S(1)}, u32[]{:S(2)}) copy-start(pred[512,1024]{0,1:T(8,128)(4,1)S(1)} %fusion.56) | copy-start | bytes 1572868
  82.4 51.5 %copy-start.40 = (f32[1024,8]{0,1:T(8,128)}, f32[1024,8]{0,1:T(8,128)S(1)}, u32[]{:S(2)}) copy-start(f32[1024,8]{0,1:T(8,128)S(1)} %add_rsqrt_fusion.1) | copy-start | bytes 98308
  138.0 94.3 %copy-start.3 = (bf16[1024,8,64]{2,0,1:T(8,128)(2,1)}, bf16[1024,8,64]{2,0,1:T(8,128)(2,1)S(1)}, u32[]{:S(2)}) copy-start(bf16[1024,8,64]{2,0,1:T(8,128)(2,1)S(1)} %get-tuple-element.147) | copy-start | bytes 3145732
  216.4 15.9 %copy-start.23 = (bf16[512,16,128]{2,0,1:T(8,128)(2,1)}, bf16[512,16,128]{2,0,1:T(8,128)(2,1)S(1)}, u32[]{:S(2)}) copy-start(bf16[512,16,128]{2,0,1:T(8,128)(2,1)S(1)} %copy.111) | copy-start | bytes 6291460
  217.0 15.3 %copy-start.17 = (bf16[512,16,128]{2,0,1:T(8,128)(2,1)}, bf16[512,16,128]{2,0,1:T(8,128)(2,1)S(1)}, u32[]{:S(2)}) copy-start(bf16[512,16,128]{2,0,1:T(8,128)(2,1)S(1)} %copy.109) | copy-start | bytes 6291460
  273.7 17.3 %copy-start.8 = (bf16[1024,1024]{0,1:T(8,128)(2,1)S(1)}, bf16[1024,1024]{0,1:T(8,128)(2,1)}, u32[]{:S(2)}) copy-start(bf16[1024,1024]{0,1:T(8,128)(2,1)} %copy-done.7) | copy-start | bytes 6291460
  301.1 25.2 %copy-start.38 = (bf16[1024,1024]{0,1:T(8,128)(2,1)}, bf16[1024,1024]{0,1:T(8,128)(2,1)S(1)}, u32[]{:S(2)}) copy-start(bf16[1024,1024]{0,1:T(8,128)(2,1)S(1)} %multiply_convert_fusion.3) | copy-start | bytes 6291460
  338.7 129.3 %copy-start.37 = (bf16[1024,1024]{1,0:T(8,128)(2,1)S(1)}, bf16[1024,1024]{1,0:T(8,128)(2,1)}, u32[]{:S(2)}) copy-start(bf16[1024,1024]{1,0:T(8,128)(2,1)} %param.28) | copy-start | bytes 6291460
  545.8 13.3 copy-start.4
  545.8 13.3 copy-start.6
  782.6 12.9 copy-start.24
  817.4 15.6 %copy-start.9 = (bf16[1024,1024]{0,1:T(8,128)(2,1)S(1)}, bf16[1024,1024]{0,1:T(8,128)(2,1)}, u32[]{:S(2)}) copy-start(bf16[1024,1024]{0,1:T(8,128)(2,1)} %copy-done.7) | copy-start | bytes 6291460
  817.4 15.6 %copy-start.39 = (bf16[1024,1024]{1,0:T(8,128)(2,1)S(1)}, bf16[1024,1024]{1,0:T(8,128)(2,1)}, u32[]{:S(2)}) copy-start(bf16[1024,1024]{1,0:T(8,128)(2,1)} %copy.190) | copy-start | bytes 6291460
  817.4 15.6 %copy-start.44 = (f32[1024]{0:T(1024)S(1)}, f32[1024]{0:T(1024)}, u32[]{:S(2)}) copy-start(f32[1024]{0:T(1024)} %copy-done.43) | copy-start | bytes 12292
  817.4 15.6 %copy-start.46 = (f32[1024]{0:T(1024)S(1)}, f32[1024]{0:T(1024)}, u32[]{:S(2)}) copy-start(f32[1024]{0:T(1024)} %copy-done.45) | copy-start | bytes 12292
  (43 other events, 269.2 us)
Sparse Core Ops, SparseCore 0:
  10.9 59.1 all-gather.9
  73.0 55.2 all-gather.7
  131.2 60.8 all-gather.11
  194.8 60.5 all-gather.13
  258.2 68.0 all-gather.15
  329.0 68.0 all-gather.17
  399.9 68.0 all-gather.19
  890.6 512.4 reduce-scatter.1
where the time goes:
time: 1430 us; the launch traced here: 1420 us
  waiting for transfers between devices  679 us (47%)
  matrix products  333 us (23%)
  other arithmetic  209 us (15%)
  local copies, waits for them, and re-layouts  97.1 us (7%)
  blocking collectives  81 us (6%)
  between operations  16.2 us (1%)
    reduce_scatter x1, waiting for transfers between devices, per_device(): lax.psum_scatter(jnp.concatenate([jnp.concatenate([column_product(first_n...  433 us
    dot_general x4, matrix products, column_product(): jnp.einsum('td,tc->dc', left, right, preferred_element_type=jnp.float32)  62.2 us
    all_gather x1, waiting for transfers between devices, per_device(): lax.all_gather(w_down, 'fsdp', axis=1, tiled=True)  58.5 us
    all_gather x1, waiting for transfers between devices, per_device(): lax.all_gather(w_up, 'fsdp', axis=0, tiled=True)  58.4 us
    all_gather x1, waiting for transfers between devices, per_device(): lax.all_gather(w_query, 'fsdp', axis=0, tiled=True)  54.1 us
    all_gather x1, waiting for transfers between devices, per_device(): lax.all_gather(w_value, 'fsdp', axis=0, tiled=True)  45.9 us
    unnamed x145, local copies, waits for them, and re-layouts  43.2 us
    concatenate x1, other arithmetic, per_device(): jnp.concatenate([jnp.concatenate([column_product(first_norm_output, joine...  42.3 us
  transfers between devices with their start and end apart: 8, of which 6 were waited for; matrix products, arithmetic and copies ran while one was open for 14% of the time, Pallas kernels for 0%

commit v1 on v0

v1 whole, which is shorter than its diff:
```python
import functools
import math

import jax
import jax.numpy as jnp
from jax import lax
from jax.experimental import pallas as pl
from jax.experimental.pallas import tpu as pltpu
from jax.sharding import PartitionSpec as P

AX = "fsdp"
D = 1024
HALF = D // 2
QUERY_HEADS = 16
KEY_VALUE_HEADS = 8
HEAD_SIZE = 128
FF = 3072
PART = FF // 2
GROUP = QUERY_HEADS // KEY_VALUE_HEADS
QW = QUERY_HEADS * HEAD_SIZE
KW = KEY_VALUE_HEADS * HEAD_SIZE
LONGEST = 512
BLK = 256
COLS = 512
EPS = 1e-06
THETA = 1000000.0
ROOT = math.sqrt(HEAD_SIZE)
SCALE2 = math.log2(math.e) / ROOT
VMEM = 56 * 1024 * 1024
F32 = jnp.float32
B16 = jnp.bfloat16


def axes_of(n):
    out, stride = [(1, 2)], 2
    for radix in (2, 2, 4, 4, 4, 4):
        if stride * radix <= n:
            out.append((stride, radix))
            stride *= radix
    while stride < n:
        out.append((stride, 2))
        stride *= 2
    return out


def move(value, n, axis, k):
    s, r = axis
    pairs = [(i, i + ((i // s % r + k) % r - i // s % r) * s) for i in range(n)]
    return lax.ppermute(value, AX, pairs)


def orders(n):
    m = len(axes_of(n)) - 1
    if m == 3:
        return [(2, 0, 1), (2, 1, 0), (0, 2, 1), (1, 2, 0)]
    return [tuple(range(m))[::-1]] * 4


def gather(value, n, order):
    ax = axes_of(n)[1:]
    rows, cols = value.shape
    value = value.reshape((1,) * len(ax) + value.shape)
    for a in order:
        cur, got = value, [value]
        for _ in range(ax[a][1] - 1):
            cur = move(cur, n, ax[a], -1)
            got.append(cur)
        value = jnp.concatenate(got, axis=a)
    value = value.reshape(rows * n // 2, cols)
    return value, move(value, n, (1, 2), 1)


def scatter(keep, give, n, order):
    ax = axes_of(n)[1:]
    rows, cols = keep.shape
    acc = keep.astype(F32) + move(give, n, (1, 2), 1).astype(F32)
    acc = acc.astype(B16).reshape(tuple(r for _, r in ax) + (rows * 2 // n, cols))
    for place, a in enumerate(order):
        r = ax[a][1]
        run = lax.index_in_dim(acc, r - 1, a, keepdims=True)
        for j in range(r - 2, -1, -1):
            mine = lax.index_in_dim(acc, j, a, keepdims=True).astype(F32)
            run = move(run, n, ax[a], 1).astype(F32) + mine
            if j > 0 or place < len(order) - 1:
                run = run.astype(B16)
        acc = run
    return acc.reshape(rows * 2 // n, cols)


def absolute_rows(n):
    ax = axes_of(n)
    me = lax.axis_index(AX)
    share = D // n
    place = lax.broadcasted_iota(jnp.int32, (D,), 0)
    rem = place // share
    owner = jnp.zeros_like(place)
    for s, r in ax[:0:-1]:
        owner = owner + ((me // s + rem % r) % r) * s
        rem = rem // r
    owner = owner + (me + rem) % 2
    return owner * share + place % share


def sum_all(value, n):
    step = 1
    while step < n:
        value = value + lax.ppermute(value, AX, [(i, i ^ step) for i in range(n)])
        step *= 2
    return value


def call(kernel, grid, ins, outs, shapes, scratch=(), flops=0, moved=0, name=None):
    return pl.pallas_call(
        kernel,
        grid=grid,
        in_specs=ins,
        out_specs=outs,
        out_shape=shapes,
        scratch_shapes=list(scratch),
        compiler_params=pltpu.CompilerParams(vmem_limit_bytes=VMEM),
        cost_estimate=pl.CostEstimate(flops=flops, bytes_accessed=moved, transcendentals=0),
        name=name,
    )


def whole(shape):
    return pl.BlockSpec(shape, lambda *_: (0,) * len(shape))


def rows_of(cols, blk=BLK):
    return pl.BlockSpec((blk, cols), lambda i: (i, 0))


def sds(shape, dtype):
    return jax.ShapeDtypeStruct(shape, dtype)


def nn(a, b):
    return lax.dot_general(a, b, (((1,), (0,)), ((), ())), preferred_element_type=F32)


def nt(a, b):
    return lax.dot_general(a, b, (((1,), (1,)), ((), ())), preferred_element_type=F32)


def inv_rms(x):
    return lax.rsqrt(jnp.mean(x * x, axis=-1, keepdims=True) + EPS)


def prep_kernel(tok, cot, perm, gain, trel, crel, n1):
    t = nn(tok[...], perm[...])
    trel[...] = t.astype(B16)
    n1[...] = (t * inv_rms(t) * gain[...]).astype(B16)
    crel[...] = nn(cot[...], perm[...]).astype(B16)


def prep(tokens, cotangent, perm, gain):
    t = tokens.shape[0]
    return call(
        prep_kernel,
        (t // BLK,),
        [rows_of(D), rows_of(D), whole((D, D)), whole((1, D))],
        [rows_of(D)] * 3,
        [sds((t, D), B16)] * 3,
        flops=4 * t * D * D,
        moved=12 * t * D,
        name="prep",
    )(tokens, cotangent, perm, gain)


def project_kernel(n1, wa, wb, cos, sin, gain, out, raw):
    for i in range(n1.shape[0] // BLK):
        at = pl.ds(i * BLK, BLK)
        x = nn(n1[at, :HALF], wa[...]) + nn(n1[at, HALF:], wb[...])
        raw[at, :] = x.astype(B16)
        for h in range(COLS // HEAD_SIZE):
            lanes = slice(h * HEAD_SIZE, (h + 1) * HEAD_SIZE)
            y = x[:, lanes]
            y = y * inv_rms(y) * gain[...]
            y = y * cos[at, :] + pltpu.roll(y, HEAD_SIZE // 2, 1) * sin[at, :]
            out[at, lanes] = y.astype(B16)


def project(n1, w, cos, sin, gain):
    t, cols = n1.shape[0], w[0].shape[1]
    wide = pl.BlockSpec((HALF, COLS), lambda j: (0, j))
    tall = pl.BlockSpec((t, COLS), lambda j: (0, j))
    return call(
        project_kernel,
        (cols // COLS,),
        [whole((t, D)), wide, wide, whole((t, HEAD_SIZE)), whole((t, HEAD_SIZE)), whole((1, HEAD_SIZE))],
        [tall, tall],
        [sds((t, cols), B16)] * 2,
        flops=2 * t * D * cols,
        moved=2 * (t * D + D * cols + 2 * t * cols),
        name="project",
    )(n1, *w, cos, sin, gain)


def plain_kernel(n1, wa, wb, out):
    out[...] = (nn(n1[:, :HALF], wa[...]) + nn(n1[:, HALF:], wb[...])).astype(B16)


def project_plain(n1, w):
    t, cols = n1.shape[0], w[0].shape[1]
    wide = pl.BlockSpec((HALF, COLS), lambda j: (0, j))
    return call(
        plain_kernel,
        (cols // COLS,),
        [whole((t, D)), wide, wide],
        pl.BlockSpec((t, COLS), lambda j: (0, j)),
        sds((t, cols), B16),
        flops=2 * t * D * cols,
        moved=2 * (t * D + D * cols + t * cols),
        name="project_plain",
    )(n1, *w)


def build_bias(first, bias):
    t = bias.shape[0]
    for i in range(t // BLK):
        at = slice(i * BLK, (i + 1) * BLK)
        key = lax.broadcasted_iota(jnp.int32, (t, BLK), 0)
        query = lax.broadcasted_iota(jnp.int32, (t, BLK), 1) + i * BLK
        allowed = (key >= first[:, at]) & (key <= query)
        bias[:, at] = jnp.where(allowed, 0.0, -1e30)


def window(i):
    return slice(max(0, i - LONGEST // BLK) * BLK, (i + 1) * BLK)


def stacked(ref, at):
    return jnp.concatenate([ref[at, :HEAD_SIZE], ref[at, HEAD_SIZE:]], axis=0)


def attend_kernel(q, k, v, first, out, lse, bias):
    @pl.when(pl.program_id(0) == 0)
    def _():
        build_bias(first, bias)

    vt = v[...].T
    for i in range(q.shape[0] // BLK):
        at = slice(i * BLK, (i + 1) * BLK)
        keys = window(i)
        s = nt(k[keys, :], stacked(q, at))
        b = bias[keys, at]
        e = jnp.exp2(s * SCALE2 + jnp.concatenate([b, b], axis=1))
        total = jnp.sum(e, axis=0, keepdims=True)
        o = (nn(vt[:, keys], e.astype(B16)) * (1.0 / total)).T.astype(B16)
        level = jnp.log2(total)
        for r in range(GROUP):
            mine = slice(r * BLK, (r + 1) * BLK)
            out[at, r * HEAD_SIZE : (r + 1) * HEAD_SIZE] = o[mine, :]
            lse[0, r : r + 1, at] = level[:, mine]


def attend(q, k, v, first):
    t = k.shape[0]
    pair = GROUP * HEAD_SIZE
    groups = k.shape[1] // HEAD_SIZE
    head = pl.BlockSpec((t, HEAD_SIZE), lambda g: (0, g))
    both = pl.BlockSpec((t, pair), lambda g: (0, g))
    return call(
        attend_kernel,
        (groups,),
        [both, head, head, whole((1, t))],
        [both, pl.BlockSpec((1, GROUP, t), lambda g: (g, 0, 0))],
        [sds((t, groups * pair), B16), sds((groups, GROUP, t), F32)],
        [pltpu.VMEM((t, t), F32)],
        flops=8 * groups * t * t * pair,
        moved=12 * t * groups * HEAD_SIZE,
        name="attend",
    )(q, k, v, first)


def after_kernel(o, wa, wb, trel, gain, x1, n2):
    x = jnp.concatenate([nt(o[...], wa[...]), nt(o[...], wb[...])], axis=1)
    x = x + trel[...].astype(F32)
    x1[...] = x
    n2[...] = (x * inv_rms(x) * gain[...]).astype(B16)


def after_attention(o, w, trel, gain):
    t = o.shape[0]
    return call(
        after_kernel,
        (t // BLK,),
        [rows_of(QW), whole((HALF, QW)), whole((HALF, QW)), rows_of(D), whole((1, D))],
        [rows_of(D), rows_of(D)],
        [sds((t, D), F32), sds((t, D), B16)],
        flops=2 * t * D * QW,
        moved=2 * (t * QW + D * QW + 4 * t * D),
        name="after_attention",
    )(o, *w, trel, gain)


def mlp_kernel(n2, c, ga, gb, ua, ub, da, db, hidden, dgate, dup):
    for i in range(n2.shape[0] // BLK):
        at = slice(i * BLK, (i + 1) * BLK)
        n_a, n_b = n2[at, :HALF], n2[at, HALF:]
        gate = nn(n_a, ga[...]) + nn(n_b, gb[...])
        up = nn(n_a, ua[...]) + nn(n_b, ub[...])
        dh = nn(c[at, :HALF], da[...]) + nn(c[at, HALF:], db[...])
        sig = jax.nn.sigmoid(gate)
        silu = gate * sig
        hidden[at, :] = (silu * up).astype(B16)
        dgate[at, :] = (dh * up * sig * (1.0 + gate * (1.0 - sig))).astype(B16)
        dup[at, :] = (dh * silu).astype(B16)


def mlp(n2, c, wg, wu, wd):
    t, cols = n2.shape[0], wg[0].shape[1]
    wide = pl.BlockSpec((HALF, COLS), lambda j: (0, j))
    return call(
        mlp_kernel,
        (cols // COLS,),
        [whole((t, D))] * 2 + [wide] * 6,
        [pl.BlockSpec((t, COLS), lambda j: (0, j))] * 3,
        [sds((t, cols), B16)] * 3,
        flops=6 * t * D * cols,
        moved=2 * (2 * t * D + 3 * D * cols + 3 * t * cols),
        name="mlp",
    )(n2, c, *wg, *wu, *wd)


def result_kernel(x1, perm, *refs):
    *pairs, out = refs
    lower, upper = x1[:, :HALF], x1[:, HALF:]
    for i in range(0, len(pairs), 3):
        h, wa, wb = pairs[i : i + 3]
        lower = lower + nt(h[...], wa[...])
        upper = upper + nt(h[...], wb[...])
    x = jnp.concatenate([lower, upper], axis=1).astype(B16)
    out[...] = nt(x, perm[...]).astype(B16)


def make_result(x1, perm, terms):
    t = x1.shape[0]
    specs, args = [], []
    for h, w in terms:
        specs += [rows_of(h.shape[1]), whole(w[0].shape), whole(w[1].shape)]
        args += [h, *w]
    return call(
        result_kernel,
        (t // BLK,),
        [rows_of(D), whole((D, D))] + specs,
        rows_of(D),
        sds((t, D), B16),
        flops=2 * t * D * (FF + D),
        moved=2 * (t * FF + D * FF + 3 * t * D + D * D),
        name="result",
    )(x1, perm, *args)


def mlp_back_kernel(x1, crel, gain, *refs):
    *pairs, dx1, datt = refs
    lower = upper = 0.0
    for i in range(0, len(pairs), 3):
        h, wa, wb = pairs[i : i + 3]
        lower = lower + nt(h[...], wa[...])
        upper = upper + nt(h[...], wb[...])
    x = x1[...]
    s = inv_rms(x)
    r = x * s
    grad = jnp.concatenate([lower, upper], axis=1) * gain[...]
    inner = jnp.mean(grad * r, axis=-1, keepdims=True)
    d = crel[...].astype(F32) + s * (grad - r * inner)
    dx1[...] = d
    datt[...] = d.astype(B16)


def mlp_back(x1, crel, gain, terms):
    t = x1.shape[0]
    specs, args = [], []
    for h, w in terms:
        specs += [rows_of(h.shape[1]), whole(w[0].shape), whole(w[1].shape)]
        args += [h, *w]
    return call(
        mlp_back_kernel,
        (t // BLK,),
        [rows_of(D), rows_of(D), whole((1, D))] + specs,
        [rows_of(D), rows_of(D)],
        [sds((t, D), F32), sds((t, D), B16)],
        flops=4 * t * D * FF,
        moved=4 * (t * FF + D * FF + 3 * t * D),
        name="mlp_back",
    )(x1, crel, gain, *args)


def head_back(dy, raw, cos, sin, gain):
    dn = dy * cos - pltpu.roll(dy, HEAD_SIZE // 2, 1) * sin
    x = raw.astype(F32)
    s = inv_rms(x)
    r = x * s
    grad = dn * gain
    inner = jnp.mean(grad * r, axis=-1, keepdims=True)
    return (s * (grad - r * inner)).astype(B16), jnp.sum(dn * r, axis=0, keepdims=True)


def attend_back_kernel(
    datt, wa, wb, q, k, v, rawq, rawk, lse, first, cos, sin, qgain, kgain,
    dq, dk, dv, gains, bias, do, dk_sum, dv_sum,
):
    @pl.when(pl.program_id(0) == 0)
    def _():
        build_bias(first, bias)
        gains[...] = jnp.zeros_like(gains)

    t = q.shape[0]
    for i in range(t // BLK):
        at = slice(i * BLK, (i + 1) * BLK)
        do[at, :] = (nn(datt[at, :HALF], wa[...]) + nn(datt[at, HALF:], wb[...])).astype(B16)
    kt = k[...].T
    dk_sum[...] = jnp.zeros_like(dk_sum)
    dv_sum[...] = jnp.zeros_like(dv_sum)
    for i in range(t // BLK):
        at = slice(i * BLK, (i + 1) * BLK)
        keys = window(i)
        q2, do2 = stacked(q, at), stacked(do, at)
        b = bias[keys, at]
        level = jnp.concatenate([lse[0, r : r + 1, at] for r in range(GROUP)], axis=1)
        s = nt(k[keys, :], q2)
        p = jnp.exp2(s * SCALE2 + jnp.concatenate([b, b], axis=1) - level)
        dp = nt(v[keys, :], do2)
        delta = jnp.sum(dp * p, axis=0, keepdims=True)
        ds = (p * (dp - delta)).astype(B16)
        dv_sum[keys, :] += nn(p.astype(B16), do2)
        dk_sum[keys, :] += nn(ds, q2)
        dq2 = nn(kt[:, keys], ds).T * (1.0 / ROOT)
        for r in range(GROUP):
            lanes = slice(r * HEAD_SIZE, (r + 1) * HEAD_SIZE)
            low, part = head_back(
                dq2[r * BLK : (r + 1) * BLK, :], rawq[at, lanes], cos[at, :], sin[at, :], qgain[...]
            )
            dq[at, lanes] = low
            gains[0:1, :] += part
    for i in range(t // BLK):
        at = slice(i * BLK, (i + 1) * BLK)
        low, part = head_back(
            dk_sum[at, :] * (1.0 / ROOT), rawk[at, :], cos[at, :], sin[at, :], kgain[...]
        )
        dk[at, :] = low
        gains[1:2, :] += part
    dv[...] = dv_sum[...].astype(B16)


def attend_back(datt, w, q, k, v, rawq, rawk, lse, first, cos, sin, qgain, kgain):
    t = k.shape[0]
    pair = GROUP * HEAD_SIZE
    groups = k.shape[1] // HEAD_SIZE
    head = pl.BlockSpec((t, HEAD_SIZE), lambda g: (0, g))
    both = pl.BlockSpec((t, pair), lambda g: (0, g))
    wide = pl.BlockSpec((HALF, pair), lambda g: (0, g))
    table = whole((t, HEAD_SIZE))
    gain = whole((1, HEAD_SIZE))
    return call(
        attend_back_kernel,
        (groups,),
        [whole((t, D)), wide, wide, both, head, head, both, head,
         pl.BlockSpec((1, GROUP, t), lambda g: (g, 0, 0)), whole((1, t)), table, table, gain, gain],
        [both, head, head, whole((8, HEAD_SIZE))],
        [sds((t, groups * pair), B16), sds((t, groups * HEAD_SIZE), B16),
         sds((t, groups * HEAD_SIZE), B16), sds((8, HEAD_SIZE), F32)],
        [pltpu.VMEM((t, t), F32), pltpu.VMEM((t, pair), B16),
         pltpu.VMEM((t, HEAD_SIZE), F32), pltpu.VMEM((t, HEAD_SIZE), F32)],
        flops=2 * t * D * groups * pair + 10 * groups * t * t * pair,
        moved=2 * (t * D + D * groups * pair) + 24 * t * groups * HEAD_SIZE,
        name="attend_back",
    )(datt, *w, q, k, v, rawq, rawk, lse, first, cos, sin, qgain, kgain)


def weight_grad_kernel(x, g, out, xt):
    @pl.when(pl.program_id(0) == 0)
    def _():
        xt[...] = x[...].T

    out[...] = nn(xt[...], g[...]).astype(B16)


def weight_grad(x, half, g, col0=0, cols=None):
    t = x.shape[0]
    cols = g.shape[1] if cols is None else cols
    return call(
        weight_grad_kernel,
        (cols // COLS,),
        [pl.BlockSpec((t, HALF), lambda j: (0, half)),
         pl.BlockSpec((t, COLS), lambda j: (0, j + col0 // COLS))],
        pl.BlockSpec((HALF, COLS), lambda j: (0, j)),
        sds((HALF, cols), B16),
        [pltpu.VMEM((HALF, t), B16)],
        flops=2 * t * HALF * cols,
        moved=2 * (t * HALF + t * cols + HALF * cols),
        name="weight_grad",
    )(x, g)


def input_back_kernel(trel, dx1, gain, perm, *refs):
    *pairs, out = refs
    lower = upper = 0.0
    for i in range(0, len(pairs), 3):
        h, wa, wb = pairs[i : i + 3]
        lower = lower + nt(h[...], wa[...])
        upper = upper + nt(h[...], wb[...])
    x = trel[...].astype(F32)
    s = inv_rms(x)
    r = x * s
    grad = jnp.concatenate([lower, upper], axis=1) * gain[...]
    inner = jnp.mean(grad * r, axis=-1, keepdims=True)
    d = (dx1[...] + s * (grad - r * inner)).astype(B16)
    out[...] = nt(d, perm[...]).astype(B16)


def input_back(trel, dx1, gain, perm, terms):
    t = trel.shape[0]
    specs, args = [], []
    for h, at, w in terms:
        cols = w[0].shape[1]
        specs += [pl.BlockSpec((BLK, cols), lambda i, at=at: (i, at)), whole(w[0].shape), whole(w[1].shape)]
        args += [h, *w]
    return call(
        input_back_kernel,
        (t // BLK,),
        [rows_of(D), rows_of(D), whole((1, D)), whole((D, D))] + specs,
        rows_of(D),
        sds((t, D), B16),
        flops=2 * t * D * (QW + 2 * KW + D),
        moved=2 * (t * (QW + 2 * KW) + D * (QW + 2 * KW) + 4 * t * D + D * D),
        name="input_back",
    )(trel, dx1, gain, perm, *args)


def run_starts(segment_row):
    index = jnp.arange(segment_row.shape[0], dtype=jnp.int32)
    previous = jnp.concatenate([segment_row[:1] - 1, segment_row[:-1]])
    return index, lax.cummax(jnp.where(segment_row != previous, index, 0), axis=0)


def per_device(
    n, tokens, segments, cotangent, w_query, w_key, w_value, w_out, w_gate, w_up, w_down,
    attn_gain, mlp_gain, q_gain, k_gain,
):
    share = D // n
    od = orders(n)
    both = jnp.concatenate([attn_gain, mlp_gain]).reshape(1, 2 * share)
    ga, gb = gather(both, n, od[0])
    gains = jnp.concatenate([ga, gb], axis=0).astype(F32)
    gain_a = gains[:, :share].reshape(1, D)
    gain_m = gains[:, share:].reshape(1, D)
    wq = [gather(w_query[:, :KW], n, od[0]), gather(w_query[:, KW:], n, od[1])]
    wk = gather(w_key, n, od[2])
    wv = gather(w_value, n, od[3])
    out_t, down_t = w_out.T, w_down.T
    wo = gather(out_t, n, od[0])
    wg, wu, wd = [], [], []
    for i in range(2):
        cols = slice(i * PART, (i + 1) * PART)
        wg.append(gather(w_gate[:, cols], n, od[(1 + i) % 4]))
        wu.append(gather(w_up[:, cols], n, od[(2 + i) % 4]))
        wd.append(gather(down_t[:, cols], n, od[(3 + i) % 4]))

    index, first = run_starts(segments[0])
    half = HEAD_SIZE // 2
    freq = THETA ** (-jnp.arange(half, dtype=F32) / half)
    turned = (index - first).astype(F32)[:, None] * freq[None, :]
    cos, sin = jnp.cos(turned), jnp.sin(turned)
    cos = jnp.concatenate([cos, cos], axis=1)
    sin = jnp.concatenate([-sin, sin], axis=1)
    first = first.reshape(1, -1)
    qg = q_gain.astype(F32).reshape(1, HEAD_SIZE)
    kg = k_gain.astype(F32).reshape(1, HEAD_SIZE)
    perm = (jnp.arange(D, dtype=jnp.int32)[:, None] == absolute_rows(n)[None, :]).astype(B16)

    trel, crel, n1 = prep(tokens, cotangent, perm, gain_a)
    q0, rawq0 = project(n1, wq[0], cos, sin, qg)
    q1, rawq1 = project(n1, wq[1], cos, sin, qg)
    k, rawk = project(n1, wk, cos, sin, kg)
    v = project_plain(n1, wv)
    q = jnp.concatenate([q0, q1], axis=1)
    rawq = jnp.concatenate([rawq0, rawq1], axis=1)
    o, lse = attend(q, k, v, first)
    x1, n2 = after_attention(o, wo, trel, gain_m)

    acts = [mlp(n2, crel, wg[i], wu[i], wd[i]) for i in range(2)]
    sums = {}

    def send(key, x, g, order, col0=0, cols=None):
        give = weight_grad(x, 1, g, col0, cols)
        keep = weight_grad(x, 0, g, col0, cols)
        sums[key] = scatter(keep, give, n, od[order][::-1])

    for i, (hidden, dgate, dup) in enumerate(acts):
        send(("down", i), crel, hidden, 2 * i)
        send(("gate", i), n2, dgate, 2 * i + 1)
        send(("up", i), n2, dup, 2 - 2 * i)
    dx1, datt = mlp_back(
        x1, crel, gain_m, [(a[1], w) for a, w in zip(acts, wg)] + [(a[2], w) for a, w in zip(acts, wu)]
    )
    send("out", datt, o, 3)
    dq, dk, dv, head_gains = attend_back(
        datt, wo, q, k, v, rawq, rawk, lse, first, cos, sin, qg, kg
    )
    send(("q", 0), n1, dq, 0, 0, KW)
    send(("q", 1), n1, dq, 1, KW, KW)
    send("k", n1, dk, 2)
    send("v", n1, dv, 3)
    head_gains = sum_all(head_gains, n)
    grad_tokens = input_back(
        trel, dx1, gain_a, perm, [(dq, 0, wq[0]), (dq, 1, wq[1]), (dk, 0, wk), (dv, 0, wv)]
    )
    result = make_result(x1, perm, [(a[0], w) for a, w in zip(acts, wd)])

    grad_query = jnp.concatenate([sums["q", 0], sums["q", 1]], axis=1)
    grad_gate, grad_up, grad_down = [
        jnp.concatenate([sums[key, 0], sums[key, 1]], axis=1) for key in ("gate", "up", "down")
    ]

    def gain_grad(gain, *pairs):
        return sum(jnp.sum(w.astype(F32) * g, axis=1) for w, g in pairs) / gain.astype(F32)

    return (
        result,
        grad_tokens,
        grad_query,
        sums["k"],
        sums["v"],
        sums["out"].T,
        grad_gate,
        grad_up,
        grad_down.T,
        gain_grad(attn_gain, (w_query, grad_query), (w_key, sums["k"]), (w_value, sums["v"])),
        gain_grad(mlp_gain, (w_gate, grad_gate), (w_up, grad_up)),
        head_gains[0],
        head_gains[1],
    )


def solution(mesh):
    n = mesh.shape[AX]
    rows, cols, one = P(AX, None), P(None, AX), P(AX)
    in_specs = (rows, rows, rows, rows, rows, rows, cols, rows, rows, cols, one, one, P(), P())
    out_specs = (rows, rows, rows, rows, rows, cols, rows, rows, cols, one, one, P(), P())
    return jax.shard_map(
        functools.partial(per_device, n), mesh=mesh, in_specs=in_specs, out_specs=out_specs, check_vma=False
    )
```

time: 1430 us -> 868 us (0.61)
  waiting for transfers between devices: 679 us -> 340 us
  matrix products: 333 us -> 0 us
  Pallas kernels: 0 us -> 316 us
  other arithmetic: 209 us -> 39.6 us
  starting transfers between devices: 0.3 us -> 144 us
  local copies, waits for them, and re-layouts: 97.1 us -> 15.8 us
  blocking collectives: 81 us -> 0 us
    reduce_scatter x1 -> x0, waiting for transfers between devices: 433 us -> none  [per_device(): lax.psum_scatter(jnp.concatenate([jnp.concatenate([column_product(first_n...]
    ppermute x0 -> x143, waiting for transfers between devices: none -> 340 us  [the longest x138 340 us: move(): return lax.ppermute(value, AX, pairs)]
    dot_general x30 -> x0, matrix products: 333 us -> none  [the longest x4 62.2 us: column_product(): jnp.einsum('td,tc->dc', left, right, preferred_element_type=jnp.float32)]
    pallas_call x0 -> x35, Pallas kernels: none -> 316 us  [the longest x22 114 us: weight_grad(): call(weight_grad_kernel, (cols // COLS,), [pl.BlockSpec((t, HALF), lambda...]
    all_gather x7 -> x0, waiting for transfers between devices: 242 us -> none  [the longest x1 58.5 us: per_device(): lax.all_gather(w_down, 'fsdp', axis=1, tiled=True)]
    ppermute x0 -> x143, starting transfers between devices: none -> 144 us  [the longest x138 139 us: move(): return lax.ppermute(value, AX, pairs)]
    reduce_sum x10 -> x5, other arithmetic: 84.5 us -> 4.19 us  [gain_grad(): jnp.sum(w.astype(F32) * g, axis=1)]
    unnamed x1 -> x0, blocking collectives: 42 us -> none
  transfers between devices with their start and end apart: 8 -> 143, of which waited for: 6 -> 66; matrix products, arithmetic and copies ran while one was open for 14% -> 6% of each run, Pallas kernels for 0% -> 20%
where the time goes in v1:
time: 868 us; the launch traced here: 859 us
  waiting for transfers between devices  340 us (39%)
  Pallas kernels  316 us (36%)
  starting transfers between devices  144 us (17%)
  other arithmetic  39.6 us (5%)
  local copies, waits for them, and re-layouts  15.8 us (2%)
    ppermute x138, waiting for transfers between devices, move(): return lax.ppermute(value, AX, pairs)  340 us
    ppermute x138, starting transfers between devices, move(): return lax.ppermute(value, AX, pairs)  139 us
    pallas_call x22, Pallas kernels, weight_grad(): call(weight_grad_kernel, (cols // COLS,), [pl.BlockSpec((t, HALF), lambda...  114 us
    pallas_call x1, Pallas kernels, attend_back(): call(attend_back_kernel, (groups,), [whole((t, D)), wide, wide, both, hea...  51.1 us
    pallas_call x2, Pallas kernels, mlp(): call(mlp_kernel, (cols // COLS,), [whole((t, D))] * 2 + [wide] * 6, [pl.B...  33.9 us
    pallas_call x1, Pallas kernels, mlp_back(): call(mlp_back_kernel, (t // BLK,), [rows_of(D), rows_of(D), whole((1, D))...  22.5 us
    pallas_call x3, Pallas kernels, project(): call(project_kernel, (cols // COLS,), [whole((t, D)), wide, wide, whole((...  20.2 us
    pallas_call x1, Pallas kernels, input_back(): call(input_back_kernel, (t // BLK,), [rows_of(D), rows_of(D), whole((1, D...  19.1 us
  transfers between devices with their start and end apart: 143, of which 66 were waited for; matrix products, arithmetic and copies ran while one was open for 6% of the time, Pallas kernels for 20%

profile of v1, /device:TPU:0, one launch (start us, length us, event | category | flops | bytes accessed | tf_op | source)
XLA Modules:
  0.0 858.8 jit_solution(2367671472852590931)
XLA Ops:
  36.9 8.6 %prep.1 = (bf16[1024,1024]{1,0:T(8,128)(2,1)}, bf16[1024,1024]{1,0:T(8,128)(2,1)}, bf16[1024,1024]{1,0:T(8,128)(2,1)}) custom-call(bf16[1024,1024]{1,0:T(8,128)(2,1)} %tok.1, bf16[1024,1024]{1,0:T(8,128)(2,1)} %cot.1, bf16[1024,1024]{1,0:T(8,128)(2,1)} %fusion.perm, f32[1,1024]{1,0:T(1,128)} %reshape.464.gain), custom_call_target="tpu_custom_call" | custom-call | flops 4294967296 | bytes 12582912 | tf_op jit(solution)/shard_map/prep/pallas_call | solution.py:159
  175.3 7.7 collective-permute-done.22
  188.4 12.8 %collective-permute-done.40 = bf16[1,2,4,32,1536]{4,3,2,1,0:T(8,128)(2,1)S(1)} collective-permute-done((bf16[1,2,4,32,1536]{4,3,2,1,0:T(8,128)(2,1)S(1)}, bf16[1,2,4,32,1536]{4,3,2,1,0:T(8,128)(2,1)S(1)}, u32[]{:S(2)}, u32[]{:S(2)}) %collective-permute-start.40) | collective-permute-done | bytes 786464 | tf_op jit(solution)/shard_map/ppermute | solution.py:49
  206.0 11.8 %collective-permute-done.52 = bf16[1,2,4,32,1536]{4,3,2,1,0:T(8,128)(2,1)S(1)} collective-permute-done((bf16[1,2,4,32,1536]{4,3,2,1,0:T(8,128)(2,1)S(1)}, bf16[1,2,4,32,1536]{4,3,2,1,0:T(8,128)(2,1)S(1)}, u32[]{:S(2)}, u32[]{:S(2)}) %collective-permute-start.52) | collective-permute-done | bytes 786464 | tf_op jit(solution)/shard_map/ppermute | solution.py:49
  233.5 9.9 %collective-permute-done.34 = bf16[2,1,4,32,2048]{4,3,2,1,0:T(8,128)(2,1)S(1)} collective-permute-done((bf16[2,1,4,32,2048]{4,3,2,1,0:T(8,128)(2,1)S(1)}, bf16[2,1,4,32,2048]{4,3,2,1,0:T(8,128)(2,1)S(1)}, u32[]{:S(2)}, u32[]{:S(2)}) %collective-permute-start.34) | collective-permute-done | bytes 1048608 | tf_op jit(solution)/shard_map/ppermute | solution.py:49
  255.2 6.7 project.4
  268.1 6.9 project.5
  280.5 16.2 %attend.1 = (bf16[1024,2048]{1,0:T(8,128)(2,1)}, f32[8,2,1024]{2,1,0:T(2,128)}) custom-call(bf16[1024,2048]{1,0:T(8,128)(2,1)} %constant_dynamic-update-slice_fusion.q, bf16[1024,1024]{1,0:T(8,128)(2,1)} %get-tuple-element.41.k, bf16[1024,1024]{1,0:T(8,128)(2,1)} %project_plain.1.v, s32[1,1024]{1,0:T(1,128)} %bitcast.161), custom_call_target="tpu_custom_call" | custom-call | flops 17179869184 | bytes 12582912 | tf_op jit(solution)/shard_map/attend/pallas_call | solution.py:264
  297.2 9.9 %after_attention.1 = (f32[1024,1024]{1,0:T(8,128)}, bf16[1024,1024]{1,0:T(8,128)(2,1)}) custom-call(bf16[1024,2048]{1,0:T(8,128)(2,1)} %get-tuple-element.42.o.g, bf16[512,2048]{1,0:T(8,128)(2,1)} %bitcast.126, bf16[512,2048]{1,0:T(8,128)(2,1)} %collective-permute-done.35.wb, bf16[1024,1024]{1,0:T(8,128)(2,1)} %get-tuple-element.43.trel, ...), custom_call_target="tpu_custom_call" | custom-call | flops 4294967296 | bytes 16777216 | tf_op jit(solution)/shard_map/after_attention/pallas_call | solution.py:286
  308.3 17.0 %mlp.3 = (bf16[1024,1536]{1,0:T(8,128)(2,1)}, bf16[1024,1536]{1,0:T(8,128)(2,1)}, bf16[1024,1536]{1,0:T(8,128)(2,1)}) custom-call(bf16[1024,1024]{1,0:T(8,128)(2,1)} %get-tuple-element.45.n2.x, bf16[1024,1024]{1,0:T(8,128)(2,1)} %get-tuple-element.46.c.crel.x, bf16[512,1536]{1,0:T(8,128)(2,1)} %bitcast.30.ga.refs_4_, ...), custom_call_target="tpu_custom_call" | custom-call | flops 9663676416 | bytes 23068672 | tf_op jit(solution)/shard_map/mlp/pallas_call | solution.py:315
  337.7 16.8 %mlp.2 = (bf16[1024,1536]{1,0:T(8,128)(2,1)}, bf16[1024,1536]{1,0:T(8,128)(2,1)}, bf16[1024,1536]{1,0:T(8,128)(2,1)}) custom-call(bf16[1024,1024]{1,0:T(8,128)(2,1)} %get-tuple-element.45.n2.x, bf16[1024,1024]{1,0:T(8,128)(2,1)} %get-tuple-element.46.c.crel.x, bf16[512,1536]{1,0:T(8,128)(2,1)} %bitcast.23.ga.refs_1_, ...), custom_call_target="tpu_custom_call" | custom-call | flops 9663676416 | bytes 23068672 | tf_op jit(solution)/shard_map/mlp/pallas_call | solution.py:315
  399.7 22.5 %mlp_back.1 = (f32[1024,1024]{1,0:T(8,128)}, bf16[1024,1024]{1,0:T(8,128)(2,1)}) custom-call(f32[1024,1024]{1,0:T(8,128)} %get-tuple-element.44.x1, bf16[1024,1024]{1,0:T(8,128)(2,1)} %get-tuple-element.46.c.crel.x, f32[1,1024]{1,0:T(1,128)} %reshape.480.gain, bf16[1024,1536]{1,0:T(8,128)(2,1)} %get-tuple-element.49.refs_0_.g, ...), custom_call_target="tpu_custom_call" | custom-call | flops 12884901888 | bytes 37748736 | tf_op jit(solution)/shard_map/mlp_back/pallas_call | solution.py:379
  428.6 51.1 %attend_back.1 = (bf16[1024,2048]{1,0:T(8,128)(2,1)}, bf16[1024,1024]{1,0:T(8,128)(2,1)}, bf16[1024,1024]{1,0:T(8,128)(2,1)}, f32[8,128]{1,0:T(8,128)}) custom-call(bf16[1024,1024]{1,0:T(8,128)(2,1)} %get-tuple-element.54.datt.x, bf16[512,2048]{1,0:T(8,128)(2,1)} %bitcast.127, bf16[512,2048]{1,0:T(8,128)(2,1)} %collective-permute-done.35.wb, ...), custom_call_target="tpu_custom_call" | custom-call | flops 25769803776 | bytes 31457280 | tf_op jit(solution)/shard_map/attend_back/pallas_call | solution.py:457
  494.1 15.0 %result.1 = bf16[1024,1024]{1,0:T(8,128)(2,1)} custom-call(f32[1024,1024]{1,0:T(8,128)} %get-tuple-element.44.x1, bf16[1024,1024]{1,0:T(8,128)(2,1)} %fusion.perm, bf16[1024,1536]{1,0:T(8,128)(2,1)} %get-tuple-element.47.refs_0_.g, bf16[512,1536]{1,0:T(8,128)(2,1)} %bitcast.132, bf16[512,1536]{1,0:T(8,128)(2,1)} %copy-done.42, ...), custom_call_target="tpu_custom_call" | custom-call | flops 8589934592 | bytes 20971520 | tf_op jit(solution)/shard_map/result/pallas_call | solution.py:344
  509.1 19.1 %input_back.1 = bf16[1024,1024]{1,0:T(8,128)(2,1)} custom-call(bf16[1024,1024]{1,0:T(8,128)(2,1)} %get-tuple-element.43.trel, f32[1024,1024]{1,0:T(8,128)} %get-tuple-element.53.dx1, f32[1,1024]{1,0:T(1,128)} %reshape.464.gain, bf16[1024,1024]{1,0:T(8,128)(2,1)} %fusion.perm, bf16[1024,2048]{1,0:T(8,128)(2,1)} %get-tuple-element.59.refs_0_.refs_3_.g, ...), custom_call_target="tpu_custom_call" | custom-call | flops 10737418240 | bytes 27262976 | tf_op jit(solution)/shard_map/input_back/pallas_call | solution.py:521
  578.6 10.5 %collective-permute-done.73 = bf16[2,1,4,32,1024]{4,3,2,1,0:T(8,128)(2,1)S(1)} collective-permute-done((bf16[2,1,4,32,1024]{4,3,2,1,0:T(8,128)(2,1)S(1)}, bf16[2,1,4,32,1024]{4,3,2,1,0:T(8,128)(2,1)S(1)}, u32[]{:S(2)}, u32[]{:S(2)}) %collective-permute-start.73) | collective-permute-done | bytes 524320 | tf_op jit(solution)/shard_map/ppermute | solution.py:49
  590.9 8.7 %collective-permute-done.85 = bf16[2,1,4,32,1024]{4,3,2,1,0:T(8,128)(2,1)S(1)} collective-permute-done((bf16[2,1,4,32,1024]{4,3,2,1,0:T(8,128)(2,1)S(1)}, bf16[2,1,4,32,1024]{4,3,2,1,0:T(8,128)(2,1)S(1)}, u32[]{:S(2)}, u32[]{:S(2)}) %collective-permute-start.85) | collective-permute-done | bytes 524320 | tf_op jit(solution)/shard_map/ppermute | solution.py:49
  601.9 10.9 %collective-permute-done.91 = bf16[1,2,4,32,1024]{4,3,2,1,0:T(8,128)(2,1)S(1)} collective-permute-done((bf16[1,2,4,32,1024]{4,3,2,1,0:T(8,128)(2,1)S(1)}, bf16[1,2,4,32,1024]{4,3,2,1,0:T(8,128)(2,1)S(1)}, u32[]{:S(2)}, u32[]{:S(2)}) %collective-permute-start.91) | collective-permute-done | bytes 524320 | tf_op jit(solution)/shard_map/ppermute | solution.py:49
  638.6 6.7 collective-permute-done.93
  658.2 7.3 collective-permute-done.88
  665.5 6.7 collective-permute-done.94
  714.0 12.3 %collective-permute-done.115 = bf16[2,1,4,32,1536]{4,3,2,1,0:T(8,128)(2,1)S(1)} collective-permute-done((bf16[2,1,4,32,1536]{4,3,2,1,0:T(8,128)(2,1)S(1)}, bf16[2,1,4,32,1536]{4,3,2,1,0:T(8,128)(2,1)S(1)}, u32[]{:S(2)}, u32[]{:S(2)}) %collective-permute-start.115) | collective-permute-done | bytes 786464 | tf_op jit(solution)/shard_map/ppermute | solution.py:49
  728.0 12.6 %collective-permute-done.133 = bf16[2,1,4,32,1536]{4,3,2,1,0:T(8,128)(2,1)S(1)} collective-permute-done((bf16[2,1,4,32,1536]{4,3,2,1,0:T(8,128)(2,1)S(1)}, bf16[2,1,4,32,1536]{4,3,2,1,0:T(8,128)(2,1)S(1)}, u32[]{:S(2)}, u32[]{:S(2)}) %collective-permute-start.133) | collective-permute-done | bytes 786464 | tf_op jit(solution)/shard_map/ppermute | solution.py:49
  741.5 7.6 collective-permute-done.127
  749.7 9.2 %collective-permute-done.116 = bf16[2,1,1,32,1536]{4,3,2,1,0:T(8,128)(2,1)S(1)} collective-permute-done((bf16[2,1,1,32,1536]{4,3,2,1,0:T(8,128)(2,1)S(1)}, bf16[2,1,1,32,1536]{4,3,2,1,0:T(8,128)(2,1)S(1)}, u32[]{:S(2)}, u32[]{:S(2)}) %collective-permute-start.116) | collective-permute-done | bytes 196640 | tf_op jit(solution)/shard_map/ppermute | solution.py:49
  763.4 8.3 collective-permute-done.111
  784.4 9.5 %collective-permute-done.129 = bf16[1,1,1,32,1536]{4,3,2,1,0:T(8,128)(2,1)S(1)} collective-permute-done((bf16[1,1,1,32,1536]{4,3,2,1,0:T(8,128)(2,1)S(1)}, bf16[1,1,1,32,1536]{4,3,2,1,0:T(8,128)(2,1)S(1)}, u32[]{:S(2)}, u32[]{:S(2)}) %collective-permute-start.129) | collective-permute-done | bytes 98336 | tf_op jit(solution)/shard_map/ppermute | solution.py:49
  794.0 7.5 collective-permute-done.106
  801.5 7.4 collective-permute-done.124
  808.9 7.3 collective-permute-done.130
  828.3 7.6 collective-permute-done.98
  836.8 7.4 collective-permute-done.99
  (555 shorter events, 475.8 us)
Async XLA Ops:
  7.4 49.0 %collective-permute-start.6 = (bf16[1,1,1,32,1024]{4,3,2,1,0:T(8,128)(2,1)S(1)}, bf16[1,1,1,32,1024]{4,3,2,1,0:T(8,128)(2,1)S(1)}, u32[]{:S(2)}, u32[]{:S(2)}) collective-permute-start(bf16[1,1,1,32,1024]{4,3,2,1,0:T(8,128)(2,1)S(1)} %get-tuple-element.92), channel_id=1, source_target_pairs={{0,24},{1,25},{2,26},{3,27},{4,28},{5,29},{6,30},{7,31},{8,0},{9,1... | collective-permute-start | bytes 196616 | tf_op jit(solution)/shard_map/ppermute | solution.py:49
  7.9 52.8 %collective-permute-start.12 = (bf16[1,1,1,32,1024]{4,3,2,1,0:T(8,128)(2,1)S(1)}, bf16[1,1,1,32,1024]{4,3,2,1,0:T(8,128)(2,1)S(1)}, u32[]{:S(2)}, u32[]{:S(2)}) collective-permute-start(bf16[1,1,1,32,1024]{4,3,2,1,0:T(8,128)(2,1)S(1)} %get-tuple-element.91), channel_id=1, source_target_pairs={{0,24},{1,25},{2,26},{3,27},{4,28},{5,29},{6,30},{7,31},{8,0},{9,1... | collective-permute-start | bytes 196616 | tf_op jit(solution)/shard_map/ppermute | solution.py:49
  8.4 37.8 %collective-permute-start.18 = (bf16[1,1,1,32,1024]{4,3,2,1,0:T(8,128)(2,1)}, bf16[1,1,1,32,1024]{4,3,2,1,0:T(8,128)(2,1)S(1)}, u32[]{:S(2)}, u32[]{:S(2)}) collective-permute-start(bf16[1,1,1,32,1024]{4,3,2,1,0:T(8,128)(2,1)} %bitcast.140), channel_id=1, source_target_pairs={{0,2},{1,3},{2,0},{3,1},{4,6},{5,7},{6,4},{7,5},{8,10},{9,11},{10,... | collective-permute-start | bytes 196616 | tf_op jit(solution)/shard_map/ppermute | solution.py:49
  9.9 36.4 %collective-permute-start.24 = (bf16[1,1,1,32,1024]{4,3,2,1,0:T(8,128)(2,1)}, bf16[1,1,1,32,1024]{4,3,2,1,0:T(8,128)(2,1)S(1)}, u32[]{:S(2)}, u32[]{:S(2)}) collective-permute-start(bf16[1,1,1,32,1024]{4,3,2,1,0:T(8,128)(2,1)} %bitcast.144), channel_id=1, source_target_pairs={{0,4},{1,5},{2,6},{3,7},{4,0},{5,1},{6,2},{7,3},{8,12},{9,13},{10,... | collective-permute-start | bytes 196616 | tf_op jit(solution)/shard_map/ppermute | solution.py:49
  32.7 47.8 %collective-permute-start.30 = (bf16[1,1,1,32,2048]{4,3,2,1,0:T(8,128)(2,1)S(1)}, bf16[1,1,1,32,2048]{4,3,2,1,0:T(8,128)(2,1)S(1)}, u32[]{:S(2)}, u32[]{:S(2)}) collective-permute-start(bf16[1,1,1,32,2048]{4,3,2,1,0:T(8,128)(2,1)S(1)} %bitcast.136), channel_id=1, source_target_pairs={{0,24},{1,25},{2,26},{3,27},{4,28},{5,29},{6,30},{7,31},{8,0},{9,1... | collective-permute-start | bytes 393224 | tf_op jit(solution)/shard_map/ppermute | solution.py:49
  104.2 35.0 %collective-permute-start.39 = (bf16[1,1,4,32,1536]{4,3,2,1,0:T(8,128)(2,1)S(1)}, bf16[1,1,4,32,1536]{4,3,2,1,0:T(8,128)(2,1)S(1)}, u32[]{:S(2)}, u32[]{:S(2)}) collective-permute-start(bf16[1,1,4,32,1536]{4,3,2,1,0:T(8,128)(2,1)S(1)} %pad_maximum_fusion.26), channel_id=1, source_target_pairs={{0,4},{1,5},{2,6},{3,7},{4,0},{5,1},{6,2},{7,3},{8,12},{9,13},{10,... | collective-permute-start | bytes 1179656 | tf_op jit(solution)/shard_map/ppermute | solution.py:49
  123.6 45.5 %collective-permute-start.69 = (bf16[1,1,4,32,1536]{4,3,2,1,0:T(8,128)(2,1)S(1)}, bf16[1,1,4,32,1536]{4,3,2,1,0:T(8,128)(2,1)S(1)}, u32[]{:S(2)}, u32[]{:S(2)}) collective-permute-start(bf16[1,1,4,32,1536]{4,3,2,1,0:T(8,128)(2,1)S(1)} %pad_maximum_fusion.27), channel_id=1, source_target_pairs={{0,2},{1,3},{2,0},{3,1},{4,6},{5,7},{6,4},{7,5},{8,10},{9,11},{10,... | collective-permute-start | bytes 1179656 | tf_op jit(solution)/shard_map/ppermute | solution.py:49
  172.8 44.9 %collective-permute-start.52 = (bf16[1,2,4,32,1536]{4,3,2,1,0:T(8,128)(2,1)S(1)}, bf16[1,2,4,32,1536]{4,3,2,1,0:T(8,128)(2,1)S(1)}, u32[]{:S(2)}, u32[]{:S(2)}) collective-permute-start(bf16[1,2,4,32,1536]{4,3,2,1,0:T(8,128)(2,1)S(1)} %pad_maximum_fusion.15), channel_id=1, source_target_pairs={{0,2},{1,3},{2,0},{3,1},{4,6},{5,7},{6,4},{7,5},{8,10},{9,11},{10,... | collective-permute-start | bytes 2359304 | tf_op jit(solution)/shard_map/ppermute | solution.py:49
  184.9 41.3 %collective-permute-start.64 = (bf16[1,2,4,32,1536]{4,3,2,1,0:T(8,128)(2,1)S(1)}, bf16[1,2,4,32,1536]{4,3,2,1,0:T(8,128)(2,1)S(1)}, u32[]{:S(2)}, u32[]{:S(2)}) collective-permute-start(bf16[1,2,4,32,1536]{4,3,2,1,0:T(8,128)(2,1)S(1)} %pad_maximum_fusion.17), channel_id=1, source_target_pairs={{0,2},{1,3},{2,0},{3,1},{4,6},{5,7},{6,4},{7,5},{8,10},{9,11},{10,... | collective-permute-start | bytes 2359304 | tf_op jit(solution)/shard_map/ppermute | solution.py:49
  203.4 40.1 %collective-permute-start.34 = (bf16[2,1,4,32,2048]{4,3,2,1,0:T(8,128)(2,1)S(1)}, bf16[2,1,4,32,2048]{4,3,2,1,0:T(8,128)(2,1)S(1)}, u32[]{:S(2)}, u32[]{:S(2)}) collective-permute-start(bf16[2,1,4,32,2048]{4,3,2,1,0:T(8,128)(2,1)S(1)} %pad_maximum_fusion.12), channel_id=1, source_target_pairs={{0,4},{1,5},{2,6},{3,7},{4,0},{5,1},{6,2},{7,3},{8,12},{9,13},{10,... | collective-permute-start | bytes 3145736 | tf_op jit(solution)/shard_map/ppermute | solution.py:49
  218.0 37.2 %collective-permute-start.17 = (bf16[512,1024]{1,0:T(8,128)(2,1)}, bf16[512,1024]{1,0:T(8,128)(2,1)}, u32[]{:S(2)}, u32[]{:S(2)}) collective-permute-start(bf16[512,1024]{1,0:T(8,128)(2,1)} %bitcast.10.wa.refs_4_), channel_id=1, source_target_pairs={{0,1},{1,0},{2,3},{3,2},{4,5},{5,4},{6,7},{7,6},{8,9},{9,8},{10,11... | collective-permute-start | bytes 3145736 | tf_op jit(solution)/shard_map/ppermute | solution.py:49
  226.2 41.8 %collective-permute-start.23 = (bf16[512,1024]{1,0:T(8,128)(2,1)}, bf16[512,1024]{1,0:T(8,128)(2,1)}, u32[]{:S(2)}, u32[]{:S(2)}) collective-permute-start(bf16[512,1024]{1,0:T(8,128)(2,1)} %bitcast.13.wa.refs_7_), channel_id=1, source_target_pairs={{0,1},{1,0},{2,3},{3,2},{4,5},{5,4},{6,7},{7,6},{8,9},{9,8},{10,11... | collective-permute-start | bytes 3145736 | tf_op jit(solution)/shard_map/ppermute | solution.py:49
  243.4 93.1 %collective-permute-start.41 = (bf16[512,1536]{1,0:T(8,128)(2,1)}, bf16[512,1536]{1,0:T(8,128)(2,1)}, u32[]{:S(2)}, u32[]{:S(2)}) collective-permute-start(bf16[512,1536]{1,0:T(8,128)(2,1)} %bitcast.23.ga.refs_1_), channel_id=1, source_target_pairs={{0,1},{1,0},{2,3},{3,2},{4,5},{5,4},{6,7},{7,6},{8,9},{9,8},{10,11... | collective-permute-start | bytes 4718600 | tf_op jit(solution)/shard_map/ppermute | solution.py:49
  244.8 51.9 %collective-permute-start.59 = (bf16[512,1536]{1,0:T(8,128)(2,1)}, bf16[512,1536]{1,0:T(8,128)(2,1)}, u32[]{:S(2)}, u32[]{:S(2)}) collective-permute-start(bf16[512,1536]{1,0:T(8,128)(2,1)} %bitcast.30.ga.refs_4_), channel_id=1, source_target_pairs={{0,1},{1,0},{2,3},{3,2},{4,5},{5,4},{6,7},{7,6},{8,9},{9,8},{10,11... | collective-permute-start | bytes 4718600 | tf_op jit(solution)/shard_map/ppermute | solution.py:49
  255.1 52.0 %collective-permute-start.65 = (bf16[512,1536]{1,0:T(8,128)(2,1)}, bf16[512,1536]{1,0:T(8,128)(2,1)}, u32[]{:S(2)}, u32[]{:S(2)}) collective-permute-start(bf16[512,1536]{1,0:T(8,128)(2,1)} %bitcast.32.ua.refs_10_), channel_id=1, source_target_pairs={{0,1},{1,0},{2,3},{3,2},{4,5},{5,4},{6,7},{7,6},{8,9},{9,8},{10,11... | collective-permute-start | bytes 4718600 | tf_op jit(solution)/shard_map/ppermute | solution.py:49
  261.9 45.3 %collective-permute-start.71 = (bf16[512,1536]{1,0:T(8,128)(2,1)}, bf16[512,1536]{1,0:T(8,128)(2,1)S(1)}, u32[]{:S(2)}, u32[]{:S(2)}) collective-permute-start(bf16[512,1536]{1,0:T(8,128)(2,1)} %bitcast.34.da.refs_4_), channel_id=1, source_target_pairs={{0,1},{1,0},{2,3},{3,2},{4,5},{5,4},{6,7},{7,6},{8,9},{9,8},{10,11... | collective-permute-start | bytes 4718600 | tf_op jit(solution)/shard_map/ppermute | solution.py:49
  296.7 39.9 %collective-permute-start.47 = (bf16[512,1536]{1,0:T(8,128)(2,1)S(1)}, bf16[512,1536]{1,0:T(8,128)(2,1)}, u32[]{:S(2)}, u32[]{:S(2)}) collective-permute-start(bf16[512,1536]{1,0:T(8,128)(2,1)S(1)} %bitcast.135), channel_id=1, source_target_pairs={{0,1},{1,0},{2,3},{3,2},{4,5},{5,4},{6,7},{7,6},{8,9},{9,8},{10,11... | collective-permute-start | bytes 4718600 | tf_op jit(solution)/shard_map/ppermute | solution.py:49
  297.1 39.4 %collective-permute-start.53 = (bf16[512,1536]{1,0:T(8,128)(2,1)S(1)}, bf16[512,1536]{1,0:T(8,128)(2,1)S(1)}, u32[]{:S(2)}, u32[]{:S(2)}) collective-permute-start(bf16[512,1536]{1,0:T(8,128)(2,1)S(1)} %bitcast.130), channel_id=1, source_target_pairs={{0,1},{1,0},{2,3},{3,2},{4,5},{5,4},{6,7},{7,6},{8,9},{9,8},{10,11... | collective-permute-start | bytes 4718600 | tf_op jit(solution)/shard_map/ppermute | solution.py:49
  483.9 88.2 %collective-permute-start.72 = (bf16[512,1024]{1,0:T(8,128)(2,1)}, bf16[512,1024]{1,0:T(8,128)(2,1)S(1)}, u32[]{:S(2)}, u32[]{:S(2)}) collective-permute-start(bf16[512,1024]{1,0:T(8,128)(2,1)} %weight_grad.23), channel_id=1, source_target_pairs={{0,1},{1,0},{2,3},{3,2},{4,5},{5,4},{6,7},{7,6},{8,9},{9,8},{10,11... | collective-permute-start | bytes 3145736 | tf_op jit(solution)/shard_map/ppermute | solution.py:49
  488.5 84.2 %collective-permute-start.84 = (bf16[512,1024]{1,0:T(8,128)(2,1)}, bf16[512,1024]{1,0:T(8,128)(2,1)S(1)}, u32[]{:S(2)}, u32[]{:S(2)}) collective-permute-start(bf16[512,1024]{1,0:T(8,128)(2,1)} %weight_grad.27), channel_id=1, source_target_pairs={{0,1},{1,0},{2,3},{3,2},{4,5},{5,4},{6,7},{7,6},{8,9},{9,8},{10,11... | collective-permute-start | bytes 3145736 | tf_op jit(solution)/shard_map/ppermute | solution.py:49
  571.1 138.4 %collective-permute-start.96 = (bf16[512,2048]{1,0:T(8,128)(2,1)S(1)}, bf16[512,2048]{1,0:T(8,128)(2,1)S(1)}, u32[]{:S(2)}, u32[]{:S(2)}) collective-permute-start(bf16[512,2048]{1,0:T(8,128)(2,1)S(1)} %copy-done.13), channel_id=1, source_target_pairs={{0,1},{1,0},{2,3},{3,2},{4,5},{5,4},{6,7},{7,6},{8,9},{9,8},{10,11... | collective-permute-start | bytes 6291464 | tf_op jit(solution)/shard_map/ppermute | solution.py:49
  572.1 41.0 %collective-permute-start.108 = (bf16[512,1536]{1,0:T(8,128)(2,1)S(1)}, bf16[512,1536]{1,0:T(8,128)(2,1)S(1)}, u32[]{:S(2)}, u32[]{:S(2)}) collective-permute-start(bf16[512,1536]{1,0:T(8,128)(2,1)S(1)} %copy-done.21), channel_id=1, source_target_pairs={{0,1},{1,0},{2,3},{3,2},{4,5},{5,4},{6,7},{7,6},{8,9},{9,8},{10,11... | collective-permute-start | bytes 4718600 | tf_op jit(solution)/shard_map/ppermute | solution.py:49
  573.5 40.6 %collective-permute-start.102 = (bf16[512,1536]{1,0:T(8,128)(2,1)S(1)}, bf16[512,1536]{1,0:T(8,128)(2,1)S(1)}, u32[]{:S(2)}, u32[]{:S(2)}) collective-permute-start(bf16[512,1536]{1,0:T(8,128)(2,1)S(1)} %copy-done.22), channel_id=1, source_target_pairs={{0,1},{1,0},{2,3},{3,2},{4,5},{5,4},{6,7},{7,6},{8,9},{9,8},{10,11... | collective-permute-start | bytes 4718600 | tf_op jit(solution)/shard_map/ppermute | solution.py:49
  627.5 85.3 %collective-permute-start.109 = (bf16[1,2,4,32,1536]{4,3,2,1,0:T(8,128)(2,1)S(1)}, bf16[1,2,4,32,1536]{4,3,2,1,0:T(8,128)(2,1)S(1)}, u32[]{:S(2)}, u32[]{:S(2)}) collective-permute-start(bf16[1,2,4,32,1536]{4,3,2,1,0:T(8,128)(2,1)S(1)} %bitcast.152), channel_id=1, source_target_pairs={{0,2},{1,3},{2,0},{3,1},{4,6},{5,7},{6,4},{7,5},{8,10},{9,11},{10,... | collective-permute-start | bytes 2359304 | tf_op jit(solution)/shard_map/ppermute | solution.py:49
  629.3 84.4 %collective-permute-start.103 = (bf16[1,2,4,32,1536]{4,3,2,1,0:T(8,128)(2,1)S(1)}, bf16[1,2,4,32,1536]{4,3,2,1,0:T(8,128)(2,1)S(1)}, u32[]{:S(2)}, u32[]{:S(2)}) collective-permute-start(bf16[1,2,4,32,1536]{4,3,2,1,0:T(8,128)(2,1)S(1)} %bitcast.153), channel_id=1, source_target_pairs={{0,2},{1,3},{2,0},{3,1},{4,6},{5,7},{6,4},{7,5},{8,10},{9,11},{10,... | collective-permute-start | bytes 2359304 | tf_op jit(solution)/shard_map/ppermute | solution.py:49
  630.8 80.3 %collective-permute-start.121 = (bf16[2,1,4,32,1536]{4,3,2,1,0:T(8,128)(2,1)S(1)}, bf16[2,1,4,32,1536]{4,3,2,1,0:T(8,128)(2,1)S(1)}, u32[]{:S(2)}, u32[]{:S(2)}) collective-permute-start(bf16[2,1,4,32,1536]{4,3,2,1,0:T(8,128)(2,1)S(1)} %slice.516), channel_id=1, source_target_pairs={{0,4},{1,5},{2,6},{3,7},{4,0},{5,1},{6,2},{7,3},{8,12},{9,13},{10,... | collective-permute-start | bytes 2359304 | tf_op jit(solution)/shard_map/ppermute | solution.py:49
  711.1 37.9 %collective-permute-start.127 = (bf16[2,1,4,32,1536]{4,3,2,1,0:T(8,128)(2,1)S(1)}, bf16[2,1,4,32,1536]{4,3,2,1,0:T(8,128)(2,1)S(1)}, u32[]{:S(2)}, u32[]{:S(2)}) collective-permute-start(bf16[2,1,4,32,1536]{4,3,2,1,0:T(8,128)(2,1)S(1)} %slice.524), channel_id=1, source_target_pairs={{0,4},{1,5},{2,6},{3,7},{4,0},{5,1},{6,2},{7,3},{8,12},{9,13},{10,... | collective-permute-start | bytes 2359304 | tf_op jit(solution)/shard_map/ppermute | solution.py:49
  712.8 114.4 %collective-permute-start.97 = (bf16[1,2,4,32,2048]{4,3,2,1,0:T(8,128)(2,1)S(1)}, bf16[1,2,4,32,2048]{4,3,2,1,0:T(8,128)(2,1)S(1)}, u32[]{:S(2)}, u32[]{:S(2)}) collective-permute-start(bf16[1,2,4,32,2048]{4,3,2,1,0:T(8,128)(2,1)S(1)} %bitcast.151), channel_id=1, source_target_pairs={{0,2},{1,3},{2,0},{3,1},{4,6},{5,7},{6,4},{7,5},{8,10},{9,11},{10,... | collective-permute-start | bytes 3145736 | tf_op jit(solution)/shard_map/ppermute | solution.py:49
  713.7 35.8 %collective-permute-start.110 = (bf16[1,2,1,32,1536]{4,3,2,1,0:T(8,128)(2,1)S(1)}, bf16[1,2,1,32,1536]{4,3,2,1,0:T(8,128)(2,1)S(1)}, u32[]{:S(2)}, u32[]{:S(2)}) collective-permute-start(bf16[1,2,1,32,1536]{4,3,2,1,0:T(8,128)(2,1)S(1)} %slice.502), channel_id=1, source_target_pairs={{0,8},{1,9},{2,10},{3,11},{4,12},{5,13},{6,14},{7,15},{8,16},{9,17... | collective-permute-start | bytes 589832 | tf_op jit(solution)/shard_map/ppermute | solution.py:49
  726.3 36.9 %collective-permute-start.104 = (bf16[1,1,4,32,1536]{4,3,2,1,0:T(8,128)(2,1)S(1)}, bf16[1,1,4,32,1536]{4,3,2,1,0:T(8,128)(2,1)S(1)}, u32[]{:S(2)}, u32[]{:S(2)}) collective-permute-start(bf16[1,1,4,32,1536]{4,3,2,1,0:T(8,128)(2,1)S(1)} %slice.494), channel_id=1, source_target_pairs={{0,4},{1,5},{2,6},{3,7},{4,0},{5,1},{6,2},{7,3},{8,12},{9,13},{10,... | collective-permute-start | bytes 1179656 | tf_op jit(solution)/shard_map/ppermute | solution.py:49
  771.7 44.5 %collective-permute-start.112 = (bf16[1,2,1,32,1536]{4,3,2,1,0:T(8,128)(2,1)S(1)}, bf16[1,2,1,32,1536]{4,3,2,1,0:T(8,128)(2,1)S(1)}, u32[]{:S(2)}, u32[]{:S(2)}) collective-permute-start(bf16[1,2,1,32,1536]{4,3,2,1,0:T(8,128)(2,1)S(1)} %add_convert_fusion.32), channel_id=1, source_target_pairs={{0,8},{1,9},{2,10},{3,11},{4,12},{5,13},{6,14},{7,15},{8,16},{9,17... | collective-permute-start | bytes 589832 | tf_op jit(solution)/shard_map/ppermute | solution.py:49
  779.1 37.2 %collective-permute-start.118 = (bf16[2,1,1,32,1536]{4,3,2,1,0:T(8,128)(2,1)S(1)}, bf16[2,1,1,32,1536]{4,3,2,1,0:T(8,128)(2,1)S(1)}, u32[]{:S(2)}, u32[]{:S(2)}) collective-permute-start(bf16[2,1,1,32,1536]{4,3,2,1,0:T(8,128)(2,1)S(1)} %add_convert_fusion.29), channel_id=1, source_target_pairs={{0,8},{1,9},{2,10},{3,11},{4,12},{5,13},{6,14},{7,15},{8,16},{9,17... | collective-permute-start | bytes 589832 | tf_op jit(solution)/shard_map/ppermute | solution.py:49
  (157 other events, 2047.5 us)

commit v2 on v1

v2 whole, which is shorter than its diff:
```python
import functools
import math

import jax
import jax.numpy as jnp
from jax import lax
from jax.experimental import pallas as pl
from jax.experimental.pallas import tpu as pltpu
from jax.sharding import PartitionSpec as P

AX = "fsdp"
D = 1024
HALF = D // 2
QUERY_HEADS = 16
KEY_VALUE_HEADS = 8
HEAD_SIZE = 128
FF = 3072
PART = FF // 2
GROUP = QUERY_HEADS // KEY_VALUE_HEADS
QW = QUERY_HEADS * HEAD_SIZE
KW = KEY_VALUE_HEADS * HEAD_SIZE
LONGEST = 512
BLK = 256
COLS = 512
STEP = 256
MLP_COLS = 3 * PART
PAIR = GROUP * HEAD_SIZE
EPS = 1e-06
THETA = 1000000.0
ROOT = math.sqrt(HEAD_SIZE)
SCALE2 = math.log2(math.e) / ROOT
VMEM = 56 * 1024 * 1024
F32 = jnp.float32
B16 = jnp.bfloat16


def axes_of(n):
    out, stride = [(1, 2)], 2
    for radix in (2, 2, 4, 4, 4, 4):
        if stride * radix <= n:
            out.append((stride, radix))
            stride *= radix
    while stride < n:
        out.append((stride, 2))
        stride *= 2
    return out


def move(value, n, axis, k):
    s, r = axis
    pairs = [(i, i + ((i // s % r + k) % r - i // s % r) * s) for i in range(n)]
    return lax.ppermute(value, AX, pairs)


def gather_chain(value, n, ends_first=True):
    ax = axes_of(n)[1:]
    m = len(ax)
    rows, cols = value.shape
    h = rows // 2
    cur = value.reshape((1,) * m + (rows, cols))
    if ends_first:
        for a in range(2, m):
            s = yield [move(cur, n, ax[a], -k) for k in range(1, ax[a][1])]
            cur = jnp.concatenate([cur] + s, axis=a)
    parts = [cur[..., :h, :], cur[..., h:, :]]
    for pair in ((0, 1), (1, 0)):
        s = yield [move(u, n, ax[a], -1) for u, a in zip(parts, pair)]
        parts = [jnp.concatenate([u, w], axis=a) for u, w, a in zip(parts, s, pair)]
    cur = jnp.stack(parts)
    if not ends_first:
        for a in range(2, m):
            got = [cur]
            for _ in range(ax[a][1] - 1):
                got += yield [move(got[-1], n, ax[a], -1)]
            cur = jnp.concatenate(got, axis=a + 1)
    cur = cur.reshape(rows * n // 2, cols)
    s = yield [move(cur, n, (1, 2), 1)]
    return [cur] + s


def scatter_chain(blocks, n):
    ax = axes_of(n)[1:]
    cols = blocks[0].shape[1]
    h = D // n // 2
    keep, give = blocks
    (s,) = yield [move(give, n, (1, 2), 1)]
    acc = (keep.astype(F32) + s.astype(F32)).astype(B16)
    acc = acc.reshape((2,) + tuple(r for _, r in ax) + (h, cols))
    parts = [acc[0], acc[1]]

    def part(u, j, a):
        return lax.index_in_dim(u, j, a, keepdims=True)

    for pair in ((0, 1), (1, 0)):
        s = yield [move(part(u, 1, a), n, ax[a], 1) for u, a in zip(parts, pair)]
        parts = [
            (part(u, 0, a).astype(F32) + w.astype(F32)).astype(B16) for u, w, a in zip(parts, s, pair)
        ]
    acc = jnp.stack(parts)
    for a in range(len(ax) - 1, 1, -1):
        r = ax[a][1]
        s = yield [move(part(acc, k, a + 1), n, ax[a], k) for k in range(1, r)]
        terms = [part(acc, 0, a + 1)] + s
        acc = sum(u.astype(F32) for u in terms).astype(B16)
    return [u.reshape(2 * h, cols) for u in terms]


class Chain:
    def __init__(self, steps, stages=0):
        self.steps, self.sent, self.value, self.stages = steps, None, None, stages

    def start(self):
        if self.value is not None:
            return
        try:
            self.sent = self.steps.send(self.sent)
            self.stages -= 1
        except StopIteration as end:
            self.sent, self.value = None, end.value


def window(start, wait, *values):
    for c in start:
        c.start()
    live = [c for c in wait if c.sent is not None]
    if not live:
        return values
    sent, values = lax.optimization_barrier(([c.sent for c in live], values))
    for c, u in zip(live, sent):
        c.sent = u
    return values


def finish(*chains):
    while any(c.value is None for c in chains):
        left = [c for c in chains if c.value is None]
        window(left, left)


def absolute_rows(n):
    ax = axes_of(n)
    me = lax.axis_index(AX)
    share = D // n
    h = share // 2
    place = lax.broadcasted_iota(jnp.int32, (D,), 0)
    inner = place % h
    rem = place // h
    owner = jnp.zeros_like(place)
    for s, r in ax[:0:-1]:
        owner = owner + ((me // s + rem % r) % r) * s
        rem = rem // r
    owner = owner + (me + rem // 2) % 2
    return owner * share + (rem % 2) * h + inner


def sum_chain(value, n):
    step = 1
    while step < n:
        masks = (1, 2, 3) if 4 * step <= n else (1,)
        got = yield [lax.ppermute(value, AX, [(i, i ^ (m * step)) for i in range(n)]) for m in masks]
        value = value + got[0]
        if len(got) > 1:
            value = value + (got[1] + got[2])
        step *= len(masks) + 1
    return value


def call(kernel, grid, ins, outs, shapes, scratch=(), flops=0, moved=0, name=None):
    return pl.pallas_call(
        kernel,
        grid=grid,
        in_specs=ins,
        out_specs=outs,
        out_shape=shapes,
        scratch_shapes=list(scratch),
        compiler_params=pltpu.CompilerParams(vmem_limit_bytes=VMEM),
        cost_estimate=pl.CostEstimate(flops=flops, bytes_accessed=moved, transcendentals=0),
        name=name,
    )


def whole(shape):
    return pl.BlockSpec(shape, lambda *_: (0,) * len(shape))


def rows_of(cols, blk=BLK):
    return pl.BlockSpec((blk, cols), lambda i: (i, 0))


def sds(shape, dtype):
    return jax.ShapeDtypeStruct(shape, dtype)


def nn(a, b):
    return lax.dot_general(a, b, (((1,), (0,)), ((), ())), preferred_element_type=F32)


def nt(a, b):
    return lax.dot_general(a, b, (((1,), (1,)), ((), ())), preferred_element_type=F32)


def inv_rms(x):
    return lax.rsqrt(jnp.mean(x * x, axis=-1, keepdims=True) + EPS)


def chained(kernel, grid, ins, args, outs, shapes, before, scratch=(), flops=0, moved=0, name=None):
    if before is None or isinstance(before, dict):
        before = before or {}
    else:
        before = dict(enumerate(before))
    extra = list(before.values())
    n_in, n_extra = len(ins), len(extra)

    def body(*refs):
        kernel(*refs[:n_in], *refs[n_in + n_extra :])

    return pl.pallas_call(
        body,
        grid=grid,
        in_specs=list(ins) + [pl.BlockSpec(memory_space=pl.ANY)] * n_extra,
        out_specs=outs,
        out_shape=shapes,
        scratch_shapes=list(scratch),
        input_output_aliases={n_in + i: place for i, place in enumerate(before)},
        compiler_params=pltpu.CompilerParams(vmem_limit_bytes=VMEM),
        cost_estimate=pl.CostEstimate(flops=flops, bytes_accessed=moved, transcendentals=0),
        name=name,
    )(*args, *extra)


def halves_of(cols, where):
    return [pl.BlockSpec((HALF, cols), lambda j: (0, where(j)))] * 2


def joined(refs):
    return jnp.concatenate([r[...] for r in refs], axis=0)


def chunks(t):
    return [slice(i * BLK, (i + 1) * BLK) for i in range(t // BLK)]


def prep_kernel(tok, cot, perm, trel, crel, crel_t):
    trel[...] = nn(tok[...], perm[...]).astype(B16)
    c = nn(cot[...], perm[...]).astype(B16)
    crel[...] = c
    crel_t[...] = c.T


def prep(tokens, cotangent, perm):
    t = tokens.shape[0]
    return call(
        prep_kernel,
        (t // BLK,),
        [rows_of(D), rows_of(D), whole((D, D))],
        [rows_of(D), rows_of(D), pl.BlockSpec((D, BLK), lambda i: (0, i))],
        [sds((t, D), B16), sds((t, D), B16), sds((D, t), B16)],
        flops=4 * t * D * D,
        moved=12 * t * D,
        name="prep",
    )(tokens, cotangent, perm)


def head_rows(n1, w, cos, sin, gain, out, raw):
    for at in chunks(n1.shape[0]):
        x = nn(n1[at, :], w)
        raw[at, :] = x.astype(B16)
        for h in range(COLS // HEAD_SIZE):
            lanes = slice(h * HEAD_SIZE, (h + 1) * HEAD_SIZE)
            y = x[:, lanes]
            y = y * inv_rms(y) * gain[...]
            y = y * cos[at, :] + pltpu.roll(y, HEAD_SIZE // 2, 1) * sin[at, :]
            out[at, lanes] = y.astype(B16)


def queries_kernel(trel, gain, w0, w1, cos, sin, qg, q, rawq, n1, n1_t):
    @pl.when(pl.program_id(0) == 0)
    def _():
        for at in chunks(trel.shape[0]):
            x = trel[at, :].astype(F32)
            x = (x * inv_rms(x) * gain[...]).astype(B16)
            n1[at, :] = x
            n1_t[:, at] = x.T

    head_rows(n1, joined((w0, w1)), cos, sin, qg, q, rawq)


def project_queries(trel, gain, w, cos, sin, qg):
    t = trel.shape[0]
    table, one = whole((t, HEAD_SIZE)), whole((1, HEAD_SIZE))
    out = pl.BlockSpec((t, COLS), lambda j: (0, j))
    return call(
        queries_kernel,
        (QW // COLS,),
        [whole((t, D)), whole((1, D))] + halves_of(COLS, lambda j: j) + [table, table, one],
        [out, out, whole((t, D)), whole((D, t))],
        [sds((t, QW), B16)] * 2 + [sds((t, D), B16), sds((D, t), B16)],
        flops=2 * t * D * QW,
        moved=2 * (D * QW + t * (2 * QW + 3 * D)),
        name="project_queries",
    )(trel, gain, *w, cos, sin, qg)


def keys_kernel(n1, w0, w1, cos, sin, kg, k, rawk, v):
    w = joined((w0, w1))

    @pl.when(pl.program_id(0) < KW // COLS)
    def _():
        head_rows(n1, w, cos, sin, kg, k, rawk)

    @pl.when(pl.program_id(0) >= KW // COLS)
    def _():
        for at in chunks(n1.shape[0]):
            v[at, :] = nn(n1[at, :], w).astype(B16)


def project_keys(n1, w, cos, sin, kg):
    t = n1.shape[0]
    nk = KW // COLS
    table, one = whole((t, HEAD_SIZE)), whole((1, HEAD_SIZE))
    early = pl.BlockSpec((t, COLS), lambda j: (0, jnp.minimum(j, nk - 1)))
    late = pl.BlockSpec((t, COLS), lambda j: (0, jnp.maximum(j - nk, 0)))
    return call(
        keys_kernel,
        (2 * nk,),
        [whole((t, D))] + halves_of(COLS, lambda j: QW // COLS + j) + [table, table, one],
        [early, early, late],
        [sds((t, KW), B16)] * 3,
        flops=4 * t * D * KW,
        moved=2 * (2 * D * KW + t * (3 * KW + D)),
        name="project_keys",
    )(n1, *w, cos, sin, kg)


def build_bias(first, bias):
    t = bias.shape[0]
    for i, at in enumerate(chunks(t)):
        key = lax.broadcasted_iota(jnp.int32, (t, BLK), 0)
        query = lax.broadcasted_iota(jnp.int32, (t, BLK), 1) + i * BLK
        allowed = (key >= first[:, at]) & (key <= query)
        bias[:, at] = jnp.where(allowed, 0.0, -1e30)


def window_of(i):
    return slice(max(0, i - LONGEST // BLK) * BLK, (i + 1) * BLK)


def stacked(ref, at):
    return jnp.concatenate([ref[at, :HEAD_SIZE], ref[at, HEAD_SIZE:]], axis=0)


def attend_kernel(q, k, v, first, out, lse, bias):
    @pl.when(pl.program_id(0) == 0)
    def _():
        build_bias(first, bias)

    vt = v[...].T
    for i, at in enumerate(chunks(q.shape[0])):
        keys = window_of(i)
        s = nt(k[keys, :], stacked(q, at))
        b = bias[keys, at]
        e = jnp.exp2(s * SCALE2 + jnp.concatenate([b, b], axis=1))
        total = jnp.sum(e, axis=0, keepdims=True)
        o = (nn(vt[:, keys], e.astype(B16)) * (1.0 / total)).T.astype(B16)
        level = jnp.log2(total)
        for r in range(GROUP):
            mine = slice(r * BLK, (r + 1) * BLK)
            out[at, r * HEAD_SIZE : (r + 1) * HEAD_SIZE] = o[mine, :]
            lse[0, r : r + 1, at] = level[:, mine]


def attend(q, k, v, first):
    t = k.shape[0]
    groups = k.shape[1] // HEAD_SIZE
    head = pl.BlockSpec((t, HEAD_SIZE), lambda g: (0, g))
    both = pl.BlockSpec((t, PAIR), lambda g: (0, g))
    return call(
        attend_kernel,
        (groups,),
        [both, head, head, whole((1, t))],
        [both, pl.BlockSpec((1, GROUP, t), lambda g: (g, 0, 0))],
        [sds((t, groups * PAIR), B16), sds((groups, GROUP, t), F32)],
        [pltpu.VMEM((t, t), F32)],
        flops=8 * groups * t * t * PAIR,
        moved=12 * t * groups * HEAD_SIZE,
        name="attend",
    )(q, k, v, first)


def after_kernel(o, w0, w1, trel, gain, x1, n2, n2_t):
    j = pl.program_id(0)

    @pl.when(j == 0)
    def _():
        x1[...] = trel[...].astype(F32)

    w = joined((w0, w1))
    for at in chunks(o.shape[0]):
        x1[at, :] += nt(o[at, :], w)

    @pl.when(j == pl.num_programs(0) - 1)
    def _():
        for at in chunks(o.shape[0]):
            x = x1[at, :]
            y = (x * inv_rms(x) * gain[...]).astype(B16)
            n2[at, :] = y
            n2_t[:, at] = y.T


def after_attention(o, w, trel, gain):
    t = o.shape[0]
    return call(
        after_kernel,
        (QW // COLS,),
        [pl.BlockSpec((t, COLS), lambda j: (0, j))]
        + halves_of(COLS, lambda j: MLP_COLS // COLS + j)
        + [whole((t, D)), whole((1, D))],
        [whole((t, D)), whole((t, D)), whole((D, t))],
        [sds((t, D), F32), sds((t, D), B16), sds((D, t), B16)],
        flops=2 * t * D * QW,
        moved=2 * (t * QW + D * QW + 5 * t * D),
        name="after_attention",
    )(o, *w, trel, gain)


def mlp_kernel(n2, n2_t, c, c_t, w0, w1, hidden, dact, g0, g1):
    w = joined((w0, w1))
    for at in chunks(n2.shape[0]):
        x = nn(n2[at, :], w[:, STEP:])
        gate, up = x[:, :STEP], x[:, STEP:]
        dh = nn(c[at, :], w[:, :STEP])
        sig = jax.nn.sigmoid(gate)
        silu = gate * sig
        hidden[at, :] = (silu * up).astype(B16)
        dact[at, :STEP] = (dh * up * sig * (1.0 + gate * (1.0 - sig))).astype(B16)
        dact[at, STEP:] = (dh * silu).astype(B16)
    for p, out in enumerate((g0, g1)):
        mine = slice(p * HALF, (p + 1) * HALF)
        out[:, :STEP] = nn(c_t[mine, :], hidden[...]).astype(B16)
        out[:, STEP:] = nn(n2_t[mine, :], dact[...]).astype(B16)


def mlp(n2, n2_t, c, c_t, w, base, steps, cols, before):
    t = n2.shape[0]

    def at(width):
        return pl.BlockSpec((t, width), lambda j: (0, base + j))

    return chained(
        mlp_kernel,
        (steps,),
        [whole((t, D)), whole((D, t))] * 2 + halves_of(3 * STEP, lambda j: base + j),
        [n2, n2_t, c, c_t, *w],
        [at(STEP), at(2 * STEP)] + halves_of(3 * STEP, lambda j: base + j),
        [sds((t, PART), B16), sds((t, 2 * PART), B16)] + [sds((HALF, cols), B16)] * 2,
        before,
        flops=12 * t * D * STEP * steps,
        moved=8 * t * D + steps * STEP * (12 * D + 6 * t),
        name="mlp",
    )


def mlp_back0_kernel(x1, hidden, dact, w0, w1, dn2, res):
    @pl.when(pl.program_id(0) == 0)
    def _():
        dn2[...] = jnp.zeros_like(dn2)
        res[...] = x1[...]

    w = joined((w0, w1))
    for at in chunks(x1.shape[0]):
        dn2[at, :] += nt(dact[at, :], w[:, STEP:])
        res[at, :] += nt(hidden[at, :], w[:, :STEP])


def mlp_back0(x1, hidden, dact, w):
    t = x1.shape[0]

    def at(width):
        return pl.BlockSpec((t, width), lambda j: (0, j))

    return call(
        mlp_back0_kernel,
        (PART // STEP,),
        [whole((t, D)), at(STEP), at(2 * STEP)] + halves_of(3 * STEP, lambda j: j),
        [whole((t, D)), whole((t, D))],
        [sds((t, D), F32)] * 2,
        flops=6 * t * D * PART,
        moved=12 * t * D + 6 * PART * (t + D),
        name="mlp_back0",
    )(x1, hidden, dact, *w)


def mlp_back1_kernel(x1, crel, gain, dn2, dact, w0, w1, dx1, datt, datt_t):
    j = pl.program_id(0)
    w = joined((w0, w1))[:, STEP:]

    @pl.when(j == 0)
    def _():
        dx1[...] = dn2[...]

    for at in chunks(x1.shape[0]):
        dx1[at, :] += nt(dact[at, :], w)

    @pl.when(j == pl.num_programs(0) - 1)
    def _():
        for at in chunks(x1.shape[0]):
            x = x1[at, :]
            s = inv_rms(x)
            r = x * s
            grad = dx1[at, :] * gain[...]
            inner = jnp.mean(grad * r, axis=-1, keepdims=True)
            d = crel[at, :].astype(F32) + s * (grad - r * inner)
            dx1[at, :] = d
            low = d.astype(B16)
            datt[at, :] = low
            datt_t[:, at] = low.T


def mlp_back1(x1, crel, gain, dn2, dact, w):
    t = x1.shape[0]
    return call(
        mlp_back1_kernel,
        (PART // STEP,),
        [whole((t, D)), whole((t, D)), whole((1, D)), whole((t, D)),
         pl.BlockSpec((t, 2 * STEP), lambda j: (0, j))] + halves_of(3 * STEP, lambda j: j),
        [whole((t, D)), whole((t, D)), whole((D, t))],
        [sds((t, D), F32), sds((t, D), B16), sds((D, t), B16)],
        flops=4 * t * D * PART,
        moved=18 * t * D + 4 * PART * (t + D),
        name="mlp_back1",
    )(x1, crel, gain, dn2, dact, *w)


def out_grad_kernel(datt_t, o, g0, g1):
    for p, out in enumerate((g0, g1)):
        out[...] = nn(datt_t[p * HALF : (p + 1) * HALF, :], o[...]).astype(B16)


def out_grad(datt_t, o):
    t = o.shape[0]
    return chained(
        out_grad_kernel,
        (QW // COLS,),
        [whole((D, t)), pl.BlockSpec((t, COLS), lambda j: (0, j))],
        [datt_t, o],
        halves_of(COLS, lambda j: j),
        [sds((HALF, 2 * QW), B16)] * 2,
        None,
        flops=2 * t * D * QW,
        moved=2 * (t * D + t * QW + D * QW),
        name="out_grad",
    )


def result_kernel(res, perm, hidden, w0, w1, out, acc):
    j = pl.program_id(0)

    @pl.when(j == 0)
    def _():
        acc[...] = res[...]

    w = joined((w0, w1))
    for at in chunks(res.shape[0]):
        acc[at, :] += nt(hidden[at, :], w)

    @pl.when(j == pl.num_programs(0) - 1)
    def _():
        for at in chunks(res.shape[0]):
            out[at, :] = nt(acc[at, :].astype(B16), perm[...]).astype(B16)


def make_result(res, perm, hidden, w):
    t = res.shape[0]
    return call(
        result_kernel,
        (PART // STEP,),
        [whole((t, D)), whole((D, D)), pl.BlockSpec((t, STEP), lambda j: (0, j))]
        + halves_of(STEP, lambda j: 3 * j),
        whole((t, D)),
        sds((t, D), B16),
        [pltpu.VMEM((t, D), F32)],
        flops=2 * t * D * (PART + D),
        moved=2 * (t * PART + D * PART + 3 * t * D + D * D),
        name="result",
    )(res, perm, hidden, *w)


def head_back(dy, raw, cos, sin, gain):
    dn = dy * cos - pltpu.roll(dy, HEAD_SIZE // 2, 1) * sin
    x = raw.astype(F32)
    s = inv_rms(x)
    r = x * s
    grad = dn * gain
    inner = jnp.mean(grad * r, axis=-1, keepdims=True)
    return (s * (grad - r * inner)).astype(B16), jnp.sum(dn * r, axis=0, keepdims=True)


def attend_back_kernel(
    datt, n1_t, w0, w1, q, k, v, rawq, rawk, lse, first, cos, sin, qgain, kgain,
    gains, g0, g1, dq, dk, dv, bias, do, dk_sum, dv_sum, low,
):
    @pl.when(pl.program_id(0) == 0)
    def _():
        build_bias(first, bias)
        gains[...] = jnp.zeros_like(gains)

    t = q.shape[0]
    w = joined((w0, w1))
    for at in chunks(t):
        do[at, :] = nn(datt[at, :], w).astype(B16)
    kt = k[...].T
    dk_sum[...] = jnp.zeros_like(dk_sum)
    dv_sum[...] = jnp.zeros_like(dv_sum)
    for i, at in enumerate(chunks(t)):
        keys = window_of(i)
        q2, do2 = stacked(q, at), stacked(do, at)
        b = bias[keys, at]
        level = jnp.concatenate([lse[0, r : r + 1, at] for r in range(GROUP)], axis=1)
        s = nt(k[keys, :], q2)
        p = jnp.exp2(s * SCALE2 + jnp.concatenate([b, b], axis=1) - level)
        dp = nt(v[keys, :], do2)
        delta = jnp.sum(dp * p, axis=0, keepdims=True)
        ds = (p * (dp - delta)).astype(B16)
        dv_sum[keys, :] += nn(p.astype(B16), do2)
        dk_sum[keys, :] += nn(ds, q2)
        dq2 = nn(kt[:, keys], ds).T * (1.0 / ROOT)
        for r in range(GROUP):
            lanes = slice(r * HEAD_SIZE, (r + 1) * HEAD_SIZE)
            grad, part = head_back(
                dq2[r * BLK : (r + 1) * BLK, :], rawq[at, lanes], cos[at, :], sin[at, :], qgain[...]
            )
            low[at, lanes] = grad
            gains[0:1, :] += part
    for at in chunks(t):
        grad, part = head_back(
            dk_sum[at, :] * (1.0 / ROOT), rawk[at, :], cos[at, :], sin[at, :], kgain[...]
        )
        low[at, PAIR : PAIR + HEAD_SIZE] = grad
        gains[1:2, :] += part
    low[:, PAIR + HEAD_SIZE :] = dv_sum[...].astype(B16)
    dq[...] = low[:, :PAIR]
    dk[...] = low[:, PAIR : PAIR + HEAD_SIZE]
    dv[...] = low[:, PAIR + HEAD_SIZE :]
    for p, out in enumerate((g0, g1)):
        out[...] = nn(n1_t[p * HALF : (p + 1) * HALF, :], low[...]).astype(B16)


def attend_back(datt, n1_t, w, q, k, v, rawq, rawk, lse, first, tables, base, count, before, grads):
    t = k.shape[0]
    groups = k.shape[1] // HEAD_SIZE
    per = groups // 2
    ahead = QW // (2 * PAIR) if base < per else 0
    head = pl.BlockSpec((t, HEAD_SIZE), lambda g: (0, base + g))
    both = pl.BlockSpec((t, PAIR), lambda g: (0, base + g))
    table, one = whole((t, HEAD_SIZE)), whole((1, HEAD_SIZE))
    shapes = [sds((8, HEAD_SIZE), F32)] + [sds((HALF, (ahead + per) * 2 * PAIR), B16)] * 2
    shapes += [sds((t, QW), B16), sds((t, KW), B16), sds((t, KW), B16)]
    earlier = {1 + i: u for i, u in enumerate(grads or ())}
    earlier.update({3 + i: u for i, u in enumerate(before or ())})
    return chained(
        attend_back_kernel,
        (count,),
        [whole((t, D)), whole((D, t))] + halves_of(PAIR, lambda g: MLP_COLS // PAIR + base + g)
        + [both, head, head, both, head, pl.BlockSpec((1, GROUP, t), lambda g: (base + g, 0, 0)),
           whole((1, t)), table, table, one, one],
        [datt, n1_t, *w, q, k, v, rawq, rawk, lse, first, *tables],
        [whole((8, HEAD_SIZE))] + halves_of(2 * PAIR, lambda g: ahead + (base + g) % per) + [both, head, head],
        shapes,
        earlier,
        [pltpu.VMEM((t, t), F32), pltpu.VMEM((t, PAIR), B16), pltpu.VMEM((t, HEAD_SIZE), F32),
         pltpu.VMEM((t, HEAD_SIZE), F32), pltpu.VMEM((t, 2 * PAIR), B16)],
        flops=count * (6 * t * D * PAIR + 10 * t * t * PAIR),
        moved=4 * t * D + count * (12 * t * HEAD_SIZE * 2 + 6 * D * PAIR),
        name="attend_back",
    )


def input_back_kernel(trel, dx1, gain, perm, dq, dk, dv, w0, w1, out):
    grad = jnp.concatenate(
        [
            nt(dq[...], w[:, :QW]) + nt(dk[...], w[:, QW : QW + KW]) + nt(dv[...], w[:, QW + KW :])
            for w in (w0, w1)
        ],
        axis=1,
    )
    x = trel[...].astype(F32)
    s = inv_rms(x)
    r = x * s
    grad = grad * gain[...]
    inner = jnp.mean(grad * r, axis=-1, keepdims=True)
    d = (dx1[...] + s * (grad - r * inner)).astype(B16)
    out[...] = nt(d, perm[...]).astype(B16)


def input_back(trel, dx1, gain, perm, dq, dk, dv, w):
    t = trel.shape[0]
    return call(
        input_back_kernel,
        (t // BLK,),
        [rows_of(D), rows_of(D), whole((1, D)), whole((D, D)), rows_of(QW), rows_of(KW), rows_of(KW)]
        + halves_of(QW + 2 * KW, lambda i: 0),
        rows_of(D),
        sds((t, D), B16),
        flops=2 * t * D * (QW + 2 * KW + D),
        moved=2 * (t * (QW + 2 * KW) + D * (QW + 2 * KW) + 4 * t * D + D * D),
        name="input_back",
    )(trel, dx1, gain, perm, dq, dk, dv, *w)


def added(refs, cols):
    return functools.reduce(lambda u, w: u + w, [r[:, cols].astype(F32) for r in refs])


def mlp_total_kernel(count, gain, wg, wu, *refs):
    sums, (down, gate, up, grad_gain) = (refs[:count], refs[count : 2 * count]), refs[2 * count :]
    total = jnp.zeros(grad_gain.shape, F32)
    for i, terms in enumerate(sums):
        for j in range(PART // STEP):
            x = added(terms, slice(3 * j * STEP, 3 * (j + 1) * STEP))
            at = slice(i * PART + j * STEP, i * PART + (j + 1) * STEP)
            down[:, at] = x[:, :STEP]
            gate[:, at] = x[:, STEP : 2 * STEP]
            up[:, at] = x[:, 2 * STEP :]
            both = wg[:, at].astype(F32) * x[:, STEP : 2 * STEP] + wu[:, at].astype(F32) * x[:, 2 * STEP :]
            total = total + jnp.sum(both, axis=1, keepdims=True)
    grad_gain[...] = total / gain[...].astype(F32)


def mlp_total(gain, wg, wu, first, second):
    share = wg.shape[0]
    ins = [gain.reshape(share, 1), wg, wu, *first, *second]
    shapes = [sds((share, FF), F32)] * 3 + [sds((share, 1), F32)]
    return call(
        functools.partial(mlp_total_kernel, len(first)),
        (1,),
        [whole(u.shape) for u in ins],
        [whole(u.shape) for u in shapes],
        shapes,
        moved=share * FF * 40,
        name="mlp_total",
    )(*ins)


def attn_total_kernel(count, gain, wq, wk, wv, *refs):
    early, late = refs[:count], refs[count : 2 * count]
    out, q, k, v, grad_gain = refs[2 * count :]
    out[...] = added(early, slice(0, QW))
    total = jnp.zeros(grad_gain.shape, F32)
    half = KEY_VALUE_HEADS // 2
    for g in range(KEY_VALUE_HEADS):
        terms, start = (early, QW + 2 * PAIR * g) if g < half else (late, 2 * PAIR * (g - half))
        x = added(terms, slice(start, start + 2 * PAIR))
        wide, head = slice(g * PAIR, (g + 1) * PAIR), slice(g * HEAD_SIZE, (g + 1) * HEAD_SIZE)
        q[:, wide] = x[:, :PAIR]
        k[:, head] = x[:, PAIR : PAIR + HEAD_SIZE]
        v[:, head] = x[:, PAIR + HEAD_SIZE :]
        w = jnp.concatenate([wq[:, wide], wk[:, head], wv[:, head]], axis=1)
        total = total + jnp.sum(w.astype(F32) * x, axis=1, keepdims=True)
    grad_gain[...] = total / gain[...].astype(F32)


def attn_total(gain, wq, wk, wv, early, late):
    share = wq.shape[0]
    ins = [gain.reshape(share, 1), wq, wk, wv, *early, *late]
    shapes = [sds((share, QW), F32)] * 2 + [sds((share, KW), F32)] * 2 + [sds((share, 1), F32)]
    return call(
        functools.partial(attn_total_kernel, len(early)),
        (1,),
        [whole(u.shape) for u in ins],
        [whole(u.shape) for u in shapes],
        shapes,
        moved=share * (QW + KW) * 40,
        name="attn_total",
    )(*ins)


def run_starts(segment_row):
    index = jnp.arange(segment_row.shape[0], dtype=jnp.int32)
    previous = jnp.concatenate([segment_row[:1] - 1, segment_row[:-1]])
    return index, lax.cummax(jnp.where(segment_row != previous, index, 0), axis=0)


def by_step(gate, up, down):
    rows = gate.shape[0]
    three = [w.reshape(rows, -1, 1, STEP) for w in (down, gate, up)]
    return jnp.concatenate(three, axis=2).reshape(rows, -1)


def per_device(
    n, tokens, segments, cotangent, w_query, w_key, w_value, w_out, w_gate, w_up, w_down,
    attn_gain, mlp_gain, q_gain, k_gain,
):
    share = D // n
    steps = PART // STEP
    count = len(axes_of(n))
    gain_cols = jnp.concatenate([attn_gain[:, None], mlp_gain[:, None]], axis=1)
    gain_cols = jnp.pad(gain_cols, ((0, 0), (0, HEAD_SIZE - 2)))
    down_t = w_down.T
    halves = [
        by_step(w_gate[:, cols], w_up[:, cols], down_t[:, cols])
        for cols in (slice(0, PART), slice(PART, FF))
    ]
    shards1 = jnp.concatenate([w_query, w_key, w_value, gain_cols], axis=1)
    shards2 = jnp.concatenate([halves[0], w_out.T], axis=1)
    chain1 = Chain(gather_chain(shards1, n), count)
    chain2 = Chain(gather_chain(shards2, n), count)
    chain3 = Chain(gather_chain(halves[1], n, ends_first=False), count)

    index, first = run_starts(segments[0])
    half = HEAD_SIZE // 2
    freq = THETA ** (-jnp.arange(half, dtype=F32) / half)
    turned = (index - first).astype(F32)[:, None] * freq[None, :]
    cos, sin = jnp.cos(turned), jnp.sin(turned)
    cos = jnp.concatenate([cos, cos], axis=1)
    sin = jnp.concatenate([-sin, sin], axis=1)
    first = first.reshape(1, -1)
    qg = q_gain.astype(F32).reshape(1, HEAD_SIZE)
    kg = k_gain.astype(F32).reshape(1, HEAD_SIZE)
    perm = (jnp.arange(D, dtype=jnp.int32)[:, None] == absolute_rows(n)[None, :]).astype(B16)

    window([chain1, chain3], [chain3])
    cos, sin, perm = window([chain3], [chain1, chain3], cos, sin, perm)
    while chain1.stages > 3:
        window([chain1], [chain1])
    tokens, cotangent = window([chain1, chain2], [chain1], tokens, cotangent)
    trel, crel, crel_t = prep(tokens, cotangent, perm)
    trel, crel, crel_t = window([chain1], [chain1, chain2], trel, crel, crel_t)
    while chain2.stages > 3:
        window([chain2], [chain2])
    window([chain1, chain2, chain3], [chain1])
    finish(chain1)
    w_in = chain1.value
    gains = jnp.concatenate([w[:, QW + 2 * KW :] for w in w_in], axis=0).astype(F32).T
    gain_a, gain_m = gains[0:1], gains[1:2]

    q, rawq, n1, n1_t = project_queries(trel, gain_a, w_in, cos, sin, qg)
    q, rawq, n1, n1_t = window([], [chain2], q, rawq, n1, n1_t)
    k, rawk, v = project_keys(n1, w_in, cos, sin, kg)
    k, rawk, v = window([chain2], [chain3], k, rawk, v)
    o, lse = attend(q, k, v, first)
    o, lse = window([chain3], [chain2], o, lse)
    window([chain2], [chain2, chain3])
    finish(chain2)
    x1, n2, n2_t = after_attention(o, chain2.value, trel, gain_m)

    def units(w, base, acts):
        return mlp(n2, n2_t, crel, crel_t, w, base, steps // 3, MLP_COLS, acts)

    acts = units(chain2.value, 0, None)
    acts = window([chain3], [chain3], *acts)
    while chain3.stages > 1:
        window([chain3], [chain3])
    acts = units(chain2.value, steps // 3, acts)
    acts = units(chain2.value, 2 * steps // 3, acts)
    acts = window([chain3], [chain3], *acts)
    finish(chain3)
    hidden0, dact0, *grads = acts
    sum1 = Chain(scatter_chain(grads, n))
    dn2, res = mlp_back0(x1, hidden0, dact0, chain2.value)
    dn2, res = window([sum1], [sum1], dn2, res)

    acts = units(chain3.value, 0, None)
    acts = units(chain3.value, steps // 3, acts)
    acts = window([sum1], [sum1], *acts)
    acts = units(chain3.value, 2 * steps // 3, acts)
    acts = window([sum1], [sum1], *acts)
    hidden1, dact1, *grads = acts
    sum2 = Chain(scatter_chain(grads, n))
    dx1, datt, datt_t = mlp_back1(x1, crel, gain_m, dn2, dact1, chain3.value)
    dx1, datt, datt_t = window([sum1, sum2], [sum2], dx1, datt, datt_t)

    tables = (cos, sin, qg, kg)
    per = KEY_VALUE_HEADS // 4

    def heads(i, before, grads):
        return attend_back(
            datt, n1_t, chain2.value, q, k, v, rawq, rawk, lse, first, tables,
            i * per, per, before, grads,
        )

    gain0, *rest = heads(0, None, out_grad(datt_t, o))
    gain0, *rest = window([sum2], [sum1, sum2], gain0, *rest)
    gain1, *rest = heads(1, rest[2:], rest[:2])
    gain1, *rest = window([sum2], [sum2], gain1, *rest)
    sum3 = Chain(scatter_chain(rest[:2], n))
    gain2, *rest = heads(2, rest[2:], None)
    gain2, *rest = window([sum2, sum3], [sum3], gain2, *rest)
    gain3, *rest = heads(3, rest[2:], rest[:2])
    gain3, res, *rest = window([sum3], [sum2, sum3], gain3, res, *rest)
    sum4 = Chain(scatter_chain(rest[:2], n))
    dq, dk, dv = rest[2:]
    total = Chain(sum_chain((gain0 + gain1) + (gain2 + gain3), n))
    result = make_result(res, perm, hidden1, chain3.value)
    result, dq, dk, dv = window([sum3, sum4, total], [sum3, sum4, total], result, dq, dk, dv)
    grad_tokens = input_back(trel, dx1, gain_a, perm, dq, dk, dv, w_in)
    (grad_tokens,) = window([sum4, sum3, total], [sum4, total], grad_tokens)
    window([sum4, total], [sum4, total])
    finish(sum1, sum2, sum3, sum4, total)

    grad_down, grad_gate, grad_up, grad_mlp_gain = mlp_total(
        mlp_gain, w_gate, w_up, sum1.value, sum2.value
    )
    grad_out, grad_query, grad_key, grad_value, grad_attn_gain = attn_total(
        attn_gain, w_query, w_key, w_value, sum3.value, sum4.value
    )
    return (
        result,
        grad_tokens,
        grad_query,
        grad_key,
        grad_value,
        grad_out.T,
        grad_gate,
        grad_up,
        grad_down.T,
        grad_attn_gain[:, 0],
        grad_mlp_gain[:, 0],
        total.value[0],
        total.value[1],
    )


def solution(mesh):
    n = mesh.shape[AX]
    rows, cols, one = P(AX, None), P(None, AX), P(AX)
    in_specs = (rows, rows, rows, rows, rows, rows, cols, rows, rows, cols, one, one, P(), P())
    out_specs = (rows, rows, rows, rows, rows, cols, rows, rows, cols, one, one, P(), P())
    return jax.shard_map(
        functools.partial(per_device, n), mesh=mesh, in_specs=in_specs, out_specs=out_specs, check_vma=False
    )
```

time: 868 us -> 561 us (0.65)
  waiting for transfers between devices: 340 us -> 110 us
  starting transfers between devices: 144 us -> 73.4 us
  Pallas kernels: 316 us -> 296 us
    ppermute x138 -> x56, waiting for transfers between devices: 340 us -> 106 us  [move(): return lax.ppermute(value, AX, pairs)]
    ppermute x138 -> x56, starting transfers between devices: 139 us -> 62.9 us  [move(): return lax.ppermute(value, AX, pairs)]
    pallas_call x33 -> x20, Pallas kernels: 281 us -> 260 us  [the longest x11 159 us: chained(): pl.pallas_call(body, grid=grid, in_specs=list(ins) + [pl.BlockSpec(memory...]
    another operation x3 -> x23, other arithmetic: 1.11 us -> 11.2 us  [the longest x9 6.85 us: gather_chain(): cur = jnp.stack(parts)]
    slice x35 -> x33, local copies, waits for them, and re-layouts: 1.26 us -> 10.3 us  [the longest x3 3.75 us: per_device(): gain_a, gain_m = (gains[0:1], gains[1:2])]
  transfers between devices with their start and end apart: 143 -> 63, of which waited for: 66 -> 19; matrix products, arithmetic and copies ran while one was open for 6% -> 7% of each run, Pallas kernels for 20% -> 53%
where the time goes in v2:
time: 561 us; the launch traced here: 552 us
  Pallas kernels  296 us (53%)
  waiting for transfers between devices  110 us (20%)
  starting transfers between devices  73.4 us (13%)
  other arithmetic  46.1 us (8%)
  local copies, waits for them, and re-layouts  23.3 us (4%)
    pallas_call x11, Pallas kernels, chained(): pl.pallas_call(body, grid=grid, in_specs=list(ins) + [pl.BlockSpec(memory...  159 us
    ppermute x56, waiting for transfers between devices, move(): return lax.ppermute(value, AX, pairs)  106 us
    ppermute x56, starting transfers between devices, move(): return lax.ppermute(value, AX, pairs)  62.9 us
    pallas_call x1, Pallas kernels, mlp_back1(): call(mlp_back1_kernel, (PART // STEP,), [whole((t, D)), whole((t, D)), wh...  20.2 us
    pallas_call x1, Pallas kernels, input_back(): call(input_back_kernel, (t // BLK,), [rows_of(D), rows_of(D), whole((1, D...  19.4 us
    pallas_call x1, Pallas kernels, mlp_back0(): call(mlp_back0_kernel, (PART // STEP,), [whole((t, D)), at(STEP), at(2 *...  18.2 us
    pallas_call x1, Pallas kernels, attend(): call(attend_kernel, (groups,), [both, head, head, whole((1, t))], [both,...  16.1 us
    pallas_call x1, Pallas kernels, make_result(): call(result_kernel, (PART // STEP,), [whole((t, D)), whole((D, D)), pl.Bl...  12.8 us
  transfers between devices with their start and end apart: 63, of which 19 were waited for; matrix products, arithmetic and copies ran while one was open for 7% of the time, Pallas kernels for 53%

profile of v2, /device:TPU:0, one launch (start us, length us, event | category | flops | bytes accessed | tf_op | source)
XLA Modules:
  0.0 551.7 jit_solution(15323900987113387692)
XLA Ops:
  2.4 5.1 collective-permute-start.2
  24.9 5.7 %collective-permute-done.3 = bf16[1,1,1,32,4224]{4,3,2,1,0:T(8,128)(2,1)} collective-permute-done((bf16[1,1,1,32,4224]{4,3,2,1,0:T(8,128)(2,1)S(1)}, bf16[1,1,1,32,4224]{4,3,2,1,0:T(8,128)(2,1)}, u32[]{:S(2)}, u32[]{:S(2)}) %collective-permute-start.3) | collective-permute-done | bytes 270368 | tf_op jit(solution)/shard_map/ppermute | solution.py:52
  36.4 9.0 %collective-permute-done.8 = bf16[1,1,4,16,4224]{4,3,2,1,0:T(8,128)(2,1)S(1)} collective-permute-done((bf16[1,1,4,16,4224]{4,3,2,1,0:T(8,128)(2,1)S(1)}, bf16[1,1,4,16,4224]{4,3,2,1,0:T(8,128)(2,1)S(1)}, u32[]{:S(2)}, u32[]{:S(2)}) %collective-permute-start.8) | collective-permute-done | bytes 540704 | tf_op jit(solution)/shard_map/ppermute | solution.py:52
  54.2 8.4 %prep.1 = (bf16[1024,1024]{1,0:T(8,128)(2,1)}, bf16[1024,1024]{1,0:T(8,128)(2,1)}, bf16[1024,1024]{1,0:T(8,128)(2,1)}) custom-call(bf16[1024,1024]{1,0:T(8,128)(2,1)} %tok, bf16[1024,1024]{1,0:T(8,128)(2,1)} %cot, bf16[1024,1024]{1,0:T(8,128)(2,1)} %fusion.perm), custom_call_target="tpu_custom_call" | custom-call | flops 4294967296 | bytes 12582912 | tf_op jit(solution)/shard_map/prep/pallas_call | solution.py:252
  62.6 24.6 %collective-permute-done.13 = bf16[1,1,1,32,6656]{4,3,2,1,0:T(8,128)(2,1)} collective-permute-done((bf16[1,1,1,32,6656]{4,3,2,1,0:T(8,128)(2,1)S(1)}, bf16[1,1,1,32,6656]{4,3,2,1,0:T(8,128)(2,1)}, u32[]{:S(2)}, u32[]{:S(2)}) %collective-permute-start.13) | collective-permute-done | bytes 426016 | tf_op jit(solution)/shard_map/ppermute | solution.py:52
  99.8 12.7 %project_queries.1 = (bf16[1024,2048]{1,0:T(8,128)(2,1)}, bf16[1024,2048]{1,0:T(8,128)(2,1)}, bf16[1024,1024]{1,0:T(8,128)(2,1)}, bf16[1024,1024]{1,0:T(8,128)(2,1)}) custom-call(bf16[1024,1024]{1,0:T(8,128)(2,1)} %get-tuple-element.237.trel, f32[1,1024]{1,0:T(1,128)} %copy.72.gain, bf16[512,4224]{1,0:T(8,128)(2,1)} %bitcast.131, ...), custom_call_target="tpu_custom_call" | custom-call | flops 4294967296 | bytes 18874368 | tf_op jit(solution)/shard_map/project_queries/pallas_call | solution.py:292
  117.2 10.4 %project_keys.1 = (bf16[1024,1024]{1,0:T(8,128)(2,1)}, bf16[1024,1024]{1,0:T(8,128)(2,1)}, bf16[1024,1024]{1,0:T(8,128)(2,1)}) custom-call(bf16[1024,1024]{1,0:T(8,128)(2,1)} %get-tuple-element.246.n1, bf16[512,4224]{1,0:T(8,128)(2,1)} %bitcast.132, bf16[512,4224]{1,0:T(8,128)(2,1)} %copy-done.29, f32[1024,128]{1,0:T(8,128)} %get-tuple-element.240.cos.refs_11_, ...), custom_call_target="tpu_custom_call" | custom-call | flops 4294967296 | bytes 12582912 | tf_op jit(solution)/shard_map/project_keys/pallas_call | solution.py:323
  127.6 16.1 %attend.1 = (bf16[1024,2048]{1,0:T(8,128)(2,1)}, f32[8,2,1024]{2,1,0:T(2,128)}) custom-call(bf16[1024,2048]{1,0:T(8,128)(2,1)} %get-tuple-element.253.q.refs_4_, bf16[1024,1024]{1,0:T(8,128)(2,1)} %get-tuple-element.254.k.refs_5_, bf16[1024,1024]{1,0:T(8,128)(2,1)} %get-tuple-element.255.v.refs_6_, s32[1,1024]{1,0:T(1,128)} %bitcast.157), custom_call_target="tpu_custom_call" | custom-call | flops 17179869184 | bytes 12582912 | tf_op jit(solution)/shard_map/attend/pallas_call | solution.py:377
  143.7 9.5 %collective-permute-done.18 = bf16[2,1,4,16,6656]{4,3,2,1,0:T(8,128)(2,1)} collective-permute-done((bf16[2,1,4,16,6656]{4,3,2,1,0:T(8,128)(2,1)S(1)}, bf16[2,1,4,16,6656]{4,3,2,1,0:T(8,128)(2,1)}, u32[]{:S(2)}, u32[]{:S(2)}) %collective-permute-start.18) | collective-permute-done | bytes 1703968 | tf_op jit(solution)/shard_map/ppermute | solution.py:52
  162.5 28.4 %collective-permute-done.21 = bf16[2,2,2,1,16,4608]{5,4,2,1,3,0:T(8,128)(2,1)S(1)} collective-permute-done((bf16[2,2,2,1,16,4608]{5,4,2,1,3,0:T(8,128)(2,1)}, bf16[2,2,2,1,16,4608]{5,4,2,1,3,0:T(8,128)(2,1)S(1)}, u32[]{:S(2)}, u32[]{:S(2)}) %collective-permute-start.21) | collective-permute-done | bytes 1179680 | tf_op jit(solution)/shard_map/ppermute | solution.py:52
  196.8 12.6 %after_attention.1 = (f32[1024,1024]{1,0:T(8,128)}, bf16[1024,1024]{1,0:T(8,128)(2,1)}, bf16[1024,1024]{1,0:T(8,128)(2,1)}) custom-call(bf16[1024,2048]{1,0:T(8,128)(2,1)} %get-tuple-element.261.o.refs_1_, bf16[512,6656]{1,0:T(8,128)(2,1)} %bitcast.102, bf16[512,6656]{1,0:T(8,128)(2,1)} %copy-done.1, bf16[1024,1024]{1,0:T(8,128)(2,1)} %get-tuple-element.237.trel, ...), custom_call_target="tpu_custom_call" | custom-call | flops 4294967296 | bytes 18874368 | tf_op jit(solution)/shard_map/after_attention/pallas_call | solution.py:412
  209.5 12.2 %mlp.6 = (bf16[1024,1536]{1,0:T(8,128)(2,1)}, bf16[1024,3072]{1,0:T(8,128)(2,1)}, bf16[512,4608]{1,0:T(8,128)(2,1)}, bf16[512,4608]{1,0:T(8,128)(2,1)}) custom-call(bf16[1024,1024]{1,0:T(8,128)(2,1)} %get-tuple-element.263.refs_0_, bf16[1024,1024]{1,0:T(8,128)(2,1)} %get-tuple-element.264.refs_1_, bf16[1024,1024]{1,0:T(8,128)(2,1)} %get-tuple-element.265.refs_2_.crel, ...), custom_call_target="tpu_custom_call" | custom-call | flops 6442450944 | bytes 17825792 | tf_op jit(solution)/shard_map/mlp/pallas_call | solution.py:217
  224.8 13.8 %mlp.7 = (bf16[1024,1536]{1,0:T(8,128)(2,1)}, bf16[1024,3072]{1,0:T(8,128)(2,1)}, bf16[512,4608]{1,0:T(8,128)(2,1)}, bf16[512,4608]{1,0:T(8,128)(2,1)}) custom-call(bf16[1024,1024]{1,0:T(8,128)(2,1)} %get-tuple-element.263.refs_0_, ...), custom_call_target="tpu_custom_call", output_to_operand_aliasing={{0}: (6, {}), {1}: (7, {}), {2}: (8, {}), {3}: (9, {})} | custom-call | flops 6442450944 | bytes 17825792 | tf_op jit(solution)/shard_map/mlp/pallas_call | solution.py:217
  238.6 12.4 %mlp.8 = (bf16[1024,1536]{1,0:T(8,128)(2,1)}, bf16[1024,3072]{1,0:T(8,128)(2,1)}, bf16[512,4608]{1,0:T(8,128)(2,1)}, bf16[512,4608]{1,0:T(8,128)(2,1)}) custom-call(bf16[1024,1024]{1,0:T(8,128)(2,1)} %get-tuple-element.263.refs_0_, ...), custom_call_target="tpu_custom_call", output_to_operand_aliasing={{0}: (6, {}), {1}: (7, {}), {2}: (8, {}), {3}: (9, {})} | custom-call | flops 6442450944 | bytes 17825792 | tf_op jit(solution)/shard_map/mlp/pallas_call | solution.py:217
  251.1 18.2 %mlp_back0.1 = (f32[1024,1024]{1,0:T(8,128)}, f32[1024,1024]{1,0:T(8,128)}) custom-call(f32[1024,1024]{1,0:T(8,128)} %get-tuple-element.286.x1, bf16[1024,1536]{1,0:T(8,128)(2,1)} %get-tuple-element.287.hidden, bf16[1024,3072]{1,0:T(8,128)(2,1)} %get-tuple-element.288.dact, bf16[512,6656]{1,0:T(8,128)(2,1)} %bitcast.106, bf16[512,6656]{1,0:T(8,128)(2,1)} %copy-done.1), custom_call_target="tpu_custom_call" | custom-call | flops 9663676416 | bytes 31457280 | tf_op jit(solution)/shard_map/mlp_back0/pallas_call | solution.py:481
  276.3 12.1 %mlp.9 = (bf16[1024,1536]{1,0:T(8,128)(2,1)}, bf16[1024,3072]{1,0:T(8,128)(2,1)}, bf16[512,4608]{1,0:T(8,128)(2,1)}, bf16[512,4608]{1,0:T(8,128)(2,1)}) custom-call(bf16[1024,1024]{1,0:T(8,128)(2,1)} %get-tuple-element.263.refs_0_, bf16[1024,1024]{1,0:T(8,128)(2,1)} %get-tuple-element.264.refs_1_, bf16[1024,1024]{1,0:T(8,128)(2,1)} %get-tuple-element.265.refs_2_.crel, ...), custom_call_target="tpu_custom_call" | custom-call | flops 6442450944 | bytes 17825792 | tf_op jit(solution)/shard_map/mlp/pallas_call | solution.py:217
  288.4 12.3 %mlp.10 = (bf16[1024,1536]{1,0:T(8,128)(2,1)}, bf16[1024,3072]{1,0:T(8,128)(2,1)}, bf16[512,4608]{1,0:T(8,128)(2,1)}, bf16[512,4608]{1,0:T(8,128)(2,1)}) custom-call(bf16[1024,1024]{1,0:T(8,128)(2,1)} %get-tuple-element.263.refs_0_, ...), custom_call_target="tpu_custom_call", output_to_operand_aliasing={{0}: (6, {}), {1}: (7, {}), {2}: (8, {}), {3}: (9, {})} | custom-call | flops 6442450944 | bytes 17825792 | tf_op jit(solution)/shard_map/mlp/pallas_call | solution.py:217
  305.8 12.1 %mlp.11 = (bf16[1024,1536]{1,0:T(8,128)(2,1)}, bf16[1024,3072]{1,0:T(8,128)(2,1)}, bf16[512,4608]{1,0:T(8,128)(2,1)}, bf16[512,4608]{1,0:T(8,128)(2,1)}) custom-call(bf16[1024,1024]{1,0:T(8,128)(2,1)} %get-tuple-element.263.refs_0_, ...), custom_call_target="tpu_custom_call", output_to_operand_aliasing={{0}: (6, {}), {1}: (7, {}), {2}: (8, {}), {3}: (9, {})} | custom-call | flops 6442450944 | bytes 17825792 | tf_op jit(solution)/shard_map/mlp/pallas_call | solution.py:217
  320.6 4.6 collective-permute-start.31
  325.2 20.2 %mlp_back1.1 = (f32[1024,1024]{1,0:T(8,128)}, bf16[1024,1024]{1,0:T(8,128)(2,1)}, bf16[1024,1024]{1,0:T(8,128)(2,1)}) custom-call(f32[1024,1024]{1,0:T(8,128)} %get-tuple-element.286.x1, bf16[1024,1024]{1,0:T(8,128)(2,1)} %get-tuple-element.265.refs_2_.crel, f32[1,1024]{1,0:T(1,128)} %copy.73.gain, f32[1024,1024]{1,0:T(8,128)} %get-tuple-element.313.dn2, ...), custom_call_target="tpu_custom_call" | custom-call | flops 6442450944 | bytes 31457280 | tf_op jit(solution)/shard_map/mlp_back1/pallas_call | solution.py:521
  345.5 3.5 add_convert_fusion
  351.4 8.0 %out_grad.1 = (bf16[512,4096]{1,0:T(8,128)(2,1)}, bf16[512,4096]{1,0:T(8,128)(2,1)}) custom-call(bf16[1024,1024]{1,0:T(8,128)(2,1)} %get-tuple-element.326.refs_0_, bf16[1024,2048]{1,0:T(8,128)(2,1)} %get-tuple-element.261.o.refs_1_), custom_call_target="tpu_custom_call" | custom-call | flops 4294967296 | bytes 10485760 | tf_op jit(solution)/shard_map/out_grad/pallas_call | solution.py:217
  359.4 19.2 %attend_back.4 = (f32[8,128]{1,0:T(8,128)}, bf16[512,4096]{1,0:T(8,128)(2,1)}, bf16[512,4096]{1,0:T(8,128)(2,1)}, bf16[1024,2048]{1,0:T(8,128)(2,1)}, bf16[1024,...) custom-call(bf16[1024,1024]{1,0:T(8,128)(2,1)} %get-tuple-element.321.refs_0_, ...), custom_call_target="tpu_custom_call", output_to_operand_aliasing={{1}: (15, {}), {2}: (16, {})} | custom-call | flops 8589934592 | bytes 13631488 | tf_op jit(solution)/shard_map/attend_back/pallas_call | solution.py:217
  382.9 18.9 %attend_back.5 = (f32[8,128]{1,0:T(8,128)}, bf16[512,4096]{1,0:T(8,128)(2,1)}, bf16[512,4096]{1,0:T(8,128)(2,1)}, bf16[1024,2048]{1,0:T(8,128)(2,1)}, bf16[1024,...) custom-call(bf16[1024,1024]{1,0:T(8,128)(2,1)} %get-tuple-element.32, ...), custom_call_target="tpu_custom_call", output_to_operand_aliasing={{1}: (15, {}), {2}: (16, {}), {3}: (17, {}), {4}: (18, {}),... | custom-call | flops 8589934592 | bytes 13631488 | tf_op jit(solution)/shard_map/attend_back/pallas_call | solution.py:217
  401.9 19.2 %attend_back.6 = (f32[8,128]{1,0:T(8,128)}, bf16[512,2048]{1,0:T(8,128)(2,1)}, bf16[512,2048]{1,0:T(8,128)(2,1)}, bf16[1024,2048]{1,0:T(8,128)(2,1)}, bf16[1024,...) custom-call(bf16[1024,1024]{1,0:T(8,128)(2,1)} %get-tuple-element.321., ...), custom_call_target="tpu_custom_call", output_to_operand_aliasing={{3}: (15, {}), {4}: (16, {}), {5}: (17, {})} | custom-call | flops 8589934592 | bytes 13631488 | tf_op jit(solution)/shard_map/attend_back/pallas_call | solution.py:217
  421.4 3.7 add_convert_fusion.2
  431.7 19.1 %attend_back.7 = (f32[8,128]{1,0:T(8,128)}, bf16[512,2048]{1,0:T(8,128)(2,1)}, bf16[512,2048]{1,0:T(8,128)(2,1)}, bf16[1024,2048]{1,0:T(8,128)(2,1)}, bf16[1024,...) custom-call(bf16[1024,1024]{1,0:T(8,128)(2,1)} %get-tuple-element.32, ...), custom_call_target="tpu_custom_call", output_to_operand_aliasing={{1}: (15, {}), {2}: (16, {}), {3}: (17, {}), {4}: (18, {}),... | custom-call | flops 8589934592 | bytes 13631488 | tf_op jit(solution)/shard_map/attend_back/pallas_call | solution.py:217
  458.9 12.8 %result.1 = bf16[1024,1024]{1,0:T(8,128)(2,1)} custom-call(f32[1024,1024]{1,0:T(8,128)} %get-tuple-element.381.res, bf16[1024,1024]{1,0:T(8,128)(2,1)} %fusion.perm, bf16[1024,1536]{1,0:T(8,128)(2,1)} %get-tuple-element.382.hidden, bf16[512,4608]{1,0:T(8,128)(2,1)} %bitcast.116, bf16[512,4608]{1,0:T(8,128)(2,1)} %collective-permute-done.23.refs_5_.w1), custom_call_target="tpu_custom_call" | custom-call | flops 5368709120 | bytes 14680064 | tf_op jit(solution)/shard_map/result/pallas_call | solution.py:574
  473.6 6.4 %collective-permute-start.52 = (f32[8,128]{1,0:T(8,128)S(1)}, f32[8,128]{1,0:T(8,128)S(1)}, u32[]{:S(2)}, u32[]{:S(2)}) collective-permute-start(f32[8,128]{1,0:T(8,128)S(1)} %add_add_fusion.1), channel_id=1, source_target_pairs={{0,8},{1,9},{2,10},{3,11},{4,12},{5,13},{6,14},{7,15},{8,0},{9,1},... | collective-permute-start | bytes 12296 | tf_op jit(solution)/shard_map/ppermute | solution.py:160
  482.7 19.4 %input_back.1 = bf16[1024,1024]{1,0:T(8,128)(2,1)} custom-call(bf16[1024,1024]{1,0:T(8,128)(2,1)} %get-tuple-element.237.trel, f32[1024,1024]{1,0:T(8,128)} %get-tuple-element.392.dx1, f32[1,1024]{1,0:T(1,128)} %copy.72.gain, bf16[1024,1024]{1,0:T(8,128)(2,1)} %fusion.perm, bf16[1024,2048]{1,0:T(8,128)(2,1)} %get-tuple-element.393.dq, ...), custom_call_target="tpu_custom_call" | custom-call | flops 10737418240 | bytes 27262976 | tf_op jit(solution)/shard_map/input_back/pallas_call | solution.py:697
  506.2 3.5 collective-permute-done.59
  528.2 18.2 %collective-permute-done.61 = bf16[2,1,1,1,16,2048]{5,4,0,3,2,1:T(8,128)(2,1)S(1)} collective-permute-done((bf16[2,1,1,1,16,2048]{5,4,0,3,2,1:T(8,128)(2,1)S(1)}, bf16[2,1,1,1,16,2048]{5,4,0,3,2,1:T(8,128)(2,1)S(1)}, u32[]{:S(2)}, u32[]{:S(2)}) %collective-permute-start.61) | collective-permute-done | bytes 131104 | tf_op jit(solution)/shard_map/ppermute | solution.py:52
  (308 shorter events, 136.5 us)
Async XLA Ops:
  2.4 22.5 %collective-permute-start.2 = (bf16[1,1,1,32,4224]{4,3,2,1,0:T(8,128)(2,1)S(1)}, bf16[1,1,1,32,4224]{4,3,2,1,0:T(8,128)(2,1)S(1)}, u32[]{:S(2)}, u32[]{:S(2)}) collective-permute-start(bf16[1,1,1,32,4224]{4,3,2,1,0:T(8,128)(2,1)S(1)} %fusion.19), channel_id=1, source_target_pairs={{0,24},{1,25},{2,26},{3,27},{4,28},{5,29},{6,30},{7,31},{8,0},{9,1... | collective-permute-start | bytes 811016 | tf_op jit(solution)/shard_map/ppermute | solution.py:52
  7.5 23.1 %collective-permute-start.3 = (bf16[1,1,1,32,4224]{4,3,2,1,0:T(8,128)(2,1)S(1)}, bf16[1,1,1,32,4224]{4,3,2,1,0:T(8,128)(2,1)}, u32[]{:S(2)}, u32[]{:S(2)}) collective-permute-start(bf16[1,1,1,32,4224]{4,3,2,1,0:T(8,128)(2,1)S(1)} %fusion.19), channel_id=1, source_target_pairs={{0,16},{1,17},{2,18},{3,19},{4,20},{5,21},{6,22},{7,23},{8,24},{9,... | collective-permute-start | bytes 811016 | tf_op jit(solution)/shard_map/ppermute | solution.py:52
  7.5 23.1 %collective-permute-start.4 = (bf16[1,1,1,32,4224]{4,3,2,1,0:T(8,128)(2,1)S(1)}, bf16[1,1,1,32,4224]{4,3,2,1,0:T(8,128)(2,1)}, u32[]{:S(2)}, u32[]{:S(2)}) collective-permute-start(bf16[1,1,1,32,4224]{4,3,2,1,0:T(8,128)(2,1)S(1)} %fusion.19), channel_id=1, source_target_pairs={{0,8},{1,9},{2,10},{3,11},{4,12},{5,13},{6,14},{7,15},{8,16},{9,17... | collective-permute-start | bytes 811016 | tf_op jit(solution)/shard_map/ppermute | solution.py:52
  46.8 40.4 %collective-permute-start.10 = (bf16[2,1,4,16,4224]{4,3,2,1,0:T(8,128)(2,1)S(1)}, bf16[2,1,4,16,4224]{4,3,2,1,0:T(8,128)(2,1)S(1)}, u32[]{:S(2)}, u32[]{:S(2)}) collective-permute-start(bf16[2,1,4,16,4224]{4,3,2,1,0:T(8,128)(2,1)S(1)} %pad_maximum_fusion.8), channel_id=1, source_target_pairs={{0,4},{1,5},{2,6},{3,7},{4,0},{5,1},{6,2},{7,3},{8,12},{9,13},{10,... | collective-permute-start | bytes 3244040 | tf_op jit(solution)/shard_map/ppermute | solution.py:52
  48.5 38.7 %collective-permute-start.11 = (bf16[1,2,4,16,4224]{4,3,2,1,0:T(8,128)(2,1)S(1)}, bf16[1,2,4,16,4224]{4,3,2,1,0:T(8,128)(2,1)S(1)}, u32[]{:S(2)}, u32[]{:S(2)}) collective-permute-start(bf16[1,2,4,16,4224]{4,3,2,1,0:T(8,128)(2,1)S(1)} %pad_maximum_fusion.9), channel_id=1, source_target_pairs={{0,2},{1,3},{2,0},{3,1},{4,6},{5,7},{6,4},{7,5},{8,10},{9,11},{10,... | collective-permute-start | bytes 3244040 | tf_op jit(solution)/shard_map/ppermute | solution.py:52
  50.1 37.1 %collective-permute-start.13 = (bf16[1,1,1,32,6656]{4,3,2,1,0:T(8,128)(2,1)S(1)}, bf16[1,1,1,32,6656]{4,3,2,1,0:T(8,128)(2,1)}, u32[]{:S(2)}, u32[]{:S(2)}) collective-permute-start(bf16[1,1,1,32,6656]{4,3,2,1,0:T(8,128)(2,1)S(1)} %maximum_bitcast_fusion.6), channel_id=1, source_target_pairs={{0,16},{1,17},{2,18},{3,19},{4,20},{5,21},{6,22},{7,23},{8,24},{9,... | collective-permute-start | bytes 1277960 | tf_op jit(solution)/shard_map/ppermute | solution.py:52
  52.3 34.9 %collective-permute-start.14 = (bf16[1,1,1,32,6656]{4,3,2,1,0:T(8,128)(2,1)S(1)}, bf16[1,1,1,32,6656]{4,3,2,1,0:T(8,128)(2,1)}, u32[]{:S(2)}, u32[]{:S(2)}) collective-permute-start(bf16[1,1,1,32,6656]{4,3,2,1,0:T(8,128)(2,1)S(1)} %maximum_bitcast_fusion.6), channel_id=1, source_target_pairs={{0,8},{1,9},{2,10},{3,11},{4,12},{5,13},{6,14},{7,15},{8,16},{9,17... | collective-permute-start | bytes 1277960 | tf_op jit(solution)/shard_map/ppermute | solution.py:52
  94.4 33.2 %collective-permute-start.7 = (bf16[2,2,2,1,16,4608]{5,4,2,1,3,0:T(8,128)(2,1)}, bf16[2,2,2,1,16,4608]{5,4,2,1,3,0:T(8,128)(2,1)}, u32[]{:S(2)}, u32[]{:S(2)}) collective-permute-start(bf16[2,2,2,1,16,4608]{5,4,2,1,3,0:T(8,128)(2,1)} %pad_maximum_fusion.6), channel_id=1, source_target_pairs={{0,24},{1,25},{2,26},{3,27},{4,28},{5,29},{6,30},{7,31},{8,0},{9,1... | collective-permute-start | bytes 3538952 | tf_op jit(solution)/shard_map/ppermute | solution.py:52
  114.5 38.7 %collective-permute-start.18 = (bf16[2,1,4,16,6656]{4,3,2,1,0:T(8,128)(2,1)S(1)}, bf16[2,1,4,16,6656]{4,3,2,1,0:T(8,128)(2,1)}, u32[]{:S(2)}, u32[]{:S(2)}) collective-permute-start(bf16[2,1,4,16,6656]{4,3,2,1,0:T(8,128)(2,1)S(1)} %pad_maximum_fusion.4), channel_id=1, source_target_pairs={{0,4},{1,5},{2,6},{3,7},{4,0},{5,1},{6,2},{7,3},{8,12},{9,13},{10,... | collective-permute-start | bytes 5111816 | tf_op jit(solution)/shard_map/ppermute | solution.py:52
  116.4 38.4 %collective-permute-start.19 = (bf16[1,2,4,16,6656]{4,3,2,1,0:T(8,128)(2,1)S(1)}, bf16[1,2,4,16,6656]{4,3,2,1,0:T(8,128)(2,1)}, u32[]{:S(2)}, u32[]{:S(2)}) collective-permute-start(bf16[1,2,4,16,6656]{4,3,2,1,0:T(8,128)(2,1)S(1)} %pad_maximum_fusion.5), channel_id=1, source_target_pairs={{0,2},{1,3},{2,0},{3,1},{4,6},{5,7},{6,4},{7,5},{8,10},{9,11},{10,... | collective-permute-start | bytes 5111816 | tf_op jit(solution)/shard_map/ppermute | solution.py:52
  162.3 28.6 %collective-permute-start.20 = (bf16[512,6656]{1,0:T(8,128)(2,1)S(1)}, bf16[512,6656]{1,0:T(8,128)(2,1)S(1)}, u32[]{:S(2)}, u32[]{:S(2)}) collective-permute-start(bf16[512,6656]{1,0:T(8,128)(2,1)S(1)} %bitcast.101), channel_id=1, source_target_pairs={{0,1},{1,0},{2,3},{3,2},{4,5},{5,4},{6,7},{7,6},{8,9},{9,8},{10,11... | collective-permute-start | bytes 20447240 | tf_op jit(solution)/shard_map/ppermute | solution.py:52
  162.3 28.6 %collective-permute-start.21 = (bf16[2,2,2,1,16,4608]{5,4,2,1,3,0:T(8,128)(2,1)}, bf16[2,2,2,1,16,4608]{5,4,2,1,3,0:T(8,128)(2,1)S(1)}, u32[]{:S(2)}, u32[]{:S(2)}) collective-permute-start(bf16[2,2,2,1,16,4608]{5,4,2,1,3,0:T(8,128)(2,1)} %collective-permute-done.7), channel_id=1, source_target_pairs={{0,24},{1,25},{2,26},{3,27},{4,28},{5,29},{6,30},{7,31},{8,0},{9,1... | collective-permute-start | bytes 3538952 | tf_op jit(solution)/shard_map/ppermute | solution.py:52
  193.6 28.1 %collective-permute-start.22 = (bf16[2,2,2,1,16,4608]{5,4,2,1,3,0:T(8,128)(2,1)S(1)}, bf16[2,2,2,1,16,4608]{5,4,2,1,3,0:T(8,128)(2,1)}, u32[]{:S(2)}, u32[]{:S(2)}) collective-permute-start(bf16[2,2,2,1,16,4608]{5,4,2,1,3,0:T(8,128)(2,1)S(1)} %collective-permute-done.21), channel_id=1, source_target_pairs={{0,24},{1,25},{2,26},{3,27},{4,28},{5,29},{6,30},{7,31},{8,0},{9,1... | collective-permute-start | bytes 3538952 | tf_op jit(solution)/shard_map/ppermute | solution.py:52
  224.7 26.3 %collective-permute-start.23 = (bf16[512,4608]{1,0:T(8,128)(2,1)S(1)}, bf16[512,4608]{1,0:T(8,128)(2,1)}, u32[]{:S(2)}, u32[]{:S(2)}) collective-permute-start(bf16[512,4608]{1,0:T(8,128)(2,1)S(1)} %bitcast.111), channel_id=1, source_target_pairs={{0,1},{1,0},{2,3},{3,2},{4,5},{5,4},{6,7},{7,6},{8,9},{9,8},{10,11... | collective-permute-start | bytes 14155784 | tf_op jit(solution)/shard_map/ppermute | solution.py:52
  273.2 28.4 %collective-permute-start.25 = (bf16[1,2,4,16,4608]{4,3,2,1,0:T(8,128)(2,1)S(1)}, bf16[1,2,4,16,4608]{4,3,2,1,0:T(8,128)(2,1)S(1)}, u32[]{:S(2)}, u32[]{:S(2)}) collective-permute-start(bf16[1,2,4,16,4608]{4,3,2,1,0:T(8,128)(2,1)S(1)} %bitcast.141), channel_id=1, source_target_pairs={{0,2},{1,3},{2,0},{3,1},{4,6},{5,7},{6,4},{7,5},{8,10},{9,11},{10,... | collective-permute-start | bytes 3538952 | tf_op jit(solution)/shard_map/ppermute | solution.py:52
  274.8 28.1 %collective-permute-start.26 = (bf16[2,1,4,16,4608]{4,3,2,1,0:T(8,128)(2,1)S(1)}, bf16[2,1,4,16,4608]{4,3,2,1,0:T(8,128)(2,1)S(1)}, u32[]{:S(2)}, u32[]{:S(2)}) collective-permute-start(bf16[2,1,4,16,4608]{4,3,2,1,0:T(8,128)(2,1)S(1)} %slice.358), channel_id=1, source_target_pairs={{0,4},{1,5},{2,6},{3,7},{4,0},{5,1},{6,2},{7,3},{8,12},{9,13},{10,... | collective-permute-start | bytes 3538952 | tf_op jit(solution)/shard_map/ppermute | solution.py:52
  319.5 25.9 %collective-permute-start.29 = (bf16[512,4608]{1,0:T(8,128)(2,1)}, bf16[512,4608]{1,0:T(8,128)(2,1)}, u32[]{:S(2)}, u32[]{:S(2)}) collective-permute-start(bf16[512,4608]{1,0:T(8,128)(2,1)} %get-tuple-element.312), channel_id=1, source_target_pairs={{0,1},{1,0},{2,3},{3,2},{4,5},{5,4},{6,7},{7,6},{8,9},{9,8},{10,11... | collective-permute-start | bytes 14155784 | tf_op jit(solution)/shard_map/ppermute | solution.py:52
  320.6 58.0 %collective-permute-start.30 = (bf16[2,1,1,1,16,4608]{5,4,0,3,2,1:T(8,128)(2,1)S(1)}, bf16[2,1,1,1,16,4608]{5,4,0,3,2,1:T(8,128)(2,1)S(1)}, u32[]{:S(2)}, u32[]{:S(2)}) collective-permute-start(bf16[2,1,1,1,16,4608]{5,4,0,3,2,1:T(8,128)(2,1)S(1)} %get-tuple-element.442), channel_id=1, source_target_pairs={{0,8},{1,9},{2,10},{3,11},{4,12},{5,13},{6,14},{7,15},{8,16},{9,17... | collective-permute-start | bytes 884744 | tf_op jit(solution)/shard_map/ppermute | solution.py:52
  320.6 58.0 %collective-permute-start.31 = (bf16[2,1,1,1,16,4608]{5,4,0,3,2,1:T(8,128)(2,1)S(1)}, bf16[2,1,1,1,16,4608]{5,4,0,3,2,1:T(8,128)(2,1)}, u32[]{:S(2)}, u32[]{:S(2)}) collective-permute-start(bf16[2,1,1,1,16,4608]{5,4,0,3,2,1:T(8,128)(2,1)S(1)} %get-tuple-element.443), channel_id=1, source_target_pairs={{0,16},{1,17},{2,18},{3,19},{4,20},{5,21},{6,22},{7,23},{8,24},{9,... | collective-permute-start | bytes 884744 | tf_op jit(solution)/shard_map/ppermute | solution.py:52
  325.2 53.4 %collective-permute-start.32 = (bf16[2,1,1,1,16,4608]{5,4,0,3,2,1:T(8,128)(2,1)S(1)}, bf16[2,1,1,1,16,4608]{5,4,0,3,2,1:T(8,128)(2,1)}, u32[]{:S(2)}, u32[]{:S(2)}) collective-permute-start(bf16[2,1,1,1,16,4608]{5,4,0,3,2,1:T(8,128)(2,1)S(1)} %get-tuple-element.444), channel_id=1, source_target_pairs={{0,24},{1,25},{2,26},{3,27},{4,28},{5,29},{6,30},{7,31},{8,0},{9,1... | collective-permute-start | bytes 884744 | tf_op jit(solution)/shard_map/ppermute | solution.py:52
  350.2 28.4 %collective-permute-start.33 = (bf16[1,2,4,16,4608]{4,3,2,1,0:T(8,128)(2,1)}, bf16[1,2,4,16,4608]{4,3,2,1,0:T(8,128)(2,1)S(1)}, u32[]{:S(2)}, u32[]{:S(2)}) collective-permute-start(bf16[1,2,4,16,4608]{4,3,2,1,0:T(8,128)(2,1)} %bitcast.31), channel_id=1, source_target_pairs={{0,2},{1,3},{2,0},{3,1},{4,6},{5,7},{6,4},{7,5},{8,10},{9,11},{10,... | collective-permute-start | bytes 3538952 | tf_op jit(solution)/shard_map/ppermute | solution.py:52
  351.0 27.7 %collective-permute-start.34 = (bf16[2,1,4,16,4608]{4,3,2,1,0:T(8,128)(2,1)S(1)}, bf16[2,1,4,16,4608]{4,3,2,1,0:T(8,128)(2,1)S(1)}, u32[]{:S(2)}, u32[]{:S(2)}) collective-permute-start(bf16[2,1,4,16,4608]{4,3,2,1,0:T(8,128)(2,1)S(1)} %slice.373), channel_id=1, source_target_pairs={{0,4},{1,5},{2,6},{3,7},{4,0},{5,1},{6,2},{7,3},{8,12},{9,13},{10,... | collective-permute-start | bytes 3538952 | tf_op jit(solution)/shard_map/ppermute | solution.py:52
  379.4 22.4 %collective-permute-start.35 = (bf16[1,1,4,16,4608]{4,3,2,1,0:T(8,128)(2,1)S(1)}, bf16[1,1,4,16,4608]{4,3,2,1,0:T(8,128)(2,1)S(1)}, u32[]{:S(2)}, u32[]{:S(2)}) collective-permute-start(bf16[1,1,4,16,4608]{4,3,2,1,0:T(8,128)(2,1)S(1)} %slice.374), channel_id=1, source_target_pairs={{0,4},{1,5},{2,6},{3,7},{4,0},{5,1},{6,2},{7,3},{8,12},{9,13},{10,... | collective-permute-start | bytes 1769480 | tf_op jit(solution)/shard_map/ppermute | solution.py:52
  425.4 25.7 %collective-permute-start.41 = (bf16[1,2,4,16,4096]{4,3,2,1,0:T(8,128)(2,1)S(1)}, bf16[1,2,4,16,4096]{4,3,2,1,0:T(8,128)(2,1)}, u32[]{:S(2)}, u32[]{:S(2)}) collective-permute-start(bf16[1,2,4,16,4096]{4,3,2,1,0:T(8,128)(2,1)S(1)} %bitcast.142), channel_id=1, source_target_pairs={{0,2},{1,3},{2,0},{3,1},{4,6},{5,7},{6,4},{7,5},{8,10},{9,11},{10,... | collective-permute-start | bytes 3145736 | tf_op jit(solution)/shard_map/ppermute | solution.py:52
  426.1 25.3 %collective-permute-start.42 = (bf16[2,1,4,16,4096]{4,3,2,1,0:T(8,128)(2,1)S(1)}, bf16[2,1,4,16,4096]{4,3,2,1,0:T(8,128)(2,1)S(1)}, u32[]{:S(2)}, u32[]{:S(2)}) collective-permute-start(bf16[2,1,4,16,4096]{4,3,2,1,0:T(8,128)(2,1)S(1)} %slice.388), channel_id=1, source_target_pairs={{0,4},{1,5},{2,6},{3,7},{4,0},{5,1},{6,2},{7,3},{8,12},{9,13},{10,... | collective-permute-start | bytes 3145736 | tf_op jit(solution)/shard_map/ppermute | solution.py:52
  427.4 23.4 %collective-permute-start.38 = (bf16[2,1,1,1,16,4608]{5,4,0,3,2,1:T(8,128)(2,1)S(1)}, bf16[2,1,1,1,16,4608]{5,4,0,3,2,1:T(8,128)(2,1)S(1)}, u32[]{:S(2)}, u32[]{:S(2)}) collective-permute-start(bf16[2,1,1,1,16,4608]{5,4,0,3,2,1:T(8,128)(2,1)S(1)} %get-tuple-element.438), channel_id=1, source_target_pairs={{0,8},{1,9},{2,10},{3,11},{4,12},{5,13},{6,14},{7,15},{8,16},{9,17... | collective-permute-start | bytes 884744 | tf_op jit(solution)/shard_map/ppermute | solution.py:52
  472.8 29.5 %collective-permute-start.51 = (f32[8,128]{1,0:T(8,128)S(1)}, f32[8,128]{1,0:T(8,128)S(1)}, u32[]{:S(2)}, u32[]{:S(2)}) collective-permute-start(f32[8,128]{1,0:T(8,128)S(1)} %add_add_fusion.1), channel_id=1, source_target_pairs={{0,4},{1,5},{2,6},{3,7},{4,0},{5,1},{6,2},{7,3},{8,12},{9,13},{10,... | collective-permute-start | bytes 12296 | tf_op jit(solution)/shard_map/ppermute | solution.py:160
  473.6 28.7 %collective-permute-start.52 = (f32[8,128]{1,0:T(8,128)S(1)}, f32[8,128]{1,0:T(8,128)S(1)}, u32[]{:S(2)}, u32[]{:S(2)}) collective-permute-start(f32[8,128]{1,0:T(8,128)S(1)} %add_add_fusion.1), channel_id=1, source_target_pairs={{0,8},{1,9},{2,10},{3,11},{4,12},{5,13},{6,14},{7,15},{8,0},{9,1},... | collective-permute-start | bytes 12296 | tf_op jit(solution)/shard_map/ppermute | solution.py:160
  480.0 22.3 %collective-permute-start.53 = (f32[8,128]{1,0:T(8,128)S(1)}, f32[8,128]{1,0:T(8,128)S(1)}, u32[]{:S(2)}, u32[]{:S(2)}) collective-permute-start(f32[8,128]{1,0:T(8,128)S(1)} %add_add_fusion.1), channel_id=1, source_target_pairs={{0,12},{1,13},{2,14},{3,15},{4,8},{5,9},{6,10},{7,11},{8,4},{9,5},... | collective-permute-start | bytes 12296 | tf_op jit(solution)/shard_map/ppermute | solution.py:160
  514.8 31.6 %collective-permute-start.54 = (bf16[2,1,1,1,16,4096]{5,4,0,3,2,1:T(8,128)(2,1)S(1)}, bf16[2,1,1,1,16,4096]{5,4,0,3,2,1:T(8,128)(2,1)S(1)}, u32[]{:S(2)}, u32[]{:S(2)}) collective-permute-start(bf16[2,1,1,1,16,4096]{5,4,0,3,2,1:T(8,128)(2,1)S(1)} %get-tuple-element.449), channel_id=1, source_target_pairs={{0,8},{1,9},{2,10},{3,11},{4,12},{5,13},{6,14},{7,15},{8,16},{9,17... | collective-permute-start | bytes 786440 | tf_op jit(solution)/shard_map/ppermute | solution.py:52
  514.8 31.6 %collective-permute-start.55 = (bf16[2,1,1,1,16,4096]{5,4,0,3,2,1:T(8,128)(2,1)S(1)}, bf16[2,1,1,1,16,4096]{5,4,0,3,2,1:T(8,128)(2,1)S(1)}, u32[]{:S(2)}, u32[]{:S(2)}) collective-permute-start(bf16[2,1,1,1,16,4096]{5,4,0,3,2,1:T(8,128)(2,1)S(1)} %get-tuple-element.450), channel_id=1, source_target_pairs={{0,16},{1,17},{2,18},{3,19},{4,20},{5,21},{6,22},{7,23},{8,24},{9,... | collective-permute-start | bytes 786440 | tf_op jit(solution)/shard_map/ppermute | solution.py:52
  517.4 29.0 %collective-permute-start.56 = (bf16[2,1,1,1,16,4096]{5,4,0,3,2,1:T(8,128)(2,1)S(1)}, bf16[2,1,1,1,16,4096]{5,4,0,3,2,1:T(8,128)(2,1)S(1)}, u32[]{:S(2)}, u32[]{:S(2)}) collective-permute-start(bf16[2,1,1,1,16,4096]{5,4,0,3,2,1:T(8,128)(2,1)S(1)} %get-tuple-element.447), channel_id=1, source_target_pairs={{0,24},{1,25},{2,26},{3,27},{4,28},{5,29},{6,30},{7,31},{8,0},{9,1... | collective-permute-start | bytes 786440 | tf_op jit(solution)/shard_map/ppermute | solution.py:52
  (69 other events, 700.4 us)

commit v3 on v2

--- a/solution.py
+++ b/solution.py
@@ -52,7 +52,16 @@
     return lax.ppermute(value, AX, pairs)
 
 
-def gather_chain(value, n, ends_first=True):
+def spread(values, n, axis, sign, split):
+    places = list(range(1, len(values)))
+    stages = [[k for k in places if k % 2 == 0], [k for k in places if k % 2]]
+    got = {}
+    for stage in stages if split and stages[0] else [places]:
+        got.update(zip(stage, (yield [move(values[k], n, axis, sign * k) for k in stage])))
+    return [got[k] for k in places]
+
+
+def gather_chain(value, n, ends_first=True, ring=True):
     ax = axes_of(n)[1:]
     m = len(ax)
     rows, cols = value.shape
@@ -60,8 +69,13 @@
     cur = value.reshape((1,) * m + (rows, cols))
     if ends_first:
         for a in range(2, m):
-            s = yield [move(cur, n, ax[a], -k) for k in range(1, ax[a][1])]
-            cur = jnp.concatenate([cur] + s, axis=a)
+            if ring:
+                got = [cur]
+                for _ in range(ax[a][1] - 1):
+                    got += yield [move(got[-1], n, ax[a], -1)]
+            else:
+                got = [cur] + (yield from spread([None] + [cur] * (ax[a][1] - 1), n, ax[a], -1, True))
+            cur = jnp.concatenate(got, axis=a)
     parts = [cur[..., :h, :], cur[..., h:, :]]
     for pair in ((0, 1), (1, 0)):
         s = yield [move(u, n, ax[a], -1) for u, a in zip(parts, pair)]
@@ -78,7 +92,7 @@
     return [cur] + s
 
 
-def scatter_chain(blocks, n):
+def scatter_chain(blocks, n, split=True):
     ax = axes_of(n)[1:]
     cols = blocks[0].shape[1]
     h = D // n // 2
@@ -99,7 +113,7 @@
     acc = jnp.stack(parts)
     for a in range(len(ax) - 1, 1, -1):
         r = ax[a][1]
-        s = yield [move(part(acc, k, a + 1), n, ax[a], k) for k in range(1, r)]
+        s = yield from spread([part(acc, k, a + 1) for k in range(r)], n, ax[a], 1, split)
         terms = [part(acc, 0, a + 1)] + s
         acc = sum(u.astype(F32) for u in terms).astype(B16)
     return [u.reshape(2 * h, cols) for u in terms]
@@ -273,32 +287,35 @@
             out[at, lanes] = y.astype(B16)
 
 
-def queries_kernel(trel, gain, w0, w1, cos, sin, qg, q, rawq, n1, n1_t):
+def queries_kernel(trel, g0, g1, w0, w1, cos, sin, qg, q, rawq, n1, n1_t, gains):
     @pl.when(pl.program_id(0) == 0)
     def _():
+        gains[...] = joined((g0, g1)).astype(F32).T[:8]
+        gain = gains[0:1, :]
         for at in chunks(trel.shape[0]):
             x = trel[at, :].astype(F32)
-            x = (x * inv_rms(x) * gain[...]).astype(B16)
+            x = (x * inv_rms(x) * gain).astype(B16)
             n1[at, :] = x
             n1_t[:, at] = x.T
 
     head_rows(n1, joined((w0, w1)), cos, sin, qg, q, rawq)
 
 
-def project_queries(trel, gain, w, cos, sin, qg):
+def project_queries(trel, w, cos, sin, qg):
     t = trel.shape[0]
     table, one = whole((t, HEAD_SIZE)), whole((1, HEAD_SIZE))
     out = pl.BlockSpec((t, COLS), lambda j: (0, j))
     return call(
         queries_kernel,
         (QW // COLS,),
-        [whole((t, D)), whole((1, D))] + halves_of(COLS, lambda j: j) + [table, table, one],
-        [out, out, whole((t, D)), whole((D, t))],
-        [sds((t, QW), B16)] * 2 + [sds((t, D), B16), sds((D, t), B16)],
+        [whole((t, D))] + halves_of(HEAD_SIZE, lambda j: 3 * QW // HEAD_SIZE)
+        + halves_of(COLS, lambda j: j) + [table, table, one],
+        [out, out, whole((t, D)), whole((D, t)), whole((8, D))],
+        [sds((t, QW), B16)] * 2 + [sds((t, D), B16), sds((D, t), B16), sds((8, D), F32)],
         flops=2 * t * D * QW,
         moved=2 * (D * QW + t * (2 * QW + 3 * D)),
         name="project_queries",
-    )(trel, gain, *w, cos, sin, qg)
+    )(trel, *w, *w, cos, sin, qg)
 
 
 def keys_kernel(n1, w0, w1, cos, sin, kg, k, rawk, v):
@@ -413,7 +430,7 @@
         after_kernel,
         (QW // COLS,),
         [pl.BlockSpec((t, COLS), lambda j: (0, j))]
-        + halves_of(COLS, lambda j: MLP_COLS // COLS + j)
+        + halves_of(COLS, lambda j: 2 * QW // COLS + j)
         + [whole((t, D)), whole((1, D))],
         [whole((t, D)), whole((t, D)), whole((D, t))],
         [sds((t, D), F32), sds((t, D), B16), sds((D, t), B16)],
@@ -660,7 +677,7 @@
     return chained(
         attend_back_kernel,
         (count,),
-        [whole((t, D)), whole((D, t))] + halves_of(PAIR, lambda g: MLP_COLS // PAIR + base + g)
+        [whole((t, D)), whole((D, t))] + halves_of(PAIR, lambda g: 2 * QW // PAIR + base + g)
         + [both, head, head, both, head, pl.BlockSpec((1, GROUP, t), lambda g: (base + g, 0, 0)),
            whole((1, t)), table, table, one, one],
         [datt, n1_t, *w, q, k, v, rawq, rawk, lse, first, *tables],
@@ -800,11 +817,11 @@
         by_step(w_gate[:, cols], w_up[:, cols], down_t[:, cols])
         for cols in (slice(0, PART), slice(PART, FF))
     ]
-    shards1 = jnp.concatenate([w_query, w_key, w_value, gain_cols], axis=1)
-    shards2 = jnp.concatenate([halves[0], w_out.T], axis=1)
-    chain1 = Chain(gather_chain(shards1, n), count)
-    chain2 = Chain(gather_chain(shards2, n), count)
-    chain3 = Chain(gather_chain(halves[1], n, ends_first=False), count)
+    shards1 = jnp.concatenate([w_query, w_key, w_value, w_out.T, gain_cols], axis=1)
+    ends = [r for _, r in axes_of(n)[3:]]
+    chain1 = Chain(gather_chain(shards1, n), 3 + sum(r - 1 for r in ends))
+    chain2 = Chain(gather_chain(halves[0], n, ring=False), 3 + sum(1 + (r > 2) for r in ends))
+    chain3 = Chain(gather_chain(halves[1], n, ends_first=False), 3 + sum(r - 1 for r in ends))
 
     index, first = run_starts(segments[0])
     half = HEAD_SIZE // 2
@@ -818,88 +835,81 @@
     kg = k_gain.astype(F32).reshape(1, HEAD_SIZE)
     perm = (jnp.arange(D, dtype=jnp.int32)[:, None] == absolute_rows(n)[None, :]).astype(B16)
 
-    window([chain1, chain3], [chain3])
-    cos, sin, perm = window([chain3], [chain1, chain3], cos, sin, perm)
+    window([chain1, chain3], [chain1, chain3])
+    cos, sin, perm = window([chain1, chain3], [chain1, chain3], cos, sin, perm)
     while chain1.stages > 3:
         window([chain1], [chain1])
-    tokens, cotangent = window([chain1, chain2], [chain1], tokens, cotangent)
+    tokens, cotangent = window([chain1, chain2], [chain1, chain2], tokens, cotangent)
+    while chain2.stages > 4:
+        window([chain2], [chain2])
+    every = [chain1, chain2, chain3]
     trel, crel, crel_t = prep(tokens, cotangent, perm)
-    trel, crel, crel_t = window([chain1], [chain1, chain2], trel, crel, crel_t)
-    while chain2.stages > 3:
-        window([chain2], [chain2])
-    window([chain1, chain2, chain3], [chain1])
+    trel, crel, crel_t = window(every, every, trel, crel, crel_t)
+    while chain3.stages > 3:
+        window([chain3], [chain3])
+    window([chain1, chain2], [chain1, chain2])
     finish(chain1)
     w_in = chain1.value
-    gains = jnp.concatenate([w[:, QW + 2 * KW :] for w in w_in], axis=0).astype(F32).T
+
+    q, rawq, n1, n1_t, gains = project_queries(trel, w_in, cos, sin, qg)
     gain_a, gain_m = gains[0:1], gains[1:2]
-
-    q, rawq, n1, n1_t = project_queries(trel, gain_a, w_in, cos, sin, qg)
-    q, rawq, n1, n1_t = window([], [chain2], q, rawq, n1, n1_t)
     k, rawk, v = project_keys(n1, w_in, cos, sin, kg)
-    k, rawk, v = window([chain2], [chain3], k, rawk, v)
+    q, k, v = window([chain2, chain3], [chain2, chain3], q, k, v)
     o, lse = attend(q, k, v, first)
-    o, lse = window([chain3], [chain2], o, lse)
-    window([chain2], [chain2, chain3])
+    o, lse = window([chain2], [chain2], o, lse)
     finish(chain2)
-    x1, n2, n2_t = after_attention(o, chain2.value, trel, gain_m)
-
-    def units(w, base, acts):
-        return mlp(n2, n2_t, crel, crel_t, w, base, steps // 3, MLP_COLS, acts)
-
-    acts = units(chain2.value, 0, None)
+    x1, n2, n2_t = after_attention(o, w_in, trel, gain_m)
+
+    def units(w, base, count, acts):
+        return mlp(n2, n2_t, crel, crel_t, w, base, count, MLP_COLS, acts)
+
+    acts = units(chain2.value, 0, steps, None)
     acts = window([chain3], [chain3], *acts)
-    while chain3.stages > 1:
-        window([chain3], [chain3])
-    acts = units(chain2.value, steps // 3, acts)
-    acts = units(chain2.value, 2 * steps // 3, acts)
-    acts = window([chain3], [chain3], *acts)
-    finish(chain3)
     hidden0, dact0, *grads = acts
     sum1 = Chain(scatter_chain(grads, n))
     dn2, res = mlp_back0(x1, hidden0, dact0, chain2.value)
-    dn2, res = window([sum1], [sum1], dn2, res)
-
-    acts = units(chain3.value, 0, None)
-    acts = units(chain3.value, steps // 3, acts)
-    acts = window([sum1], [sum1], *acts)
-    acts = units(chain3.value, 2 * steps // 3, acts)
+    dn2, res = window([chain3, sum1], [chain3, sum1], dn2, res)
+    finish(chain3)
+
+    acts = units(chain3.value, 0, steps, None)
     acts = window([sum1], [sum1], *acts)
     hidden1, dact1, *grads = acts
     sum2 = Chain(scatter_chain(grads, n))
     dx1, datt, datt_t = mlp_back1(x1, crel, gain_m, dn2, dact1, chain3.value)
-    dx1, datt, datt_t = window([sum1, sum2], [sum2], dx1, datt, datt_t)
+    dx1, datt, datt_t = window([sum1, sum2], [sum1, sum2], dx1, datt, datt_t)
 
     tables = (cos, sin, qg, kg)
     per = KEY_VALUE_HEADS // 4
 
     def heads(i, before, grads):
         return attend_back(
-            datt, n1_t, chain2.value, q, k, v, rawq, rawk, lse, first, tables,
+            datt, n1_t, w_in, q, k, v, rawq, rawk, lse, first, tables,
             i * per, per, before, grads,
         )
 
     gain0, *rest = heads(0, None, out_grad(datt_t, o))
-    gain0, *rest = window([sum2], [sum1, sum2], gain0, *rest)
+    gain0, *rest = window([sum2, sum1], [sum1, sum2], gain0, *rest)
     gain1, *rest = heads(1, rest[2:], rest[:2])
-    gain1, *rest = window([sum2], [sum2], gain1, *rest)
-    sum3 = Chain(scatter_chain(rest[:2], n))
+    gain1, *rest = window([sum2, sum1], [sum2, sum1], gain1, *rest)
+    sum3 = Chain(scatter_chain(rest[:2], n, split=False))
     gain2, *rest = heads(2, rest[2:], None)
-    gain2, *rest = window([sum2, sum3], [sum3], gain2, *rest)
+    gain2, *rest = window([sum2, sum3], [sum2, sum3], gain2, *rest)
     gain3, *rest = heads(3, rest[2:], rest[:2])
-    gain3, res, *rest = window([sum3], [sum2, sum3], gain3, res, *rest)
-    sum4 = Chain(scatter_chain(rest[:2], n))
+    gain3, res, *rest = window([sum2, sum3], [sum2, sum3], gain3, res, *rest)
+    sum4 = Chain(scatter_chain(rest[:2], n, split=False))
     dq, dk, dv = rest[2:]
+    result = make_result(res, perm, hidden1, chain3.value)
+    result, dq, dk, dv = window([sum4, sum3], [sum4, sum3], result, dq, dk, dv)
     total = Chain(sum_chain((gain0 + gain1) + (gain2 + gain3), n))
-    result = make_result(res, perm, hidden1, chain3.value)
-    result, dq, dk, dv = window([sum3, sum4, total], [sum3, sum4, total], result, dq, dk, dv)
+    last = [sum4, sum3, total]
     grad_tokens = input_back(trel, dx1, gain_a, perm, dq, dk, dv, w_in)
-    (grad_tokens,) = window([sum4, sum3, total], [sum4, total], grad_tokens)
-    window([sum4, total], [sum4, total])
-    finish(sum1, sum2, sum3, sum4, total)
-
+    (grad_tokens,) = window(last, last, grad_tokens)
+    finish(sum1, sum2)
     grad_down, grad_gate, grad_up, grad_mlp_gain = mlp_total(
         mlp_gain, w_gate, w_up, sum1.value, sum2.value
     )
+    (grad_mlp_gain,) = window(last, last, grad_mlp_gain)
+    finish(*last)
     grad_out, grad_query, grad_key, grad_value, grad_attn_gain = attn_total(
         attn_gain, w_query, w_key, w_value, sum3.value, sum4.value
     )

time: 561 us -> 499 us (0.89)
  waiting for transfers between devices: 110 us -> 71.1 us
  Pallas kernels: 296 us -> 272 us
  starting transfers between devices: 73.4 us -> 81.2 us
  local copies, waits for them, and re-layouts: 23.3 us -> 17.5 us
    ppermute x56, waiting for transfers between devices: 106 us -> 64.3 us  [move(): return lax.ppermute(value, AX, pairs)]
    pallas_call x11 -> x7, Pallas kernels: 159 us -> 136 us  [chained(): pl.pallas_call(body, grid=grid, in_specs=list(ins) + [pl.BlockSpec(memory...]
    ppermute x56, starting transfers between devices: 62.9 us -> 73.9 us  [move(): return lax.ppermute(value, AX, pairs)]
  transfers between devices with their start and end apart: 63 -> 63, of which waited for: 19 -> 16; matrix products, arithmetic and copies ran while one was open for 7% -> 5% of each run, Pallas kernels for 53% -> 55%
where the time goes in v3:
time: 499 us; the launch traced here: 490 us
  Pallas kernels  272 us (55%)
  starting transfers between devices  81.2 us (16%)
  waiting for transfers between devices  71.1 us (14%)
  other arithmetic  44.5 us (9%)
  local copies, waits for them, and re-layouts  17.5 us (4%)
    pallas_call x7, Pallas kernels, chained(): pl.pallas_call(body, grid=grid, in_specs=list(ins) + [pl.BlockSpec(memory...  136 us
    ppermute x56, starting transfers between devices, move(): return lax.ppermute(value, AX, pairs)  73.9 us
    ppermute x56, waiting for transfers between devices, move(): return lax.ppermute(value, AX, pairs)  64.3 us
    pallas_call x1, Pallas kernels, mlp_back1(): call(mlp_back1_kernel, (PART // STEP,), [whole((t, D)), whole((t, D)), wh...  19.9 us
    pallas_call x1, Pallas kernels, mlp_back0(): call(mlp_back0_kernel, (PART // STEP,), [whole((t, D)), at(STEP), at(2 *...  19.4 us
    pallas_call x1, Pallas kernels, input_back(): call(input_back_kernel, (t // BLK,), [rows_of(D), rows_of(D), whole((1, D...  19.1 us
    pallas_call x1, Pallas kernels, attend(): call(attend_kernel, (groups,), [both, head, head, whole((1, t))], [both,...  16 us
    convert_element_type x4, other arithmetic, scatter_chain(): acc = (keep.astype(F32) + s.astype(F32)).astype(B16)  13.3 us
  transfers between devices with their start and end apart: 63, of which 16 were waited for; matrix products, arithmetic and copies ran while one was open for 5% of the time, Pallas kernels for 55%

profile of v3, /device:TPU:0, one launch (start us, length us, event | category | flops | bytes accessed | tf_op | source)
XLA Modules:
  0.0 489.9 jit_solution(2613285710799153602)
XLA Ops:
  9.6 3.7 collective-permute-start
  21.3 4.3 collective-permute-start.3
  29.0 3.7 collective-permute-done.5
  33.0 4.0 collective-permute-start.6
  38.2 8.1 %collective-permute-done.6 = bf16[1,1,1,32,6272]{4,3,2,1,0:T(8,128)(2,1)S(1)} collective-permute-done((bf16[1,1,1,32,6272]{4,3,2,1,0:T(8,128)(2,1)S(1)}, bf16[1,1,1,32,6272]{4,3,2,1,0:T(8,128)(2,1)S(1)}, u32[]{:S(2)}, u32[]{:S(2)}) %collective-permute-start.6) | collective-permute-done | bytes 401440 | tf_op jit(solution)/shard_map/ppermute | solution.py:52
  47.9 5.8 %collective-permute-done.9 = bf16[1,1,1,32,4608]{4,3,2,1,0:T(8,128)(2,1)S(1)} collective-permute-done((bf16[1,1,1,32,4608]{4,3,2,1,0:T(8,128)(2,1)S(1)}, bf16[1,1,1,32,4608]{4,3,2,1,0:T(8,128)(2,1)S(1)}, u32[]{:S(2)}, u32[]{:S(2)}) %collective-permute-start.9) | collective-permute-done | bytes 294944 | tf_op jit(solution)/shard_map/ppermute | solution.py:52
  53.8 9.2 %collective-permute-done.8 = bf16[1,1,4,16,6272]{4,3,2,1,0:T(8,128)(2,1)S(1)} collective-permute-done((bf16[1,1,4,16,6272]{4,3,2,1,0:T(8,128)(2,1)S(1)}, bf16[1,1,4,16,6272]{4,3,2,1,0:T(8,128)(2,1)S(1)}, u32[]{:S(2)}, u32[]{:S(2)}) %collective-permute-start.8) | collective-permute-done | bytes 802848 | tf_op jit(solution)/shard_map/ppermute | solution.py:52
  73.3 8.4 %prep.1 = (bf16[1024,1024]{1,0:T(8,128)(2,1)}, bf16[1024,1024]{1,0:T(8,128)(2,1)}, bf16[1024,1024]{1,0:T(8,128)(2,1)}) custom-call(bf16[1024,1024]{1,0:T(8,128)(2,1)} %tok, bf16[1024,1024]{1,0:T(8,128)(2,1)} %cot, bf16[1024,1024]{1,0:T(8,128)(2,1)} %fusion.perm), custom_call_target="tpu_custom_call" | custom-call | flops 4294967296 | bytes 12582912 | tf_op jit(solution)/shard_map/prep/pallas_call | solution.py:266
  81.7 18.2 %collective-permute-done.13 = bf16[1,1,1,32,4608]{4,3,2,1,0:T(8,128)(2,1)S(1)} collective-permute-done((bf16[1,1,1,32,4608]{4,3,2,1,0:T(8,128)(2,1)S(1)}, bf16[1,1,1,32,4608]{4,3,2,1,0:T(8,128)(2,1)S(1)}, u32[]{:S(2)}, u32[]{:S(2)}) %collective-permute-start.13) | collective-permute-done | bytes 294944 | tf_op jit(solution)/shard_map/ppermute | solution.py:52
  109.9 4.8 collective-permute-start.20
  114.7 7.5 %collective-permute-done.17 = bf16[1,1,4,16,4608]{4,3,2,1,0:T(8,128)(2,1)S(1)} collective-permute-done((bf16[1,1,4,16,4608]{4,3,2,1,0:T(8,128)(2,1)S(1)}, bf16[1,1,4,16,4608]{4,3,2,1,0:T(8,128)(2,1)S(1)}, u32[]{:S(2)}, u32[]{:S(2)}) %collective-permute-start.17) | collective-permute-done | bytes 589856 | tf_op jit(solution)/shard_map/ppermute | solution.py:52
  128.4 12.4 %project_queries.1 = (bf16[1024,2048]{1,0:T(8,128)(2,1)}, bf16[1024,2048]{1,0:T(8,128)(2,1)}, bf16[1024,1024]{1,0:T(8,128)(2,1)}, bf16[1024,1024]{1,0:T(8,128)(2,1)}, f32[8,1024]{1,0:T(8,128)}) custom-call(bf16[1024,1024]{1,0:T(8,128)(2,1)} %get-tuple-element.218.trel, bf16[512,6272]{1,0:T(8,128)(2,1)} %bitcast.98, ...), custom_call_target="tpu_custom_call" | custom-call | flops 4294967296 | bytes 18874368 | tf_op jit(solution)/shard_map/project_queries/pallas_call | solution.py:308
  140.8 10.7 %project_keys.1 = (bf16[1024,1024]{1,0:T(8,128)(2,1)}, bf16[1024,1024]{1,0:T(8,128)(2,1)}, bf16[1024,1024]{1,0:T(8,128)(2,1)}) custom-call(bf16[1024,1024]{1,0:T(8,128)(2,1)} %get-tuple-element.223.n1, bf16[512,6272]{1,0:T(8,128)(2,1)} %bitcast.100, bf16[512,6272]{1,0:T(8,128)(2,1)} %collective-permute-done.15.g1.w1.refs_3_, ...), custom_call_target="tpu_custom_call" | custom-call | flops 4294967296 | bytes 12582912 | tf_op jit(solution)/shard_map/project_keys/pallas_call | solution.py:340
  159.9 4.5 collective-permute-start.21
  164.5 16.0 %attend.1 = (bf16[1024,2048]{1,0:T(8,128)(2,1)}, f32[8,2,1024]{2,1,0:T(2,128)}) custom-call(bf16[1024,2048]{1,0:T(8,128)(2,1)} %get-tuple-element.229.q.refs_4_, bf16[1024,1024]{1,0:T(8,128)(2,1)} %get-tuple-element.230.k.refs_5_, bf16[1024,1024]{1,0:T(8,128)(2,1)} %get-tuple-element.231.v.refs_6_, s32[1,1024]{1,0:T(1,128)} %bitcast.149), custom_call_target="tpu_custom_call" | custom-call | flops 17179869184 | bytes 12582912 | tf_op jit(solution)/shard_map/attend/pallas_call | solution.py:394
  180.5 12.5 %after_attention.1 = (f32[1024,1024]{1,0:T(8,128)}, bf16[1024,1024]{1,0:T(8,128)(2,1)}, bf16[1024,1024]{1,0:T(8,128)(2,1)}) custom-call(bf16[1024,2048]{1,0:T(8,128)(2,1)} %get-tuple-element.234.o.refs_1_, bf16[512,6272]{1,0:T(8,128)(2,1)} %bitcast.101, bf16[512,6272]{1,0:T(8,128)(2,1)} %collective-permute-done.15.g1.w1.refs_3_, ...), custom_call_target="tpu_custom_call" | custom-call | flops 4294967296 | bytes 18874368 | tf_op jit(solution)/shard_map/after_attention/pallas_call | solution.py:429
  193.0 26.5 %mlp.2 = (bf16[1024,1536]{1,0:T(8,128)(2,1)}, bf16[1024,3072]{1,0:T(8,128)(2,1)}, bf16[512,4608]{1,0:T(8,128)(2,1)}, bf16[512,4608]{1,0:T(8,128)(2,1)}) custom-call(bf16[1024,1024]{1,0:T(8,128)(2,1)} %get-tuple-element.236.refs_0_, bf16[1024,1024]{1,0:T(8,128)(2,1)} %get-tuple-element.237.refs_1_, bf16[1024,1024]{1,0:T(8,128)(2,1)} %get-tuple-element.238.refs_2_.crel, ...), custom_call_target="tpu_custom_call" | custom-call | flops 19327352832 | bytes 36700160 | tf_op jit(solution)/shard_map/mlp/pallas_call | solution.py:231
  223.0 19.4 %mlp_back0.1 = (f32[1024,1024]{1,0:T(8,128)}, f32[1024,1024]{1,0:T(8,128)}) custom-call(f32[1024,1024]{1,0:T(8,128)} %get-tuple-element.248.x1, bf16[1024,1536]{1,0:T(8,128)(2,1)} %get-tuple-element.249.hidden, bf16[1024,3072]{1,0:T(8,128)(2,1)} %get-tuple-element.250.dact, bf16[512,4608]{1,0:T(8,128)(2,1)} %bitcast.121, ...), custom_call_target="tpu_custom_call" | custom-call | flops 9663676416 | bytes 31457280 | tf_op jit(solution)/shard_map/mlp_back0/pallas_call | solution.py:498
  242.4 4.9 %add_convert_fusion.1 = bf16[512,4608]{1,0:T(8,128)(2,1)S(1)} fusion(bf16[512,4608]{1,0:T(8,128)(2,1)} %collective-permute-done.24, bf16[512,4608]{1,0:T(8,128)(2,1)} %get-tuple-element.245), kind=kLoop, calls=%fused_computation.1 | loop fusion | flops 9437184 | bytes 14155776 | tf_op jit(solution)/shard_map/convert_element_type | solution.py:101
  249.0 26.7 %mlp.3 = (bf16[1024,1536]{1,0:T(8,128)(2,1)}, bf16[1024,3072]{1,0:T(8,128)(2,1)}, bf16[512,4608]{1,0:T(8,128)(2,1)}, bf16[512,4608]{1,0:T(8,128)(2,1)}) custom-call(bf16[1024,1024]{1,0:T(8,128)(2,1)} %get-tuple-element.236.refs_0_, bf16[1024,1024]{1,0:T(8,128)(2,1)} %get-tuple-element.237.refs_1_, bf16[1024,1024]{1,0:T(8,128)(2,1)} %get-tuple-element.238.refs_2_.crel, ...), custom_call_target="tpu_custom_call" | custom-call | flops 19327352832 | bytes 36700160 | tf_op jit(solution)/shard_map/mlp/pallas_call | solution.py:231
  281.0 19.9 %mlp_back1.1 = (f32[1024,1024]{1,0:T(8,128)}, bf16[1024,1024]{1,0:T(8,128)(2,1)}, bf16[1024,1024]{1,0:T(8,128)(2,1)}) custom-call(f32[1024,1024]{1,0:T(8,128)} %get-tuple-element.248.x1, bf16[1024,1024]{1,0:T(8,128)(2,1)} %get-tuple-element.238.refs_2_.crel, f32[1,1024]{1,0:T(1,128)} %get-tuple-element.416.gain, f32[1024,1024]{1,0:T(8,128)} %get-tuple-element.263.dn2, ...), custom_call_target="tpu_custom_call" | custom-call | flops 6442450944 | bytes 31457280 | tf_op jit(solution)/shard_map/mlp_back1/pallas_call | solution.py:538
  300.9 3.8 add_convert_fusion
  312.5 8.4 %out_grad.1 = (bf16[512,4096]{1,0:T(8,128)(2,1)}, bf16[512,4096]{1,0:T(8,128)(2,1)}) custom-call(bf16[1024,1024]{1,0:T(8,128)(2,1)} %get-tuple-element.276.refs_0_, bf16[1024,2048]{1,0:T(8,128)(2,1)} %get-tuple-element.234.o.refs_1_), custom_call_target="tpu_custom_call" | custom-call | flops 4294967296 | bytes 10485760 | tf_op jit(solution)/shard_map/out_grad/pallas_call | solution.py:231
  320.9 18.4 %attend_back.4 = (f32[8,128]{1,0:T(8,128)}, bf16[512,4096]{1,0:T(8,128)(2,1)}, bf16[512,4096]{1,0:T(8,128)(2,1)}, bf16[1024,2048]{1,0:T(8,128)(2,1)}, bf16[1024,...) custom-call(bf16[1024,1024]{1,0:T(8,128)(2,1)} %get-tuple-element.271.refs_0_, ...), custom_call_target="tpu_custom_call", output_to_operand_aliasing={{1}: (15, {}), {2}: (16, {})} | custom-call | flops 8589934592 | bytes 13631488 | tf_op jit(solution)/shard_map/attend_back/pallas_call | solution.py:231
  342.9 18.6 %attend_back.5 = (f32[8,128]{1,0:T(8,128)}, bf16[512,4096]{1,0:T(8,128)(2,1)}, bf16[512,4096]{1,0:T(8,128)(2,1)}, bf16[1024,2048]{1,0:T(8,128)(2,1)}, bf16[1024,...) custom-call(bf16[1024,1024]{1,0:T(8,128)(2,1)} %get-tuple-element.27, ...), custom_call_target="tpu_custom_call", output_to_operand_aliasing={{1}: (15, {}), {2}: (16, {}), {3}: (17, {}), {4}: (18, {}),... | custom-call | flops 8589934592 | bytes 13631488 | tf_op jit(solution)/shard_map/attend_back/pallas_call | solution.py:231
  363.8 18.7 %attend_back.6 = (f32[8,128]{1,0:T(8,128)}, bf16[512,2048]{1,0:T(8,128)(2,1)}, bf16[512,2048]{1,0:T(8,128)(2,1)}, bf16[1024,2048]{1,0:T(8,128)(2,1)}, bf16[1024,...) custom-call(bf16[1024,1024]{1,0:T(8,128)(2,1)} %get-tuple-element.271., ...), custom_call_target="tpu_custom_call", output_to_operand_aliasing={{3}: (15, {}), {4}: (16, {}), {5}: (17, {})} | custom-call | flops 8589934592 | bytes 13631488 | tf_op jit(solution)/shard_map/attend_back/pallas_call | solution.py:231
  382.5 3.8 add_convert_fusion.2
  388.0 3.8 collective-permute-start.38
  391.8 18.6 %attend_back.7 = (f32[8,128]{1,0:T(8,128)}, bf16[512,2048]{1,0:T(8,128)(2,1)}, bf16[512,2048]{1,0:T(8,128)(2,1)}, bf16[1024,2048]{1,0:T(8,128)(2,1)}, bf16[1024,...) custom-call(bf16[1024,1024]{1,0:T(8,128)(2,1)} %get-tuple-element.27, ...), custom_call_target="tpu_custom_call", output_to_operand_aliasing={{1}: (15, {}), {2}: (16, {}), {3}: (17, {}), {4}: (18, {}),... | custom-call | flops 8589934592 | bytes 13631488 | tf_op jit(solution)/shard_map/attend_back/pallas_call | solution.py:231
  418.2 12.8 %result.1 = bf16[1024,1024]{1,0:T(8,128)(2,1)} custom-call(f32[1024,1024]{1,0:T(8,128)} %get-tuple-element.327.res, bf16[1024,1024]{1,0:T(8,128)(2,1)} %fusion.perm, bf16[1024,1536]{1,0:T(8,128)(2,1)} %get-tuple-element.328.hidden, bf16[512,4608]{1,0:T(8,128)(2,1)} %bitcast.110, bf16[512,4608]{1,0:T(8,128)(2,1)} %collective-permute-done.23.refs_5_.w1), custom_call_target="tpu_custom_call" | custom-call | flops 5368709120 | bytes 14680064 | tf_op jit(solution)/shard_map/result/pallas_call | solution.py:591
  441.6 19.1 %input_back.1 = bf16[1024,1024]{1,0:T(8,128)(2,1)} custom-call(bf16[1024,1024]{1,0:T(8,128)(2,1)} %get-tuple-element.218.trel, f32[1024,1024]{1,0:T(8,128)} %get-tuple-element.341.dx1, f32[1,1024]{1,0:T(1,128)} %get-tuple-element.415.gain, bf16[1024,1024]{1,0:T(8,128)(2,1)} %fusion.perm, bf16[1024,2048]{1,0:T(8,128)(2,1)} %get-tuple-element.342.dq, ...), custom_call_target="tpu_custom_call" | custom-call | flops 10737418240 | bytes 27262976 | tf_op jit(solution)/shard_map/input_back/pallas_call | solution.py:714
  478.0 6.8 %collective-permute-done.62 = f32[8,128]{1,0:T(8,128)S(1)} collective-permute-done((f32[8,128]{1,0:T(8,128)S(1)}, f32[8,128]{1,0:T(8,128)S(1)}, u32[]{:S(2)}, u32[]{:S(2)}) %collective-permute-start.62) | collective-permute-done | bytes 4128 | tf_op jit(solution)/shard_map/ppermute | solution.py:174
  (332 shorter events, 122.7 us)
Async XLA Ops:
  65.1 37.1 %collective-permute-start.11 = (bf16[1,2,4,16,6272]{4,3,2,1,0:T(8,128)(2,1)}, bf16[1,2,4,16,6272]{4,3,2,1,0:T(8,128)(2,1)S(1)}, u32[]{:S(2)}, u32[]{:S(2)}) collective-permute-start(bf16[1,2,4,16,6272]{4,3,2,1,0:T(8,128)(2,1)} %pad_maximum_fusion.5), channel_id=1, source_target_pairs={{0,2},{1,3},{2,0},{3,1},{4,6},{5,7},{6,4},{7,5},{8,10},{9,11},{10,... | collective-permute-start | bytes 4816904 | tf_op jit(solution)/shard_map/ppermute | solution.py:52
  65.6 36.6 %collective-permute-start.10 = (bf16[2,1,4,16,6272]{4,3,2,1,0:T(8,128)(2,1)S(1)}, bf16[2,1,4,16,6272]{4,3,2,1,0:T(8,128)(2,1)}, u32[]{:S(2)}, u32[]{:S(2)}) collective-permute-start(bf16[2,1,4,16,6272]{4,3,2,1,0:T(8,128)(2,1)S(1)} %pad_maximum_fusion.4), channel_id=1, source_target_pairs={{0,4},{1,5},{2,6},{3,7},{4,0},{5,1},{6,2},{7,3},{8,12},{9,13},{10,... | collective-permute-start | bytes 4816904 | tf_op jit(solution)/shard_map/ppermute | solution.py:52
  68.3 33.9 %collective-permute-start.14 = (bf16[2,2,2,1,16,4608]{5,4,2,1,3,0:T(8,128)(2,1)}, bf16[2,2,2,1,16,4608]{5,4,2,1,3,0:T(8,128)(2,1)}, u32[]{:S(2)}, u32[]{:S(2)}) collective-permute-start(bf16[2,2,2,1,16,4608]{5,4,2,1,3,0:T(8,128)(2,1)} %pad_maximum_fusion.6), channel_id=1, source_target_pairs={{0,24},{1,25},{2,26},{3,27},{4,28},{5,29},{6,30},{7,31},{8,0},{9,1... | collective-permute-start | bytes 3538952 | tf_op jit(solution)/shard_map/ppermute | solution.py:52
  69.5 30.4 %collective-permute-start.13 = (bf16[1,1,1,32,4608]{4,3,2,1,0:T(8,128)(2,1)S(1)}, bf16[1,1,1,32,4608]{4,3,2,1,0:T(8,128)(2,1)S(1)}, u32[]{:S(2)}, u32[]{:S(2)}) collective-permute-start(bf16[1,1,1,32,4608]{4,3,2,1,0:T(8,128)(2,1)S(1)} %reshape_reshape.6), channel_id=1, source_target_pairs={{0,8},{1,9},{2,10},{3,11},{4,12},{5,13},{6,14},{7,15},{8,16},{9,17... | collective-permute-start | bytes 884744 | tf_op jit(solution)/shard_map/ppermute | solution.py:52
  70.3 31.8 %collective-permute-start.12 = (bf16[1,1,1,32,4608]{4,3,2,1,0:T(8,128)(2,1)S(1)}, bf16[1,1,1,32,4608]{4,3,2,1,0:T(8,128)(2,1)}, u32[]{:S(2)}, u32[]{:S(2)}) collective-permute-start(bf16[1,1,1,32,4608]{4,3,2,1,0:T(8,128)(2,1)S(1)} %reshape_reshape.6), channel_id=1, source_target_pairs={{0,24},{1,25},{2,26},{3,27},{4,28},{5,29},{6,30},{7,31},{8,0},{9,1... | collective-permute-start | bytes 884744 | tf_op jit(solution)/shard_map/ppermute | solution.py:52
  109.9 41.6 %collective-permute-start.20 = (bf16[2,2,2,1,16,4608]{5,4,2,1,3,0:T(8,128)(2,1)}, bf16[2,2,2,1,16,4608]{5,4,2,1,3,0:T(8,128)(2,1)}, u32[]{:S(2)}, u32[]{:S(2)}) collective-permute-start(bf16[2,2,2,1,16,4608]{5,4,2,1,3,0:T(8,128)(2,1)} %collective-permute-done.14), channel_id=1, source_target_pairs={{0,24},{1,25},{2,26},{3,27},{4,28},{5,29},{6,30},{7,31},{8,0},{9,1... | collective-permute-start | bytes 3538952 | tf_op jit(solution)/shard_map/ppermute | solution.py:52
  125.9 27.3 %collective-permute-start.19 = (bf16[1,2,4,16,4608]{4,3,2,1,0:T(8,128)(2,1)}, bf16[1,2,4,16,4608]{4,3,2,1,0:T(8,128)(2,1)}, u32[]{:S(2)}, u32[]{:S(2)}) collective-permute-start(bf16[1,2,4,16,4608]{4,3,2,1,0:T(8,128)(2,1)} %pad_maximum_fusion.8), channel_id=1, source_target_pairs={{0,2},{1,3},{2,0},{3,1},{4,6},{5,7},{6,4},{7,5},{8,10},{9,11},{10,... | collective-permute-start | bytes 3538952 | tf_op jit(solution)/shard_map/ppermute | solution.py:52
  127.4 27.0 %collective-permute-start.18 = (bf16[2,1,4,16,4608]{4,3,2,1,0:T(8,128)(2,1)}, bf16[2,1,4,16,4608]{4,3,2,1,0:T(8,128)(2,1)}, u32[]{:S(2)}, u32[]{:S(2)}) collective-permute-start(bf16[2,1,4,16,4608]{4,3,2,1,0:T(8,128)(2,1)} %pad_maximum_fusion.7), channel_id=1, source_target_pairs={{0,4},{1,5},{2,6},{3,7},{4,0},{5,1},{6,2},{7,3},{8,12},{9,13},{10,... | collective-permute-start | bytes 3538952 | tf_op jit(solution)/shard_map/ppermute | solution.py:52
  157.9 22.6 %collective-permute-start.22 = (bf16[512,4608]{1,0:T(8,128)(2,1)S(1)}, bf16[512,4608]{1,0:T(8,128)(2,1)}, u32[]{:S(2)}, u32[]{:S(2)}) collective-permute-start(bf16[512,4608]{1,0:T(8,128)(2,1)S(1)} %bitcast.119), channel_id=1, source_target_pairs={{0,1},{1,0},{2,3},{3,2},{4,5},{5,4},{6,7},{7,6},{8,9},{9,8},{10,11... | collective-permute-start | bytes 14155784 | tf_op jit(solution)/shard_map/ppermute | solution.py:52
  159.9 59.5 %collective-permute-start.21 = (bf16[2,2,2,1,16,4608]{5,4,2,1,3,0:T(8,128)(2,1)}, bf16[2,2,2,1,16,4608]{5,4,2,1,3,0:T(8,128)(2,1)S(1)}, u32[]{:S(2)}, u32[]{:S(2)}) collective-permute-start(bf16[2,2,2,1,16,4608]{5,4,2,1,3,0:T(8,128)(2,1)} %collective-permute-done.20), channel_id=1, source_target_pairs={{0,24},{1,25},{2,26},{3,27},{4,28},{5,29},{6,30},{7,31},{8,0},{9,1... | collective-permute-start | bytes 3538952 | tf_op jit(solution)/shard_map/ppermute | solution.py:52
  247.7 28.0 %collective-permute-start.26 = (bf16[2,1,4,16,4608]{4,3,2,1,0:T(8,128)(2,1)S(1)}, bf16[2,1,4,16,4608]{4,3,2,1,0:T(8,128)(2,1)S(1)}, u32[]{:S(2)}, u32[]{:S(2)}) collective-permute-start(bf16[2,1,4,16,4608]{4,3,2,1,0:T(8,128)(2,1)S(1)} %slice.345), channel_id=1, source_target_pairs={{0,4},{1,5},{2,6},{3,7},{4,0},{5,1},{6,2},{7,3},{8,12},{9,13},{10,... | collective-permute-start | bytes 3538952 | tf_op jit(solution)/shard_map/ppermute | solution.py:52
  248.5 27.3 %collective-permute-start.25 = (bf16[1,2,4,16,4608]{4,3,2,1,0:T(8,128)(2,1)S(1)}, bf16[1,2,4,16,4608]{4,3,2,1,0:T(8,128)(2,1)S(1)}, u32[]{:S(2)}, u32[]{:S(2)}) collective-permute-start(bf16[1,2,4,16,4608]{4,3,2,1,0:T(8,128)(2,1)S(1)} %bitcast.132), channel_id=1, source_target_pairs={{0,2},{1,3},{2,0},{3,1},{4,6},{5,7},{6,4},{7,5},{8,10},{9,11},{10,... | collective-permute-start | bytes 3538952 | tf_op jit(solution)/shard_map/ppermute | solution.py:52
  275.7 25.1 %collective-permute-start.29 = (bf16[512,4608]{1,0:T(8,128)(2,1)}, bf16[512,4608]{1,0:T(8,128)(2,1)}, u32[]{:S(2)}, u32[]{:S(2)}) collective-permute-start(bf16[512,4608]{1,0:T(8,128)(2,1)} %get-tuple-element.262), channel_id=1, source_target_pairs={{0,1},{1,0},{2,3},{3,2},{4,5},{5,4},{6,7},{7,6},{8,9},{9,8},{10,11... | collective-permute-start | bytes 14155784 | tf_op jit(solution)/shard_map/ppermute | solution.py:52
  278.1 22.8 %collective-permute-start.28 = (bf16[1,1,4,16,4608]{4,3,2,1,0:T(8,128)(2,1)}, bf16[1,1,4,16,4608]{4,3,2,1,0:T(8,128)(2,1)S(1)}, u32[]{:S(2)}, u32[]{:S(2)}) collective-permute-start(bf16[1,1,4,16,4608]{4,3,2,1,0:T(8,128)(2,1)} %slice.349), channel_id=1, source_target_pairs={{0,2},{1,3},{2,0},{3,1},{4,6},{5,7},{6,4},{7,5},{8,10},{9,11},{10,... | collective-permute-start | bytes 1769480 | tf_op jit(solution)/shard_map/ppermute | solution.py:52
  279.6 21.3 %collective-permute-start.27 = (bf16[1,1,4,16,4608]{4,3,2,1,0:T(8,128)(2,1)}, bf16[1,1,4,16,4608]{4,3,2,1,0:T(8,128)(2,1)S(1)}, u32[]{:S(2)}, u32[]{:S(2)}) collective-permute-start(bf16[1,1,4,16,4608]{4,3,2,1,0:T(8,128)(2,1)} %slice.347), channel_id=1, source_target_pairs={{0,4},{1,5},{2,6},{3,7},{4,0},{5,1},{6,2},{7,3},{8,12},{9,13},{10,... | collective-permute-start | bytes 1769480 | tf_op jit(solution)/shard_map/ppermute | solution.py:52
  307.4 31.9 %collective-permute-start.30 = (bf16[2,1,1,1,16,4608]{5,4,0,3,2,1:T(8,128)(2,1)}, bf16[2,1,1,1,16,4608]{5,4,0,3,2,1:T(8,128)(2,1)}, u32[]{:S(2)}, u32[]{:S(2)}) collective-permute-start(bf16[2,1,1,1,16,4608]{5,4,0,3,2,1:T(8,128)(2,1)} %get-tuple-element.396), channel_id=1, source_target_pairs={{0,16},{1,17},{2,18},{3,19},{4,20},{5,21},{6,22},{7,23},{8,24},{9,... | collective-permute-start | bytes 884744 | tf_op jit(solution)/shard_map/ppermute | solution.py:52
  307.4 54.1 %collective-permute-start.35 = (bf16[2,1,1,1,16,4608]{5,4,0,3,2,1:T(8,128)(2,1)}, bf16[2,1,1,1,16,4608]{5,4,0,3,2,1:T(8,128)(2,1)}, u32[]{:S(2)}, u32[]{:S(2)}) collective-permute-start(bf16[2,1,1,1,16,4608]{5,4,0,3,2,1:T(8,128)(2,1)} %get-tuple-element.397), channel_id=1, source_target_pairs={{0,8},{1,9},{2,10},{3,11},{4,12},{5,13},{6,14},{7,15},{8,16},{9,17... | collective-permute-start | bytes 884744 | tf_op jit(solution)/shard_map/ppermute | solution.py:52
  308.0 53.5 %collective-permute-start.36 = (bf16[2,1,1,1,16,4608]{5,4,0,3,2,1:T(8,128)(2,1)}, bf16[2,1,1,1,16,4608]{5,4,0,3,2,1:T(8,128)(2,1)}, u32[]{:S(2)}, u32[]{:S(2)}) collective-permute-start(bf16[2,1,1,1,16,4608]{5,4,0,3,2,1:T(8,128)(2,1)} %get-tuple-element.398), channel_id=1, source_target_pairs={{0,24},{1,25},{2,26},{3,27},{4,28},{5,29},{6,30},{7,31},{8,0},{9,1... | collective-permute-start | bytes 884744 | tf_op jit(solution)/shard_map/ppermute | solution.py:52
  311.3 28.0 %collective-permute-start.32 = (bf16[2,1,4,16,4608]{4,3,2,1,0:T(8,128)(2,1)S(1)}, bf16[2,1,4,16,4608]{4,3,2,1,0:T(8,128)(2,1)S(1)}, u32[]{:S(2)}, u32[]{:S(2)}) collective-permute-start(bf16[2,1,4,16,4608]{4,3,2,1,0:T(8,128)(2,1)S(1)} %slice.357), channel_id=1, source_target_pairs={{0,4},{1,5},{2,6},{3,7},{4,0},{5,1},{6,2},{7,3},{8,12},{9,13},{10,... | collective-permute-start | bytes 3538952 | tf_op jit(solution)/shard_map/ppermute | solution.py:52
  312.0 27.3 %collective-permute-start.31 = (bf16[1,2,4,16,4608]{4,3,2,1,0:T(8,128)(2,1)S(1)}, bf16[1,2,4,16,4608]{4,3,2,1,0:T(8,128)(2,1)S(1)}, u32[]{:S(2)}, u32[]{:S(2)}) collective-permute-start(bf16[1,2,4,16,4608]{4,3,2,1,0:T(8,128)(2,1)S(1)} %bitcast.131), channel_id=1, source_target_pairs={{0,2},{1,3},{2,0},{3,1},{4,6},{5,7},{6,4},{7,5},{8,10},{9,11},{10,... | collective-permute-start | bytes 3538952 | tf_op jit(solution)/shard_map/ppermute | solution.py:52
  340.0 21.5 %collective-permute-start.34 = (bf16[1,1,4,16,4608]{4,3,2,1,0:T(8,128)(2,1)S(1)}, bf16[1,1,4,16,4608]{4,3,2,1,0:T(8,128)(2,1)S(1)}, u32[]{:S(2)}, u32[]{:S(2)}) collective-permute-start(bf16[1,1,4,16,4608]{4,3,2,1,0:T(8,128)(2,1)S(1)} %slice.361), channel_id=1, source_target_pairs={{0,2},{1,3},{2,0},{3,1},{4,6},{5,7},{6,4},{7,5},{8,10},{9,11},{10,... | collective-permute-start | bytes 1769480 | tf_op jit(solution)/shard_map/ppermute | solution.py:52
  361.5 21.0 %collective-permute-start.40 = (bf16[512,4096]{1,0:T(8,128)(2,1)}, bf16[512,4096]{1,0:T(8,128)(2,1)}, u32[]{:S(2)}, u32[]{:S(2)}) collective-permute-start(bf16[512,4096]{1,0:T(8,128)(2,1)} %get-tuple-element.301), channel_id=1, source_target_pairs={{0,1},{1,0},{2,3},{3,2},{4,5},{5,4},{6,7},{7,6},{8,9},{9,8},{10,11... | collective-permute-start | bytes 12582920 | tf_op jit(solution)/shard_map/ppermute | solution.py:52
  386.8 25.4 %collective-permute-start.42 = (bf16[2,1,4,16,4096]{4,3,2,1,0:T(8,128)(2,1)S(1)}, bf16[2,1,4,16,4096]{4,3,2,1,0:T(8,128)(2,1)S(1)}, u32[]{:S(2)}, u32[]{:S(2)}) collective-permute-start(bf16[2,1,4,16,4096]{4,3,2,1,0:T(8,128)(2,1)S(1)} %slice.375), channel_id=1, source_target_pairs={{0,4},{1,5},{2,6},{3,7},{4,0},{5,1},{6,2},{7,3},{8,12},{9,13},{10,... | collective-permute-start | bytes 3145736 | tf_op jit(solution)/shard_map/ppermute | solution.py:52
  387.5 25.1 %collective-permute-start.41 = (bf16[1,2,4,16,4096]{4,3,2,1,0:T(8,128)(2,1)S(1)}, bf16[1,2,4,16,4096]{4,3,2,1,0:T(8,128)(2,1)}, u32[]{:S(2)}, u32[]{:S(2)}) collective-permute-start(bf16[1,2,4,16,4096]{4,3,2,1,0:T(8,128)(2,1)S(1)} %bitcast.133), channel_id=1, source_target_pairs={{0,2},{1,3},{2,0},{3,1},{4,6},{5,7},{6,4},{7,5},{8,10},{9,11},{10,... | collective-permute-start | bytes 3145736 | tf_op jit(solution)/shard_map/ppermute | solution.py:52
  388.0 22.5 %collective-permute-start.37 = (bf16[2,1,1,1,16,4608]{5,4,0,3,2,1:T(8,128)(2,1)S(1)}, bf16[2,1,1,1,16,4608]{5,4,0,3,2,1:T(8,128)(2,1)S(1)}, u32[]{:S(2)}, u32[]{:S(2)}) collective-permute-start(bf16[2,1,1,1,16,4608]{5,4,0,3,2,1:T(8,128)(2,1)S(1)} %get-tuple-element.392), channel_id=1, source_target_pairs={{0,8},{1,9},{2,10},{3,11},{4,12},{5,13},{6,14},{7,15},{8,16},{9,17... | collective-permute-start | bytes 884744 | tf_op jit(solution)/shard_map/ppermute | solution.py:52
  388.0 22.5 %collective-permute-start.38 = (bf16[2,1,1,1,16,4608]{5,4,0,3,2,1:T(8,128)(2,1)S(1)}, bf16[2,1,1,1,16,4608]{5,4,0,3,2,1:T(8,128)(2,1)S(1)}, u32[]{:S(2)}, u32[]{:S(2)}) collective-permute-start(bf16[2,1,1,1,16,4608]{5,4,0,3,2,1:T(8,128)(2,1)S(1)} %get-tuple-element.393), channel_id=1, source_target_pairs={{0,24},{1,25},{2,26},{3,27},{4,28},{5,29},{6,30},{7,31},{8,0},{9,1... | collective-permute-start | bytes 884744 | tf_op jit(solution)/shard_map/ppermute | solution.py:52
  417.6 21.9 %collective-permute-start.52 = (f32[8,128]{1,0:T(8,128)S(1)}, f32[8,128]{1,0:T(8,128)S(1)}, u32[]{:S(2)}, u32[]{:S(2)}) collective-permute-start(f32[8,128]{1,0:T(8,128)S(1)} %add_add_fusion.2), channel_id=1, source_target_pairs={{0,2},{1,3},{2,0},{3,1},{4,6},{5,7},{6,4},{7,5},{8,10},{9,11},{10,... | collective-permute-start | bytes 12296 | tf_op jit(solution)/shard_map/ppermute | solution.py:174
  434.3 26.4 %collective-permute-start.48 = (bf16[2,1,1,1,16,4096]{5,4,0,3,2,1:T(8,128)(2,1)S(1)}, bf16[2,1,1,1,16,4096]{5,4,0,3,2,1:T(8,128)(2,1)S(1)}, u32[]{:S(2)}, u32[]{:S(2)}) collective-permute-start(bf16[2,1,1,1,16,4096]{5,4,0,3,2,1:T(8,128)(2,1)S(1)} %get-tuple-element.402), channel_id=1, source_target_pairs={{0,8},{1,9},{2,10},{3,11},{4,12},{5,13},{6,14},{7,15},{8,16},{9,17... | collective-permute-start | bytes 786440 | tf_op jit(solution)/shard_map/ppermute | solution.py:52
  434.4 26.4 %collective-permute-start.49 = (bf16[2,1,1,1,16,4096]{5,4,0,3,2,1:T(8,128)(2,1)S(1)}, bf16[2,1,1,1,16,4096]{5,4,0,3,2,1:T(8,128)(2,1)S(1)}, u32[]{:S(2)}, u32[]{:S(2)}) collective-permute-start(bf16[2,1,1,1,16,4096]{5,4,0,3,2,1:T(8,128)(2,1)S(1)} %get-tuple-element.403), channel_id=1, source_target_pairs={{0,16},{1,17},{2,18},{3,19},{4,20},{5,21},{6,22},{7,23},{8,24},{9,... | collective-permute-start | bytes 786440 | tf_op jit(solution)/shard_map/ppermute | solution.py:52
  436.3 24.5 %collective-permute-start.50 = (bf16[2,1,1,1,16,4096]{5,4,0,3,2,1:T(8,128)(2,1)S(1)}, bf16[2,1,1,1,16,4096]{5,4,0,3,2,1:T(8,128)(2,1)S(1)}, u32[]{:S(2)}, u32[]{:S(2)}) collective-permute-start(bf16[2,1,1,1,16,4096]{5,4,0,3,2,1:T(8,128)(2,1)S(1)} %get-tuple-element.404), channel_id=1, source_target_pairs={{0,24},{1,25},{2,26},{3,27},{4,28},{5,29},{6,30},{7,31},{8,0},{9,1... | collective-permute-start | bytes 786440 | tf_op jit(solution)/shard_map/ppermute | solution.py:52
  439.5 21.3 %collective-permute-start.47 = (bf16[2,1,4,16,2048]{4,3,2,1,0:T(8,128)(2,1)S(1)}, bf16[2,1,4,16,2048]{4,3,2,1,0:T(8,128)(2,1)S(1)}, u32[]{:S(2)}, u32[]{:S(2)}) collective-permute-start(bf16[2,1,4,16,2048]{4,3,2,1,0:T(8,128)(2,1)S(1)} %slice.382), channel_id=1, source_target_pairs={{0,4},{1,5},{2,6},{3,7},{4,0},{5,1},{6,2},{7,3},{8,12},{9,13},{10,... | collective-permute-start | bytes 1572872 | tf_op jit(solution)/shard_map/ppermute | solution.py:52
  440.1 20.7 %collective-permute-start.46 = (bf16[1,2,4,16,2048]{4,3,2,1,0:T(8,128)(2,1)S(1)}, bf16[1,2,4,16,2048]{4,3,2,1,0:T(8,128)(2,1)S(1)}, u32[]{:S(2)}, u32[]{:S(2)}) collective-permute-start(bf16[1,2,4,16,2048]{4,3,2,1,0:T(8,128)(2,1)S(1)} %bitcast.138), channel_id=1, source_target_pairs={{0,2},{1,3},{2,0},{3,1},{4,6},{5,7},{6,4},{7,5},{8,10},{9,11},{10,... | collective-permute-start | bytes 1572872 | tf_op jit(solution)/shard_map/ppermute | solution.py:52
  (83 other events, 811.6 us)

commit v4 on v3

--- a/solution.py
+++ b/solution.py
@@ -21,6 +21,7 @@
 KW = KEY_VALUE_HEADS * HEAD_SIZE
 LONGEST = 512
 BLK = 256
+BACK_BLK = 128
 COLS = 512
 STEP = 256
 MLP_COLS = 3 * PART
@@ -250,8 +251,8 @@
     return jnp.concatenate([r[...] for r in refs], axis=0)
 
 
-def chunks(t):
-    return [slice(i * BLK, (i + 1) * BLK) for i in range(t // BLK)]
+def chunks(t, blk=BLK):
+    return [slice(i * blk, (i + 1) * blk) for i in range(t // blk)]
 
 
 def prep_kernel(tok, cot, perm, trel, crel, crel_t):
@@ -358,8 +359,8 @@
         bias[:, at] = jnp.where(allowed, 0.0, -1e30)
 
 
-def window_of(i):
-    return slice(max(0, i - LONGEST // BLK) * BLK, (i + 1) * BLK)
+def window_of(i, blk=BLK):
+    return slice(max(0, i - LONGEST // blk) * blk, (i + 1) * blk)
 
 
 def stacked(ref, at):
@@ -404,40 +405,32 @@
     )(q, k, v, first)
 
 
-def after_kernel(o, w0, w1, trel, gain, x1, n2, n2_t):
-    j = pl.program_id(0)
-
-    @pl.when(j == 0)
-    def _():
-        x1[...] = trel[...].astype(F32)
-
-    w = joined((w0, w1))
-    for at in chunks(o.shape[0]):
-        x1[at, :] += nt(o[at, :], w)
-
-    @pl.when(j == pl.num_programs(0) - 1)
-    def _():
-        for at in chunks(o.shape[0]):
-            x = x1[at, :]
-            y = (x * inv_rms(x) * gain[...]).astype(B16)
-            n2[at, :] = y
-            n2_t[:, at] = y.T
+def after_kernel(o, *refs):
+    *w, trel, gain, x1, n2, n2_t = refs
+    x = trel[...].astype(F32)
+    for i in range(len(w) // 2):
+        part = o[:, i * COLS : (i + 1) * COLS]
+        x = x + nt(part, joined(w[2 * i : 2 * i + 2]))
+    x1[...] = x
+    y = (x * inv_rms(x) * gain[...]).astype(B16)
+    n2[...] = y
+    n2_t[...] = y.T
 
 
 def after_attention(o, w, trel, gain):
     t = o.shape[0]
+    count = QW // COLS
+    specs = [halves_of(COLS, lambda i, c=c: 2 * QW // COLS + c) for c in range(count)]
     return call(
         after_kernel,
-        (QW // COLS,),
-        [pl.BlockSpec((t, COLS), lambda j: (0, j))]
-        + halves_of(COLS, lambda j: 2 * QW // COLS + j)
-        + [whole((t, D)), whole((1, D))],
-        [whole((t, D)), whole((t, D)), whole((D, t))],
+        (t // BLK,),
+        [rows_of(QW)] + [u for pair in specs for u in pair] + [rows_of(D), whole((1, D))],
+        [rows_of(D), rows_of(D), pl.BlockSpec((D, BLK), lambda i: (0, i))],
         [sds((t, D), F32), sds((t, D), B16), sds((D, t), B16)],
         flops=2 * t * D * QW,
         moved=2 * (t * QW + D * QW + 5 * t * D),
         name="after_attention",
-    )(o, *w, trel, gain)
+    )(o, *(list(w) * count), trel, gain)
 
 
 def mlp_kernel(n2, n2_t, c, c_t, w0, w1, hidden, dact, g0, g1):
@@ -507,24 +500,34 @@
     )(x1, hidden, dact, *w)
 
 
-def mlp_back1_kernel(x1, crel, gain, dn2, dact, w0, w1, dx1, datt, datt_t):
+def mlp_back1_kernel(
+    x1_in, crel_in, dn2_in, gain, dact, w0, w1, dx1, datt, datt_t, x1, crel, dn2, sems
+):
     j = pl.program_id(0)
-    w = joined((w0, w1))[:, STEP:]
+    loads = [
+        pltpu.make_async_copy(src, dst, sems.at[i])
+        for i, (src, dst) in enumerate(((x1_in, x1), (crel_in, crel), (dn2_in, dn2)))
+    ]
 
     @pl.when(j == 0)
     def _():
-        dx1[...] = dn2[...]
-
-    for at in chunks(x1.shape[0]):
+        for c in loads:
+            c.start()
+        dx1[...] = jnp.zeros_like(dx1)
+
+    w = joined((w0, w1))[:, STEP:]
+    for at in chunks(dx1.shape[0]):
         dx1[at, :] += nt(dact[at, :], w)
 
     @pl.when(j == pl.num_programs(0) - 1)
     def _():
-        for at in chunks(x1.shape[0]):
+        for c in loads:
+            c.wait()
+        for at in chunks(dx1.shape[0]):
             x = x1[at, :]
             s = inv_rms(x)
             r = x * s
-            grad = dx1[at, :] * gain[...]
+            grad = (dx1[at, :] + dn2[at, :]) * gain[...]
             inner = jnp.mean(grad * r, axis=-1, keepdims=True)
             d = crel[at, :].astype(F32) + s * (grad - r * inner)
             dx1[at, :] = d
@@ -538,14 +541,17 @@
     return call(
         mlp_back1_kernel,
         (PART // STEP,),
-        [whole((t, D)), whole((t, D)), whole((1, D)), whole((t, D)),
-         pl.BlockSpec((t, 2 * STEP), lambda j: (0, j))] + halves_of(3 * STEP, lambda j: j),
+        [pl.BlockSpec(memory_space=pl.ANY)] * 3
+        + [whole((1, D)), pl.BlockSpec((t, 2 * STEP), lambda j: (0, j))]
+        + halves_of(3 * STEP, lambda j: j),
         [whole((t, D)), whole((t, D)), whole((D, t))],
         [sds((t, D), F32), sds((t, D), B16), sds((D, t), B16)],
+        [pltpu.VMEM((t, D), F32), pltpu.VMEM((t, D), B16), pltpu.VMEM((t, D), F32),
+         pltpu.SemaphoreType.DMA((3,))],
         flops=4 * t * D * PART,
         moved=18 * t * D + 4 * PART * (t + D),
         name="mlp_back1",
-    )(x1, crel, gain, dn2, dact, *w)
+    )(x1, crel, dn2, gain, dact, *w)
 
 
 def out_grad_kernel(datt_t, o, g0, g1):
@@ -628,8 +634,8 @@
     kt = k[...].T
     dk_sum[...] = jnp.zeros_like(dk_sum)
     dv_sum[...] = jnp.zeros_like(dv_sum)
-    for i, at in enumerate(chunks(t)):
-        keys = window_of(i)
+    for i, at in enumerate(chunks(t, BACK_BLK)):
+        keys = window_of(i, BACK_BLK)
         q2, do2 = stacked(q, at), stacked(do, at)
         b = bias[keys, at]
         level = jnp.concatenate([lse[0, r : r + 1, at] for r in range(GROUP)], axis=1)
@@ -644,7 +650,7 @@
         for r in range(GROUP):
             lanes = slice(r * HEAD_SIZE, (r + 1) * HEAD_SIZE)
             grad, part = head_back(
-                dq2[r * BLK : (r + 1) * BLK, :], rawq[at, lanes], cos[at, :], sin[at, :], qgain[...]
+                dq2[r * BACK_BLK : (r + 1) * BACK_BLK, :], rawq[at, lanes], cos[at, :], sin[at, :], qgain[...]
             )
             low[at, lanes] = grad
             gains[0:1, :] += part

time: 499 us -> 493 us (0.988)
  Pallas kernels: 272 us -> 265 us
  transfers between devices with their start and end apart: 63 -> 63, of which waited for: 16 -> 19; matrix products, arithmetic and copies ran while one was open for 5% -> 5% of each run, Pallas kernels for 55% -> 54%
where the time goes in v4:
time: 493 us; the launch traced here: 483 us
  Pallas kernels  265 us (54%)
  starting transfers between devices  81.5 us (17%)
  waiting for transfers between devices  72.2 us (15%)
  other arithmetic  44.5 us (9%)
  local copies, waits for them, and re-layouts  17.5 us (4%)
    pallas_call x7, Pallas kernels, chained(): pl.pallas_call(body, grid=grid, in_specs=list(ins) + [pl.BlockSpec(memory...  132 us
    ppermute x56, starting transfers between devices, move(): return lax.ppermute(value, AX, pairs)  74 us
    ppermute x56, waiting for transfers between devices, move(): return lax.ppermute(value, AX, pairs)  66 us
    pallas_call x1, Pallas kernels, mlp_back0(): call(mlp_back0_kernel, (PART // STEP,), [whole((t, D)), at(STEP), at(2 *...  19.4 us
    pallas_call x1, Pallas kernels, input_back(): call(input_back_kernel, (t // BLK,), [rows_of(D), rows_of(D), whole((1, D...  19.3 us
    pallas_call x1, Pallas kernels, mlp_back1(): call(mlp_back1_kernel, (PART // STEP,), [pl.BlockSpec(memory_space=pl.ANY...  17.9 us
    pallas_call x1, Pallas kernels, attend(): call(attend_kernel, (groups,), [both, head, head, whole((1, t))], [both,...  16.1 us
    convert_element_type x4, other arithmetic, scatter_chain(): acc = (keep.astype(F32) + s.astype(F32)).astype(B16)  13.3 us
  transfers between devices with their start and end apart: 63, of which 19 were waited for; matrix products, arithmetic and copies ran while one was open for 5% of the time, Pallas kernels for 54%

profile of v4, /device:TPU:0, one launch (start us, length us, event | category | flops | bytes accessed | tf_op | source)
XLA Modules:
  0.0 483.3 jit_solution(3844215161937268853)
XLA Ops:
  9.6 3.7 collective-permute-start
  21.3 4.3 collective-permute-start.3
  29.0 3.7 collective-permute-done.5
  33.0 4.0 collective-permute-start.6
  38.2 8.1 %collective-permute-done.6 = bf16[1,1,1,32,6272]{4,3,2,1,0:T(8,128)(2,1)S(1)} collective-permute-done((bf16[1,1,1,32,6272]{4,3,2,1,0:T(8,128)(2,1)S(1)}, bf16[1,1,1,32,6272]{4,3,2,1,0:T(8,128)(2,1)S(1)}, u32[]{:S(2)}, u32[]{:S(2)}) %collective-permute-start.6) | collective-permute-done | bytes 401440 | tf_op jit(solution)/shard_map/ppermute | solution.py:53
  47.9 5.8 %collective-permute-done.9 = bf16[1,1,1,32,4608]{4,3,2,1,0:T(8,128)(2,1)S(1)} collective-permute-done((bf16[1,1,1,32,4608]{4,3,2,1,0:T(8,128)(2,1)S(1)}, bf16[1,1,1,32,4608]{4,3,2,1,0:T(8,128)(2,1)S(1)}, u32[]{:S(2)}, u32[]{:S(2)}) %collective-permute-start.9) | collective-permute-done | bytes 294944 | tf_op jit(solution)/shard_map/ppermute | solution.py:53
  53.8 9.2 %collective-permute-done.8 = bf16[1,1,4,16,6272]{4,3,2,1,0:T(8,128)(2,1)S(1)} collective-permute-done((bf16[1,1,4,16,6272]{4,3,2,1,0:T(8,128)(2,1)S(1)}, bf16[1,1,4,16,6272]{4,3,2,1,0:T(8,128)(2,1)S(1)}, u32[]{:S(2)}, u32[]{:S(2)}) %collective-permute-start.8) | collective-permute-done | bytes 802848 | tf_op jit(solution)/shard_map/ppermute | solution.py:53
  73.3 8.4 %prep.1 = (bf16[1024,1024]{1,0:T(8,128)(2,1)}, bf16[1024,1024]{1,0:T(8,128)(2,1)}, bf16[1024,1024]{1,0:T(8,128)(2,1)}) custom-call(bf16[1024,1024]{1,0:T(8,128)(2,1)} %tok, bf16[1024,1024]{1,0:T(8,128)(2,1)} %cot, bf16[1024,1024]{1,0:T(8,128)(2,1)} %fusion.perm), custom_call_target="tpu_custom_call" | custom-call | flops 4294967296 | bytes 12582912 | tf_op jit(solution)/shard_map/prep/pallas_call | solution.py:267
  81.7 18.2 %collective-permute-done.13 = bf16[1,1,1,32,4608]{4,3,2,1,0:T(8,128)(2,1)S(1)} collective-permute-done((bf16[1,1,1,32,4608]{4,3,2,1,0:T(8,128)(2,1)S(1)}, bf16[1,1,1,32,4608]{4,3,2,1,0:T(8,128)(2,1)S(1)}, u32[]{:S(2)}, u32[]{:S(2)}) %collective-permute-start.13) | collective-permute-done | bytes 294944 | tf_op jit(solution)/shard_map/ppermute | solution.py:53
  109.9 4.6 collective-permute-start.20
  114.4 7.7 %collective-permute-done.17 = bf16[1,1,4,16,4608]{4,3,2,1,0:T(8,128)(2,1)S(1)} collective-permute-done((bf16[1,1,4,16,4608]{4,3,2,1,0:T(8,128)(2,1)S(1)}, bf16[1,1,4,16,4608]{4,3,2,1,0:T(8,128)(2,1)S(1)}, u32[]{:S(2)}, u32[]{:S(2)}) %collective-permute-start.17) | collective-permute-done | bytes 589856 | tf_op jit(solution)/shard_map/ppermute | solution.py:53
  128.4 12.4 %project_queries.1 = (bf16[1024,2048]{1,0:T(8,128)(2,1)}, bf16[1024,2048]{1,0:T(8,128)(2,1)}, bf16[1024,1024]{1,0:T(8,128)(2,1)}, bf16[1024,1024]{1,0:T(8,128)(2,1)}, f32[8,1024]{1,0:T(8,128)}) custom-call(bf16[1024,1024]{1,0:T(8,128)(2,1)} %get-tuple-element.218.trel.refs_8_, bf16[512,6272]{1,0:T(8,128)(2,1)} %bitcast.98, ...), custom_call_target="tpu_custom_call" | custom-call | flops 4294967296 | bytes 18874368 | tf_op jit(solution)/shard_map/project_queries/pallas_call | solution.py:309
  140.8 10.7 %project_keys.1 = (bf16[1024,1024]{1,0:T(8,128)(2,1)}, bf16[1024,1024]{1,0:T(8,128)(2,1)}, bf16[1024,1024]{1,0:T(8,128)(2,1)}) custom-call(bf16[1024,1024]{1,0:T(8,128)(2,1)} %get-tuple-element.223.n1, bf16[512,6272]{1,0:T(8,128)(2,1)} %bitcast.100, bf16[512,6272]{1,0:T(8,128)(2,1)} %collective-permute-done.15.g1.w1.refs_1_.refs_3_.refs_5_.refs_7_, ...), custom_call_target="tpu_custom_call" | custom-call | flops 4294967296 | bytes 12582912 | tf_op jit(solution)/shard_map/project_keys/pallas_call | solution.py:341
  159.9 4.8 collective-permute-start.21
  164.7 16.1 %attend.1 = (bf16[1024,2048]{1,0:T(8,128)(2,1)}, f32[8,2,1024]{2,1,0:T(2,128)}) custom-call(bf16[1024,2048]{1,0:T(8,128)(2,1)} %get-tuple-element.229.q.refs_4_, bf16[1024,1024]{1,0:T(8,128)(2,1)} %get-tuple-element.230.k.refs_5_, bf16[1024,1024]{1,0:T(8,128)(2,1)} %get-tuple-element.231.v.refs_6_, s32[1,1024]{1,0:T(1,128)} %bitcast.152), custom_call_target="tpu_custom_call" | custom-call | flops 17179869184 | bytes 12582912 | tf_op jit(solution)/shard_map/attend/pallas_call | solution.py:395
  180.8 10.7 %after_attention.1 = (f32[1024,1024]{1,0:T(8,128)}, bf16[1024,1024]{1,0:T(8,128)(2,1)}, bf16[1024,1024]{1,0:T(8,128)(2,1)}) custom-call(bf16[1024,2048]{1,0:T(8,128)(2,1)} %get-tuple-element.234.o.refs_1_, bf16[512,6272]{1,0:T(8,128)(2,1)} %bitcast.101, bf16[512,6272]{1,0:T(8,128)(2,1)} %collective-permute-done.15.g1.w1.refs_1_.refs_3_.refs_5_.refs_7_, ...), custom_call_target="tpu_custom_call" | custom-call | flops 4294967296 | bytes 18874368 | tf_op jit(solution)/shard_map/after_attention/pallas_call | solution.py:424
  191.5 26.5 %mlp.2 = (bf16[1024,1536]{1,0:T(8,128)(2,1)}, bf16[1024,3072]{1,0:T(8,128)(2,1)}, bf16[512,4608]{1,0:T(8,128)(2,1)}, bf16[512,4608]{1,0:T(8,128)(2,1)}) custom-call(bf16[1024,1024]{1,0:T(8,128)(2,1)} %get-tuple-element.236.refs_0_, bf16[1024,1024]{1,0:T(8,128)(2,1)} %get-tuple-element.237.refs_1_, bf16[1024,1024]{1,0:T(8,128)(2,1)} %get-tuple-element.238.refs_2_.crel_in, ...), custom_call_target="tpu_custom_call" | custom-call | flops 19327352832 | bytes 36700160 | tf_op jit(solution)/shard_map/mlp/pallas_call | solution.py:232
  221.5 19.4 %mlp_back0.1 = (f32[1024,1024]{1,0:T(8,128)}, f32[1024,1024]{1,0:T(8,128)}) custom-call(f32[1024,1024]{1,0:T(8,128)} %get-tuple-element.248.x1.x1_in, bf16[1024,1536]{1,0:T(8,128)(2,1)} %get-tuple-element.249.hidden, bf16[1024,3072]{1,0:T(8,128)(2,1)} %get-tuple-element.250.dact, bf16[512,4608]{1,0:T(8,128)(2,1)} %bitcast.124, ...), custom_call_target="tpu_custom_call" | custom-call | flops 9663676416 | bytes 31457280 | tf_op jit(solution)/shard_map/mlp_back0/pallas_call | solution.py:491
  240.9 4.9 %add_convert_fusion.1 = bf16[512,4608]{1,0:T(8,128)(2,1)S(1)} fusion(bf16[512,4608]{1,0:T(8,128)(2,1)} %collective-permute-done.24, bf16[512,4608]{1,0:T(8,128)(2,1)} %get-tuple-element.245), kind=kLoop, calls=%fused_computation.1 | loop fusion | flops 9437184 | bytes 14155776 | tf_op jit(solution)/shard_map/convert_element_type | solution.py:102
  247.5 26.7 %mlp.3 = (bf16[1024,1536]{1,0:T(8,128)(2,1)}, bf16[1024,3072]{1,0:T(8,128)(2,1)}, bf16[512,4608]{1,0:T(8,128)(2,1)}, bf16[512,4608]{1,0:T(8,128)(2,1)}) custom-call(bf16[1024,1024]{1,0:T(8,128)(2,1)} %get-tuple-element.236.refs_0_, bf16[1024,1024]{1,0:T(8,128)(2,1)} %get-tuple-element.237.refs_1_, bf16[1024,1024]{1,0:T(8,128)(2,1)} %get-tuple-element.238.refs_2_.crel_in, ...), custom_call_target="tpu_custom_call" | custom-call | flops 19327352832 | bytes 36700160 | tf_op jit(solution)/shard_map/mlp/pallas_call | solution.py:232
  279.4 17.9 %mlp_back1.1 = (f32[1024,1024]{1,0:T(8,128)}, bf16[1024,1024]{1,0:T(8,128)(2,1)}, bf16[1024,1024]{1,0:T(8,128)(2,1)}) custom-call(f32[1024,1024]{1,0:T(8,128)} %get-tuple-element.248.x1.x1_in, bf16[1024,1024]{1,0:T(8,128)(2,1)} %get-tuple-element.238.refs_2_.crel_in, f32[1024,1024]{1,0:T(8,128)} %get-tuple-element.263.dn2_in, ...), custom_call_target="tpu_custom_call" | custom-call | flops 6442450944 | bytes 31457280 | tf_op jit(solution)/shard_map/mlp_back1/pallas_call | solution.py:541
  297.4 3.8 add_convert_fusion
  309.0 8.2 %out_grad.1 = (bf16[512,4096]{1,0:T(8,128)(2,1)}, bf16[512,4096]{1,0:T(8,128)(2,1)}) custom-call(bf16[1024,1024]{1,0:T(8,128)(2,1)} %get-tuple-element.276.refs_0_, bf16[1024,2048]{1,0:T(8,128)(2,1)} %get-tuple-element.234.o.refs_1_), custom_call_target="tpu_custom_call" | custom-call | flops 4294967296 | bytes 10485760 | tf_op jit(solution)/shard_map/out_grad/pallas_call | solution.py:232
  317.2 17.3 %attend_back.4 = (f32[8,128]{1,0:T(8,128)}, bf16[512,4096]{1,0:T(8,128)(2,1)}, bf16[512,4096]{1,0:T(8,128)(2,1)}, bf16[1024,2048]{1,0:T(8,128)(2,1)}, bf16[1024,...) custom-call(bf16[1024,1024]{1,0:T(8,128)(2,1)} %get-tuple-element.271.refs_0_, ...), custom_call_target="tpu_custom_call", output_to_operand_aliasing={{1}: (15, {}), {2}: (16, {})} | custom-call | flops 8589934592 | bytes 13631488 | tf_op jit(solution)/shard_map/attend_back/pallas_call | solution.py:232
  338.1 17.5 %attend_back.5 = (f32[8,128]{1,0:T(8,128)}, bf16[512,4096]{1,0:T(8,128)(2,1)}, bf16[512,4096]{1,0:T(8,128)(2,1)}, bf16[1024,2048]{1,0:T(8,128)(2,1)}, bf16[1024,...) custom-call(bf16[1024,1024]{1,0:T(8,128)(2,1)} %get-tuple-element.27, ...), custom_call_target="tpu_custom_call", output_to_operand_aliasing={{1}: (15, {}), {2}: (16, {}), {3}: (17, {}), {4}: (18, {}),... | custom-call | flops 8589934592 | bytes 13631488 | tf_op jit(solution)/shard_map/attend_back/pallas_call | solution.py:232
  358.0 17.9 %attend_back.6 = (f32[8,128]{1,0:T(8,128)}, bf16[512,2048]{1,0:T(8,128)(2,1)}, bf16[512,2048]{1,0:T(8,128)(2,1)}, bf16[1024,2048]{1,0:T(8,128)(2,1)}, bf16[1024,...) custom-call(bf16[1024,1024]{1,0:T(8,128)(2,1)} %get-tuple-element.271., ...), custom_call_target="tpu_custom_call", output_to_operand_aliasing={{3}: (15, {}), {4}: (16, {}), {5}: (17, {})} | custom-call | flops 8589934592 | bytes 13631488 | tf_op jit(solution)/shard_map/attend_back/pallas_call | solution.py:232
  376.0 3.8 add_convert_fusion.2
  382.4 3.5 collective-permute-start.38
  385.9 17.4 %attend_back.7 = (f32[8,128]{1,0:T(8,128)}, bf16[512,2048]{1,0:T(8,128)(2,1)}, bf16[512,2048]{1,0:T(8,128)(2,1)}, bf16[1024,2048]{1,0:T(8,128)(2,1)}, bf16[1024,...) custom-call(bf16[1024,1024]{1,0:T(8,128)(2,1)} %get-tuple-element.27, ...), custom_call_target="tpu_custom_call", output_to_operand_aliasing={{1}: (15, {}), {2}: (16, {}), {3}: (17, {}), {4}: (18, {}),... | custom-call | flops 8589934592 | bytes 13631488 | tf_op jit(solution)/shard_map/attend_back/pallas_call | solution.py:232
  412.3 12.8 %result.1 = bf16[1024,1024]{1,0:T(8,128)(2,1)} custom-call(f32[1024,1024]{1,0:T(8,128)} %get-tuple-element.327.res, bf16[1024,1024]{1,0:T(8,128)(2,1)} %fusion.perm, bf16[1024,1536]{1,0:T(8,128)(2,1)} %get-tuple-element.328.hidden, bf16[512,4608]{1,0:T(8,128)(2,1)} %bitcast.113, bf16[512,4608]{1,0:T(8,128)(2,1)} %collective-permute-done.23.refs_5_.w1), custom_call_target="tpu_custom_call" | custom-call | flops 5368709120 | bytes 14680064 | tf_op jit(solution)/shard_map/result/pallas_call | solution.py:597
  434.9 19.3 %input_back.1 = bf16[1024,1024]{1,0:T(8,128)(2,1)} custom-call(bf16[1024,1024]{1,0:T(8,128)(2,1)} %get-tuple-element.218.trel.refs_8_, f32[1024,1024]{1,0:T(8,128)} %get-tuple-element.341.dx1, f32[1,1024]{1,0:T(1,128)} %get-tuple-element.415.gain, bf16[1024,1024]{1,0:T(8,128)(2,1)} %fusion.perm, bf16[1024,2048]{1,0:T(8,128)(2,1)} %get-tuple-element.342.dq, ...), custom_call_target="tpu_custom_call" | custom-call | flops 10737418240 | bytes 27262976 | tf_op jit(solution)/shard_map/input_back/pallas_call | solution.py:720
  472.3 6.2 %collective-permute-done.62 = f32[8,128]{1,0:T(8,128)S(1)} collective-permute-done((f32[8,128]{1,0:T(8,128)S(1)}, f32[8,128]{1,0:T(8,128)S(1)}, u32[]{:S(2)}, u32[]{:S(2)}) %collective-permute-start.62) | collective-permute-done | bytes 4128 | tf_op jit(solution)/shard_map/ppermute | solution.py:175
  (332 shorter events, 124.9 us)
Async XLA Ops:
  65.1 37.1 %collective-permute-start.11 = (bf16[1,2,4,16,6272]{4,3,2,1,0:T(8,128)(2,1)}, bf16[1,2,4,16,6272]{4,3,2,1,0:T(8,128)(2,1)S(1)}, u32[]{:S(2)}, u32[]{:S(2)}) collective-permute-start(bf16[1,2,4,16,6272]{4,3,2,1,0:T(8,128)(2,1)} %pad_maximum_fusion.5), channel_id=1, source_target_pairs={{0,2},{1,3},{2,0},{3,1},{4,6},{5,7},{6,4},{7,5},{8,10},{9,11},{10,... | collective-permute-start | bytes 4816904 | tf_op jit(solution)/shard_map/ppermute | solution.py:53
  65.6 36.6 %collective-permute-start.10 = (bf16[2,1,4,16,6272]{4,3,2,1,0:T(8,128)(2,1)S(1)}, bf16[2,1,4,16,6272]{4,3,2,1,0:T(8,128)(2,1)}, u32[]{:S(2)}, u32[]{:S(2)}) collective-permute-start(bf16[2,1,4,16,6272]{4,3,2,1,0:T(8,128)(2,1)S(1)} %pad_maximum_fusion.4), channel_id=1, source_target_pairs={{0,4},{1,5},{2,6},{3,7},{4,0},{5,1},{6,2},{7,3},{8,12},{9,13},{10,... | collective-permute-start | bytes 4816904 | tf_op jit(solution)/shard_map/ppermute | solution.py:53
  68.3 33.9 %collective-permute-start.14 = (bf16[2,2,2,1,16,4608]{5,4,2,1,3,0:T(8,128)(2,1)}, bf16[2,2,2,1,16,4608]{5,4,2,1,3,0:T(8,128)(2,1)}, u32[]{:S(2)}, u32[]{:S(2)}) collective-permute-start(bf16[2,2,2,1,16,4608]{5,4,2,1,3,0:T(8,128)(2,1)} %pad_maximum_fusion.6), channel_id=1, source_target_pairs={{0,24},{1,25},{2,26},{3,27},{4,28},{5,29},{6,30},{7,31},{8,0},{9,1... | collective-permute-start | bytes 3538952 | tf_op jit(solution)/shard_map/ppermute | solution.py:53
  69.5 30.4 %collective-permute-start.13 = (bf16[1,1,1,32,4608]{4,3,2,1,0:T(8,128)(2,1)S(1)}, bf16[1,1,1,32,4608]{4,3,2,1,0:T(8,128)(2,1)S(1)}, u32[]{:S(2)}, u32[]{:S(2)}) collective-permute-start(bf16[1,1,1,32,4608]{4,3,2,1,0:T(8,128)(2,1)S(1)} %reshape_reshape.6), channel_id=1, source_target_pairs={{0,8},{1,9},{2,10},{3,11},{4,12},{5,13},{6,14},{7,15},{8,16},{9,17... | collective-permute-start | bytes 884744 | tf_op jit(solution)/shard_map/ppermute | solution.py:53
  70.3 31.8 %collective-permute-start.12 = (bf16[1,1,1,32,4608]{4,3,2,1,0:T(8,128)(2,1)S(1)}, bf16[1,1,1,32,4608]{4,3,2,1,0:T(8,128)(2,1)}, u32[]{:S(2)}, u32[]{:S(2)}) collective-permute-start(bf16[1,1,1,32,4608]{4,3,2,1,0:T(8,128)(2,1)S(1)} %reshape_reshape.6), channel_id=1, source_target_pairs={{0,24},{1,25},{2,26},{3,27},{4,28},{5,29},{6,30},{7,31},{8,0},{9,1... | collective-permute-start | bytes 884744 | tf_op jit(solution)/shard_map/ppermute | solution.py:53
  109.9 41.6 %collective-permute-start.20 = (bf16[2,2,2,1,16,4608]{5,4,2,1,3,0:T(8,128)(2,1)}, bf16[2,2,2,1,16,4608]{5,4,2,1,3,0:T(8,128)(2,1)}, u32[]{:S(2)}, u32[]{:S(2)}) collective-permute-start(bf16[2,2,2,1,16,4608]{5,4,2,1,3,0:T(8,128)(2,1)} %collective-permute-done.14), channel_id=1, source_target_pairs={{0,24},{1,25},{2,26},{3,27},{4,28},{5,29},{6,30},{7,31},{8,0},{9,1... | collective-permute-start | bytes 3538952 | tf_op jit(solution)/shard_map/ppermute | solution.py:53
  125.9 27.3 %collective-permute-start.19 = (bf16[1,2,4,16,4608]{4,3,2,1,0:T(8,128)(2,1)}, bf16[1,2,4,16,4608]{4,3,2,1,0:T(8,128)(2,1)}, u32[]{:S(2)}, u32[]{:S(2)}) collective-permute-start(bf16[1,2,4,16,4608]{4,3,2,1,0:T(8,128)(2,1)} %pad_maximum_fusion.8), channel_id=1, source_target_pairs={{0,2},{1,3},{2,0},{3,1},{4,6},{5,7},{6,4},{7,5},{8,10},{9,11},{10,... | collective-permute-start | bytes 3538952 | tf_op jit(solution)/shard_map/ppermute | solution.py:53
  127.4 27.0 %collective-permute-start.18 = (bf16[2,1,4,16,4608]{4,3,2,1,0:T(8,128)(2,1)}, bf16[2,1,4,16,4608]{4,3,2,1,0:T(8,128)(2,1)}, u32[]{:S(2)}, u32[]{:S(2)}) collective-permute-start(bf16[2,1,4,16,4608]{4,3,2,1,0:T(8,128)(2,1)} %pad_maximum_fusion.7), channel_id=1, source_target_pairs={{0,4},{1,5},{2,6},{3,7},{4,0},{5,1},{6,2},{7,3},{8,12},{9,13},{10,... | collective-permute-start | bytes 3538952 | tf_op jit(solution)/shard_map/ppermute | solution.py:53
  157.9 22.9 %collective-permute-start.22 = (bf16[512,4608]{1,0:T(8,128)(2,1)S(1)}, bf16[512,4608]{1,0:T(8,128)(2,1)}, u32[]{:S(2)}, u32[]{:S(2)}) collective-permute-start(bf16[512,4608]{1,0:T(8,128)(2,1)S(1)} %bitcast.122), channel_id=1, source_target_pairs={{0,1},{1,0},{2,3},{3,2},{4,5},{5,4},{6,7},{7,6},{8,9},{9,8},{10,11... | collective-permute-start | bytes 14155784 | tf_op jit(solution)/shard_map/ppermute | solution.py:53
  159.9 58.0 %collective-permute-start.21 = (bf16[2,2,2,1,16,4608]{5,4,2,1,3,0:T(8,128)(2,1)}, bf16[2,2,2,1,16,4608]{5,4,2,1,3,0:T(8,128)(2,1)S(1)}, u32[]{:S(2)}, u32[]{:S(2)}) collective-permute-start(bf16[2,2,2,1,16,4608]{5,4,2,1,3,0:T(8,128)(2,1)} %collective-permute-done.20), channel_id=1, source_target_pairs={{0,24},{1,25},{2,26},{3,27},{4,28},{5,29},{6,30},{7,31},{8,0},{9,1... | collective-permute-start | bytes 3538952 | tf_op jit(solution)/shard_map/ppermute | solution.py:53
  221.0 20.0 %collective-permute-start.23 = (bf16[512,4608]{1,0:T(8,128)(2,1)S(1)}, bf16[512,4608]{1,0:T(8,128)(2,1)}, u32[]{:S(2)}, u32[]{:S(2)}) collective-permute-start(bf16[512,4608]{1,0:T(8,128)(2,1)S(1)} %bitcast.110), channel_id=1, source_target_pairs={{0,1},{1,0},{2,3},{3,2},{4,5},{5,4},{6,7},{7,6},{8,9},{9,8},{10,11... | collective-permute-start | bytes 14155784 | tf_op jit(solution)/shard_map/ppermute | solution.py:53
  246.2 27.9 %collective-permute-start.26 = (bf16[2,1,4,16,4608]{4,3,2,1,0:T(8,128)(2,1)S(1)}, bf16[2,1,4,16,4608]{4,3,2,1,0:T(8,128)(2,1)S(1)}, u32[]{:S(2)}, u32[]{:S(2)}) collective-permute-start(bf16[2,1,4,16,4608]{4,3,2,1,0:T(8,128)(2,1)S(1)} %slice.345), channel_id=1, source_target_pairs={{0,4},{1,5},{2,6},{3,7},{4,0},{5,1},{6,2},{7,3},{8,12},{9,13},{10,... | collective-permute-start | bytes 3538952 | tf_op jit(solution)/shard_map/ppermute | solution.py:53
  246.9 27.3 %collective-permute-start.25 = (bf16[1,2,4,16,4608]{4,3,2,1,0:T(8,128)(2,1)S(1)}, bf16[1,2,4,16,4608]{4,3,2,1,0:T(8,128)(2,1)S(1)}, u32[]{:S(2)}, u32[]{:S(2)}) collective-permute-start(bf16[1,2,4,16,4608]{4,3,2,1,0:T(8,128)(2,1)S(1)} %bitcast.135), channel_id=1, source_target_pairs={{0,2},{1,3},{2,0},{3,1},{4,6},{5,7},{6,4},{7,5},{8,10},{9,11},{10,... | collective-permute-start | bytes 3538952 | tf_op jit(solution)/shard_map/ppermute | solution.py:53
  274.2 23.2 %collective-permute-start.29 = (bf16[512,4608]{1,0:T(8,128)(2,1)}, bf16[512,4608]{1,0:T(8,128)(2,1)}, u32[]{:S(2)}, u32[]{:S(2)}) collective-permute-start(bf16[512,4608]{1,0:T(8,128)(2,1)} %get-tuple-element.262), channel_id=1, source_target_pairs={{0,1},{1,0},{2,3},{3,2},{4,5},{5,4},{6,7},{7,6},{8,9},{9,8},{10,11... | collective-permute-start | bytes 14155784 | tf_op jit(solution)/shard_map/ppermute | solution.py:53
  276.5 20.8 %collective-permute-start.28 = (bf16[1,1,4,16,4608]{4,3,2,1,0:T(8,128)(2,1)}, bf16[1,1,4,16,4608]{4,3,2,1,0:T(8,128)(2,1)S(1)}, u32[]{:S(2)}, u32[]{:S(2)}) collective-permute-start(bf16[1,1,4,16,4608]{4,3,2,1,0:T(8,128)(2,1)} %slice.349), channel_id=1, source_target_pairs={{0,2},{1,3},{2,0},{3,1},{4,6},{5,7},{6,4},{7,5},{8,10},{9,11},{10,... | collective-permute-start | bytes 1769480 | tf_op jit(solution)/shard_map/ppermute | solution.py:53
  303.9 30.6 %collective-permute-start.30 = (bf16[2,1,1,1,16,4608]{5,4,0,3,2,1:T(8,128)(2,1)}, bf16[2,1,1,1,16,4608]{5,4,0,3,2,1:T(8,128)(2,1)}, u32[]{:S(2)}, u32[]{:S(2)}) collective-permute-start(bf16[2,1,1,1,16,4608]{5,4,0,3,2,1:T(8,128)(2,1)} %get-tuple-element.396), channel_id=1, source_target_pairs={{0,16},{1,17},{2,18},{3,19},{4,20},{5,21},{6,22},{7,23},{8,24},{9,... | collective-permute-start | bytes 884744 | tf_op jit(solution)/shard_map/ppermute | solution.py:53
  303.9 51.8 %collective-permute-start.35 = (bf16[2,1,1,1,16,4608]{5,4,0,3,2,1:T(8,128)(2,1)}, bf16[2,1,1,1,16,4608]{5,4,0,3,2,1:T(8,128)(2,1)}, u32[]{:S(2)}, u32[]{:S(2)}) collective-permute-start(bf16[2,1,1,1,16,4608]{5,4,0,3,2,1:T(8,128)(2,1)} %get-tuple-element.397), channel_id=1, source_target_pairs={{0,8},{1,9},{2,10},{3,11},{4,12},{5,13},{6,14},{7,15},{8,16},{9,17... | collective-permute-start | bytes 884744 | tf_op jit(solution)/shard_map/ppermute | solution.py:53
  304.5 51.2 %collective-permute-start.36 = (bf16[2,1,1,1,16,4608]{5,4,0,3,2,1:T(8,128)(2,1)}, bf16[2,1,1,1,16,4608]{5,4,0,3,2,1:T(8,128)(2,1)}, u32[]{:S(2)}, u32[]{:S(2)}) collective-permute-start(bf16[2,1,1,1,16,4608]{5,4,0,3,2,1:T(8,128)(2,1)} %get-tuple-element.398), channel_id=1, source_target_pairs={{0,24},{1,25},{2,26},{3,27},{4,28},{5,29},{6,30},{7,31},{8,0},{9,1... | collective-permute-start | bytes 884744 | tf_op jit(solution)/shard_map/ppermute | solution.py:53
  307.8 27.3 %collective-permute-start.32 = (bf16[2,1,4,16,4608]{4,3,2,1,0:T(8,128)(2,1)S(1)}, bf16[2,1,4,16,4608]{4,3,2,1,0:T(8,128)(2,1)S(1)}, u32[]{:S(2)}, u32[]{:S(2)}) collective-permute-start(bf16[2,1,4,16,4608]{4,3,2,1,0:T(8,128)(2,1)S(1)} %slice.357), channel_id=1, source_target_pairs={{0,4},{1,5},{2,6},{3,7},{4,0},{5,1},{6,2},{7,3},{8,12},{9,13},{10,... | collective-permute-start | bytes 3538952 | tf_op jit(solution)/shard_map/ppermute | solution.py:53
  308.5 27.0 %collective-permute-start.31 = (bf16[1,2,4,16,4608]{4,3,2,1,0:T(8,128)(2,1)S(1)}, bf16[1,2,4,16,4608]{4,3,2,1,0:T(8,128)(2,1)S(1)}, u32[]{:S(2)}, u32[]{:S(2)}) collective-permute-start(bf16[1,2,4,16,4608]{4,3,2,1,0:T(8,128)(2,1)S(1)} %bitcast.134), channel_id=1, source_target_pairs={{0,2},{1,3},{2,0},{3,1},{4,6},{5,7},{6,4},{7,5},{8,10},{9,11},{10,... | collective-permute-start | bytes 3538952 | tf_op jit(solution)/shard_map/ppermute | solution.py:53
  355.7 20.3 %collective-permute-start.40 = (bf16[512,4096]{1,0:T(8,128)(2,1)}, bf16[512,4096]{1,0:T(8,128)(2,1)}, u32[]{:S(2)}, u32[]{:S(2)}) collective-permute-start(bf16[512,4096]{1,0:T(8,128)(2,1)} %get-tuple-element.301), channel_id=1, source_target_pairs={{0,1},{1,0},{2,3},{3,2},{4,5},{5,4},{6,7},{7,6},{8,9},{9,8},{10,11... | collective-permute-start | bytes 12582920 | tf_op jit(solution)/shard_map/ppermute | solution.py:53
  380.2 25.3 %collective-permute-start.42 = (bf16[2,1,4,16,4096]{4,3,2,1,0:T(8,128)(2,1)S(1)}, bf16[2,1,4,16,4096]{4,3,2,1,0:T(8,128)(2,1)S(1)}, u32[]{:S(2)}, u32[]{:S(2)}) collective-permute-start(bf16[2,1,4,16,4096]{4,3,2,1,0:T(8,128)(2,1)S(1)} %slice.375), channel_id=1, source_target_pairs={{0,4},{1,5},{2,6},{3,7},{4,0},{5,1},{6,2},{7,3},{8,12},{9,13},{10,... | collective-permute-start | bytes 3145736 | tf_op jit(solution)/shard_map/ppermute | solution.py:53
  380.9 25.1 %collective-permute-start.41 = (bf16[1,2,4,16,4096]{4,3,2,1,0:T(8,128)(2,1)S(1)}, bf16[1,2,4,16,4096]{4,3,2,1,0:T(8,128)(2,1)}, u32[]{:S(2)}, u32[]{:S(2)}) collective-permute-start(bf16[1,2,4,16,4096]{4,3,2,1,0:T(8,128)(2,1)S(1)} %bitcast.136), channel_id=1, source_target_pairs={{0,2},{1,3},{2,0},{3,1},{4,6},{5,7},{6,4},{7,5},{8,10},{9,11},{10,... | collective-permute-start | bytes 3145736 | tf_op jit(solution)/shard_map/ppermute | solution.py:53
  382.1 21.3 %collective-permute-start.37 = (bf16[2,1,1,1,16,4608]{5,4,0,3,2,1:T(8,128)(2,1)S(1)}, bf16[2,1,1,1,16,4608]{5,4,0,3,2,1:T(8,128)(2,1)S(1)}, u32[]{:S(2)}, u32[]{:S(2)}) collective-permute-start(bf16[2,1,1,1,16,4608]{5,4,0,3,2,1:T(8,128)(2,1)S(1)} %get-tuple-element.392), channel_id=1, source_target_pairs={{0,8},{1,9},{2,10},{3,11},{4,12},{5,13},{6,14},{7,15},{8,16},{9,17... | collective-permute-start | bytes 884744 | tf_op jit(solution)/shard_map/ppermute | solution.py:53
  382.4 21.0 %collective-permute-start.38 = (bf16[2,1,1,1,16,4608]{5,4,0,3,2,1:T(8,128)(2,1)S(1)}, bf16[2,1,1,1,16,4608]{5,4,0,3,2,1:T(8,128)(2,1)S(1)}, u32[]{:S(2)}, u32[]{:S(2)}) collective-permute-start(bf16[2,1,1,1,16,4608]{5,4,0,3,2,1:T(8,128)(2,1)S(1)} %get-tuple-element.393), channel_id=1, source_target_pairs={{0,24},{1,25},{2,26},{3,27},{4,28},{5,29},{6,30},{7,31},{8,0},{9,1... | collective-permute-start | bytes 884744 | tf_op jit(solution)/shard_map/ppermute | solution.py:53
  410.6 20.1 %collective-permute-start.53 = (f32[8,128]{1,0:T(8,128)S(1)}, f32[8,128]{1,0:T(8,128)S(1)}, u32[]{:S(2)}, u32[]{:S(2)}) collective-permute-start(f32[8,128]{1,0:T(8,128)S(1)} %add_add_fusion.2), channel_id=1, source_target_pairs={{0,3},{1,2},{2,1},{3,0},{4,7},{5,6},{6,5},{7,4},{8,11},{9,10},{10,... | collective-permute-start | bytes 12296 | tf_op jit(solution)/shard_map/ppermute | solution.py:175
  411.1 22.5 %collective-permute-start.52 = (f32[8,128]{1,0:T(8,128)S(1)}, f32[8,128]{1,0:T(8,128)S(1)}, u32[]{:S(2)}, u32[]{:S(2)}) collective-permute-start(f32[8,128]{1,0:T(8,128)S(1)} %add_add_fusion.2), channel_id=1, source_target_pairs={{0,2},{1,3},{2,0},{3,1},{4,6},{5,7},{6,4},{7,5},{8,10},{9,11},{10,... | collective-permute-start | bytes 12296 | tf_op jit(solution)/shard_map/ppermute | solution.py:175
  428.4 25.8 %collective-permute-start.48 = (bf16[2,1,1,1,16,4096]{5,4,0,3,2,1:T(8,128)(2,1)S(1)}, bf16[2,1,1,1,16,4096]{5,4,0,3,2,1:T(8,128)(2,1)S(1)}, u32[]{:S(2)}, u32[]{:S(2)}) collective-permute-start(bf16[2,1,1,1,16,4096]{5,4,0,3,2,1:T(8,128)(2,1)S(1)} %get-tuple-element.402), channel_id=1, source_target_pairs={{0,8},{1,9},{2,10},{3,11},{4,12},{5,13},{6,14},{7,15},{8,16},{9,17... | collective-permute-start | bytes 786440 | tf_op jit(solution)/shard_map/ppermute | solution.py:53
  428.8 25.5 %collective-permute-start.49 = (bf16[2,1,1,1,16,4096]{5,4,0,3,2,1:T(8,128)(2,1)S(1)}, bf16[2,1,1,1,16,4096]{5,4,0,3,2,1:T(8,128)(2,1)S(1)}, u32[]{:S(2)}, u32[]{:S(2)}) collective-permute-start(bf16[2,1,1,1,16,4096]{5,4,0,3,2,1:T(8,128)(2,1)S(1)} %get-tuple-element.403), channel_id=1, source_target_pairs={{0,16},{1,17},{2,18},{3,19},{4,20},{5,21},{6,22},{7,23},{8,24},{9,... | collective-permute-start | bytes 786440 | tf_op jit(solution)/shard_map/ppermute | solution.py:53
  430.7 23.5 %collective-permute-start.50 = (bf16[2,1,1,1,16,4096]{5,4,0,3,2,1:T(8,128)(2,1)S(1)}, bf16[2,1,1,1,16,4096]{5,4,0,3,2,1:T(8,128)(2,1)S(1)}, u32[]{:S(2)}, u32[]{:S(2)}) collective-permute-start(bf16[2,1,1,1,16,4096]{5,4,0,3,2,1:T(8,128)(2,1)S(1)} %get-tuple-element.404), channel_id=1, source_target_pairs={{0,24},{1,25},{2,26},{3,27},{4,28},{5,29},{6,30},{7,31},{8,0},{9,1... | collective-permute-start | bytes 786440 | tf_op jit(solution)/shard_map/ppermute | solution.py:53
  433.6 20.7 %collective-permute-start.47 = (bf16[2,1,4,16,2048]{4,3,2,1,0:T(8,128)(2,1)S(1)}, bf16[2,1,4,16,2048]{4,3,2,1,0:T(8,128)(2,1)S(1)}, u32[]{:S(2)}, u32[]{:S(2)}) collective-permute-start(bf16[2,1,4,16,2048]{4,3,2,1,0:T(8,128)(2,1)S(1)} %slice.382), channel_id=1, source_target_pairs={{0,4},{1,5},{2,6},{3,7},{4,0},{5,1},{6,2},{7,3},{8,12},{9,13},{10,... | collective-permute-start | bytes 1572872 | tf_op jit(solution)/shard_map/ppermute | solution.py:53
  434.2 20.1 %collective-permute-start.46 = (bf16[1,2,4,16,2048]{4,3,2,1,0:T(8,128)(2,1)S(1)}, bf16[1,2,4,16,2048]{4,3,2,1,0:T(8,128)(2,1)S(1)}, u32[]{:S(2)}, u32[]{:S(2)}) collective-permute-start(bf16[1,2,4,16,2048]{4,3,2,1,0:T(8,128)(2,1)S(1)} %bitcast.141), channel_id=1, source_target_pairs={{0,2},{1,3},{2,0},{3,1},{4,6},{5,7},{6,4},{7,5},{8,10},{9,11},{10,... | collective-permute-start | bytes 1572872 | tf_op jit(solution)/shard_map/ppermute | solution.py:53
  (83 other events, 811.1 us)
